TPU v7x, 1024 devices: a whole 8x8x8 slice. The times are simulated.
1024 devices in a mesh: py: 16 (over y_lo, z), pz: 64 (over y_hi, x, core).
Axes of the slice: x: 8, y: 8 (y_hi: 4, y_lo: 2; y = y_hi * 2 + y_lo), z: 8, core: 2. Of those that a mesh axis runs over, the one named last changes fastest.
Arguments:
- velocity: float32 [3, 64, 512, 256], P(None, 'py', 'pz'), may hold values from -4 to 4
- cotangent: float32 [3, 64, 512, 256], P(None, 'py', 'pz'), may hold values from -15 to 15
Outputs:
- adjoint_velocity: float32 [3, 64, 512, 256], P(None, 'py', 'pz')
All inputs are finite; a program needn't handle non-finite values.
Results may differ from a plain program's by a relative error of at most 0.0003.
Values sent between devices are 32-bit elements; how exact they have to be, the bound alone decides.
No kernel may reach another device: no remote copies, remote signals or barrier semaphores. Data moves between devices by JAX's collectives and lax.ppermute only.
A program may use at most 32 MiB of HBM per device.

v0:
```python
import jax
import jax.numpy as jnp
from jax import lax
from jax.sharding import PartitionSpec as P

ITERS = 2


smag_coef = 0.1156
time_step = 0.2
strain_floor = 0.25


def extended(x, sides, width):
    for axis, dim in sides:
        peers, length = (lax.axis_size(axis), x.shape[dim])
        up = [(i, (i + 1) % peers) for i in range(peers)]
        down = [(j, i) for i, j in up]
        last = lax.slice_in_dim(x, length - width, length, axis=dim)
        leading = lax.slice_in_dim(x, 0, width, axis=dim)
        before = lax.ppermute(last, axis, up)
        after = lax.ppermute(leading, axis, down)
        x = jnp.concatenate([before, x, after], axis=dim)
    return x


def along_x(f):
    return (0.5 * (jnp.roll(f, -1, -1) - jnp.roll(f, 1, -1)))[..., 1:-1, 1:-1, :]


def along_y(f):
    return 0.5 * (f[..., 2:, 1:-1, :] - f[..., :-2, 1:-1, :])


def along_z(f):
    return 0.5 * (f[..., 1:-1, 2:, :] - f[..., 1:-1, :-2, :])


def trimmed(f):
    return f[..., 1:-1, 1:-1, :]


def tendency(velocity):
    gradients = [
        [along_x(velocity[i]), along_y(velocity[i]), along_z(velocity[i])] for i in range(3)
    ]
    strain = [[0.5 * (gradients[i][j] + gradients[j][i]) for j in range(3)] for i in range(3)]
    squares = strain[0][0] * strain[0][0]
    for i in range(3):
        for j in range(3):
            if i + j > 0:
                squares = squares + strain[i][j] * strain[i][j]
    viscosity = smag_coef * jnp.sqrt(2.0 * squares + strain_floor)
    centred = trimmed(velocity)
    pieces = []
    for i in range(3):
        advect = (
            centred[0] * gradients[i][0]
            + centred[1] * gradients[i][1]
            + centred[2] * gradients[i][2]
        )
        fluxes = [2.0 * viscosity * strain[i][j] for j in range(3)]
        diffuse = along_x(fluxes[0]) + along_y(fluxes[1]) + along_z(fluxes[2])
        pieces.append(time_step * (diffuse - trimmed(advect)))
    return jnp.stack(pieces)


def divergence(field):
    return along_x(field[0]) + along_y(field[1]) + along_z(field[2])


def gradient(scalar):
    return jnp.stack([along_x(scalar), along_y(scalar), along_z(scalar)])


def operate(field):
    padded = extended(field, (("py", 0), ("pz", 1)), 1)
    centre = trimmed(padded)
    beside = jnp.roll(centre, 1, -1) + jnp.roll(centre, -1, -1)
    beside = beside + padded[2:, 1:-1, :] + padded[:-2, 1:-1, :]
    beside = beside + padded[1:-1, 2:, :] + padded[1:-1, :-2, :]
    return 6.0 * centre - beside


def squares_sum(residual):
    return lax.psum(jnp.sum(residual * residual), ("py", "pz"))


def body(velocity, cotangent):
    vel_wide = extended(velocity, (("py", 1), ("pz", 2)), 4)
    reach_width = 1
    cot_wide = extended(cotangent, (("py", 1), ("pz", 2)), reach_width)
    right_side = -divergence(cot_wide)
    pressure = jnp.zeros_like(right_side)
    residual = right_side
    direction = right_side
    norm_now = squares_sum(residual)
    for iteration in range(ITERS):
        image_field = operate(direction)
        step_size = norm_now / lax.psum(jnp.sum(direction * image_field), ("py", "pz"))
        pressure = pressure + step_size * direction
        if iteration + 1 < ITERS:
            residual = residual - step_size * image_field
            norm_next = squares_sum(residual)
            direction = residual + norm_next / norm_now * direction
            norm_now = norm_next
    pressure_cycle = extended(pressure, (("py", 0), ("pz", 1)), 1)
    projected = cotangent - gradient(pressure_cycle)
    projected_wide = extended(projected, (("py", 1), ("pz", 2)), 2)
    outputs, pullback = jax.vjp(tendency, vel_wide)
    adjoint_term = pullback(projected_wide)[0]
    return projected_wide[:, 2:-2, 2:-2, :] + adjoint_term[:, 4:-4, 4:-4, :]


def solution(mesh):
    placed = (P(None, "py", "pz", None), P(None, "py", "pz", None))
    return jax.shard_map(
        body, mesh=mesh, in_specs=placed, out_specs=P(None, "py", "pz", None), check_vma=False
    )
```

profile of v0, /device:TPU:47, one launch (start us, length us, event | category | flops | bytes accessed | tf_op | source)
XLA Modules:
  0.0 493.8 jit_solution(5908982346862344420)
XLA Ops:
  0.0 0.8 fusion.131
  0.8 4.9 collective-permute-start
  5.7 15.2 %collective-permute-start.1 = (f32[3,1,8,256]{3,2,1,0:T(8,128)S(1)}, f32[3,1,8,256]{3,2,1,0:T(8,128)S(1)}, u32[]{:S(2)}, u32[]{:S(2)}) collective-permute-start(f32[3,1,8,256]{3,2,1,0:T(8,128)S(1)} %get-tuple-element.125), channel_id=1, source_target_pairs={{64,0},{128,64},{192,128},{256,192},{320,256},{384,320},{448,384},... | collective-permute-start | bytes 73736 | tf_op jit(solution)/shard_map/ppermute | solution.py:22
  21.0 0.9 collective-permute-done.1
  21.9 6.0 %collective-permute-start.2 = (f32[3,6,1,256]{3,2,1,0:T(1,128)S(1)}, f32[3,6,1,256]{3,2,1,0:T(1,128)S(1)}, u32[]{:S(2)}, u32[]{:S(2)}) collective-permute-start(f32[3,6,1,256]{3,2,1,0:T(1,128)S(1)} %get-tuple-element.99), channel_id=1, source_target_pairs={{0,1},{1,2},{2,3},{3,4},{4,5},{5,6},{6,7},{7,8},{8,9},{9,10},{10,1... | collective-permute-start | bytes 55304 | tf_op jit(solution)/shard_map/ppermute | solution.py:21
  27.8 1.9 collective-permute-start.3
  29.8 7.4 %collective-permute-done.3 = f32[3,6,1,256]{3,2,1,0:T(1,128)S(1)} collective-permute-done((f32[3,6,1,256]{3,2,1,0:T(1,128)S(1)}, f32[3,6,1,256]{3,2,1,0:T(1,128)S(1)}, u32[]{:S(2)}, u32[]{:S(2)}) %collective-permute-start.3) | collective-permute-done | bytes 18464 | tf_op jit(solution)/shard_map/ppermute | solution.py:22
  37.5 6.0 %collective-permute-start.4 = (f32[1,8,256]{2,1,0:T(8,128)S(1)}, f32[1,8,256]{2,1,0:T(8,128)S(1)}, u32[]{:S(2)}, u32[]{:S(2)}) collective-permute-start(f32[1,8,256]{2,1,0:T(8,128)S(1)} %get-tuple-element.148), channel_id=1, source_target_pairs={{64,0},{128,64},{192,128},{256,192},{320,256},{384,320},{448,384},... | collective-permute-start | bytes 24584 | tf_op jit(solution)/shard_map/ppermute | solution.py:22
  43.6 1.9 collective-permute-start.5
  45.6 4.5 collective-permute-done.5
  50.1 1.9 collective-permute-start.6
  52.0 7.9 %collective-permute-start.7 = (f32[6,1,256]{2,1,0:T(1,128)S(1)}, f32[6,1,256]{2,1,0:T(1,128)S(1)}, u32[]{:S(2)}, u32[]{:S(2)}) collective-permute-start(f32[6,1,256]{2,1,0:T(1,128)S(1)} %get-tuple-element.134), channel_id=1, source_target_pairs={{0,1},{1,2},{2,3},{3,4},{4,5},{5,6},{6,7},{7,8},{8,9},{9,10},{10,1... | collective-permute-start | bytes 18440 | tf_op jit(solution)/shard_map/ppermute | solution.py:21
  60.0 0.7 collective-permute-done.7
  60.6 0.8 multiply_reduce_fusion.1
  61.4 111.4 %all-reduce.76 = (f32[]{:T(128)}, f32[]{:T(128)}) all-reduce(f32[]{:T(128)} %get-tuple-element.6, f32[]{:T(128)} %get-tuple-element.5), channel_id=1, replica_groups=mesh['py'=16,'pz'=64] {'py','pz'}, use_global_device_ids=true, to_apply=%region_1.2 | all-reduce | flops 2 | bytes 16 | tf_op jit(solution)/shard_map/psum | solution.py:86
  174.1 0.6 multiply_reduce_fusion
  174.7 111.9 %psum.30 = f32[]{:T(128)} all-reduce(f32[]{:T(128)} %multiply_reduce_fusion), channel_id=1, replica_groups=mesh['py'=16,'pz'=64] {'py','pz'}, use_global_device_ids=true, to_apply=%region_5.6 | all-reduce | flops 1 | bytes 8 | tf_op jit(solution)/shard_map/psum | solution.py:86
  287.9 3.4 collective-permute-start.8
  291.4 1.9 collective-permute-start.9
  293.4 4.5 collective-permute-done.9
  297.9 3.8 collective-permute-start.10
  301.7 6.0 %collective-permute-start.11 = (f32[6,1,256]{2,1,0:T(1,128)S(1)}, f32[6,1,256]{2,1,0:T(1,128)S(1)}, u32[]{:S(2)}, u32[]{:S(2)}) collective-permute-start(f32[6,1,256]{2,1,0:T(1,128)S(1)} %get-tuple-element.132), channel_id=1, source_target_pairs={{0,1},{1,2},{2,3},{3,4},{4,5},{5,6},{6,7},{7,8},{8,9},{9,10},{10,1... | collective-permute-start | bytes 18440 | tf_op jit(solution)/shard_map/ppermute | solution.py:21
  307.8 0.7 collective-permute-done.11
  308.5 0.8 fusion.64
  309.2 111.3 %psum.31 = f32[]{:T(128)} all-reduce(f32[]{:T(128)} %fusion.64), channel_id=1, replica_groups=mesh['py'=16,'pz'=64] {'py','pz'}, use_global_device_ids=true, to_apply=%region_7.8 | all-reduce | flops 1 | bytes 8 | tf_op jit(solution)/shard_map/psum | solution.py:100
  421.9 3.3 collective-permute-start.12
  425.2 4.1 collective-permute-start.13
  429.3 0.8 collective-permute-done.13
  430.1 9.1 %collective-permute-start.14 = (f32[6,1,256]{2,1,0:T(1,128)S(1)}, f32[6,1,256]{2,1,0:T(1,128)S(1)}, u32[]{:S(2)}, u32[]{:S(2)}) collective-permute-start(f32[6,1,256]{2,1,0:T(1,128)S(1)} %get-tuple-element.130), channel_id=1, source_target_pairs={{0,1},{1,2},{2,3},{3,4},{4,5},{5,6},{6,7},{7,8},{8,9},{9,10},{10,1... | collective-permute-start | bytes 18440 | tf_op jit(solution)/shard_map/ppermute | solution.py:21
  439.2 1.9 collective-permute-start.15
  441.1 1.9 collective-permute-start.20
  443.1 6.0 %collective-permute-start.21 = (f32[3,4,8,256]{3,2,1,0:T(8,128)S(1)}, f32[3,4,8,256]{3,2,1,0:T(8,128)S(1)}, u32[]{:S(2)}, u32[]{:S(2)}) collective-permute-start(f32[3,4,8,256]{3,2,1,0:T(8,128)S(1)} %copy-done.1), channel_id=1, source_target_pairs={{64,0},{128,64},{192,128},{256,192},{320,256},{384,320},{448,384},... | collective-permute-start | bytes 294920 | tf_op jit(solution)/shard_map/ppermute | solution.py:22
  449.3 0.1 fusion.57
  449.5 1.9 collective-permute-start.16
  451.4 5.5 %collective-permute-start.17 = (f32[3,2,8,256]{3,2,1,0:T(8,128)S(1)}, f32[3,2,8,256]{3,2,1,0:T(8,128)S(1)}, u32[]{:S(2)}, u32[]{:S(2)}) collective-permute-start(f32[3,2,8,256]{3,2,1,0:T(8,128)S(1)} %get-tuple-element.116), channel_id=1, source_target_pairs={{64,0},{128,64},{192,128},{256,192},{320,256},{384,320},{448,384},... | collective-permute-start | bytes 147464 | tf_op jit(solution)/shard_map/ppermute | solution.py:22
  457.0 1.1 collective-permute-done.17
  458.1 9.3 %collective-permute-start.18 = (f32[3,8,2,256]{3,2,1,0:T(2,128)S(1)}, f32[3,8,2,256]{3,2,1,0:T(2,128)S(1)}, u32[]{:S(2)}, u32[]{:S(2)}) collective-permute-start(f32[3,8,2,256]{3,2,1,0:T(2,128)S(1)} %get-tuple-element.91), channel_id=1, source_target_pairs={{0,1},{1,2},{2,3},{3,4},{4,5},{5,6},{6,7},{7,8},{8,9},{9,10},{10,1... | collective-permute-start | bytes 147464 | tf_op jit(solution)/shard_map/ppermute | solution.py:21
  467.3 1.9 collective-permute-start.19
  469.3 7.9 %collective-permute-start.22 = (f32[3,12,4,256]{3,2,1,0:T(4,128)S(1)}, f32[3,12,4,256]{3,2,1,0:T(4,128)S(1)}, u32[]{:S(2)}, u32[]{:S(2)}) collective-permute-start(f32[3,12,4,256]{3,2,1,0:T(4,128)S(1)} %get-tuple-element.74), channel_id=1, source_target_pairs={{0,1},{1,2},{2,3},{3,4},{4,5},{5,6},{6,7},{7,8},{8,9},{9,10},{10,1... | collective-permute-start | bytes 442376 | tf_op jit(solution)/shard_map/ppermute | solution.py:21
  477.2 1.9 collective-permute-start.23
  479.4 0.1 split.104
  480.1 0.1 fusion.89
  480.2 8.3 %collective-permute-done.23 = f32[3,12,4,256]{3,2,1,0:T(4,128)S(1)} collective-permute-done((f32[3,12,4,256]{3,2,1,0:T(4,128)S(1)}, f32[3,12,4,256]{3,2,1,0:T(4,128)S(1)}, u32[]{:S(2)}, u32[]{:S(2)}) %collective-permute-start.23) | collective-permute-done | bytes 147488 | tf_op jit(solution)/shard_map/ppermute | solution.py:22
  488.5 0.1 pad_maximum_fusion
  488.6 0.1 fusion.123
  488.9 0.1 fusion.120
  489.0 0.2 fusion.119
  489.2 0.2 fusion.16
  489.3 0.2 fusion.10
  489.5 0.2 fusion.2
  489.7 0.8 fusion.96
  490.5 0.3 fusion.7
  490.8 0.1 split.116
  490.9 0.2 fusion.99
  491.2 0.2 fusion.105
  491.5 0.1 split.120
  491.6 0.1 split.124
  492.2 0.1 fusion.111
  492.4 0.1 add_bitcast_fusion.6
  492.6 0.1 pad_add_fusion.1
  492.7 0.1 pad_add_fusion
  492.8 0.1 add_bitcast_fusion.3
  493.0 0.1 add_bitcast_fusion
  493.1 0.7 fusion.51
  (80 shorter events, 2.5 us)
Async XLA Ops:
  0.0 20.9 %copy-start = (f32[3,4,8,256]{3,2,1,0:T(8,128)S(1)}, f32[3,4,8,256]{3,2,1,0:T(8,128)}, u32[]{:S(2)}) copy-start(f32[3,4,8,256]{3,2,1,0:T(8,128)} %param.3) | copy-start | bytes 294916
  0.8 20.1 %collective-permute-start = (f32[3,1,8,256]{3,2,1,0:T(8,128)S(1)}, f32[3,1,8,256]{3,2,1,0:T(8,128)S(1)}, u32[]{:S(2)}, u32[]{:S(2)}) collective-permute-start(f32[3,1,8,256]{3,2,1,0:T(8,128)S(1)} %get-tuple-element.126), channel_id=1, source_target_pairs={{0,64},{64,128},{128,192},{192,256},{256,320},{320,384},{384,448},... | collective-permute-start | bytes 73736 | tf_op jit(solution)/shard_map/ppermute | solution.py:21
  5.7 16.1 %collective-permute-start.1 = (f32[3,1,8,256]{3,2,1,0:T(8,128)S(1)}, f32[3,1,8,256]{3,2,1,0:T(8,128)S(1)}, u32[]{:S(2)}, u32[]{:S(2)}) collective-permute-start(f32[3,1,8,256]{3,2,1,0:T(8,128)S(1)} %get-tuple-element.125), channel_id=1, source_target_pairs={{64,0},{128,64},{192,128},{256,192},{320,256},{384,320},{448,384},... | collective-permute-start | bytes 73736 | tf_op jit(solution)/shard_map/ppermute | solution.py:22
  21.9 7.9 %collective-permute-start.2 = (f32[3,6,1,256]{3,2,1,0:T(1,128)S(1)}, f32[3,6,1,256]{3,2,1,0:T(1,128)S(1)}, u32[]{:S(2)}, u32[]{:S(2)}) collective-permute-start(f32[3,6,1,256]{3,2,1,0:T(1,128)S(1)} %get-tuple-element.99), channel_id=1, source_target_pairs={{0,1},{1,2},{2,3},{3,4},{4,5},{5,6},{6,7},{7,8},{8,9},{9,10},{10,1... | collective-permute-start | bytes 55304 | tf_op jit(solution)/shard_map/ppermute | solution.py:21
  27.8 9.3 %collective-permute-start.3 = (f32[3,6,1,256]{3,2,1,0:T(1,128)S(1)}, f32[3,6,1,256]{3,2,1,0:T(1,128)S(1)}, u32[]{:S(2)}, u32[]{:S(2)}) collective-permute-start(f32[3,6,1,256]{3,2,1,0:T(1,128)S(1)} %get-tuple-element.100), channel_id=1, source_target_pairs={{1,0},{2,1},{3,2},{4,3},{5,4},{6,5},{7,6},{8,7},{9,8},{10,9},{11,1... | collective-permute-start | bytes 55304 | tf_op jit(solution)/shard_map/ppermute | solution.py:22
  37.5 8.1 %collective-permute-start.4 = (f32[1,8,256]{2,1,0:T(8,128)S(1)}, f32[1,8,256]{2,1,0:T(8,128)S(1)}, u32[]{:S(2)}, u32[]{:S(2)}) collective-permute-start(f32[1,8,256]{2,1,0:T(8,128)S(1)} %get-tuple-element.148), channel_id=1, source_target_pairs={{64,0},{128,64},{192,128},{256,192},{320,256},{384,320},{448,384},... | collective-permute-start | bytes 24584 | tf_op jit(solution)/shard_map/ppermute | solution.py:22
  43.6 6.5 %collective-permute-start.5 = (f32[1,8,256]{2,1,0:T(8,128)S(1)}, f32[1,8,256]{2,1,0:T(8,128)S(1)}, u32[]{:S(2)}, u32[]{:S(2)}) collective-permute-start(f32[1,8,256]{2,1,0:T(8,128)S(1)} %get-tuple-element.147), channel_id=1, source_target_pairs={{0,64},{64,128},{128,192},{192,256},{256,320},{320,384},{384,448},... | collective-permute-start | bytes 24584 | tf_op jit(solution)/shard_map/ppermute | solution.py:21
  50.1 9.9 %collective-permute-start.6 = (f32[6,1,256]{2,1,0:T(1,128)S(1)}, f32[6,1,256]{2,1,0:T(1,128)S(1)}, u32[]{:S(2)}, u32[]{:S(2)}) collective-permute-start(f32[6,1,256]{2,1,0:T(1,128)S(1)} %get-tuple-element.133), channel_id=1, source_target_pairs={{1,0},{2,1},{3,2},{4,3},{5,4},{6,5},{7,6},{8,7},{9,8},{10,9},{11,1... | collective-permute-start | bytes 18440 | tf_op jit(solution)/shard_map/ppermute | solution.py:22
  52.0 8.6 %collective-permute-start.7 = (f32[6,1,256]{2,1,0:T(1,128)S(1)}, f32[6,1,256]{2,1,0:T(1,128)S(1)}, u32[]{:S(2)}, u32[]{:S(2)}) collective-permute-start(f32[6,1,256]{2,1,0:T(1,128)S(1)} %get-tuple-element.134), channel_id=1, source_target_pairs={{0,1},{1,2},{2,3},{3,4},{4,5},{5,6},{6,7},{7,8},{8,9},{9,10},{10,1... | collective-permute-start | bytes 18440 | tf_op jit(solution)/shard_map/ppermute | solution.py:21
  287.9 5.4 %collective-permute-start.8 = (f32[1,8,256]{2,1,0:T(8,128)S(1)}, f32[1,8,256]{2,1,0:T(8,128)S(1)}, u32[]{:S(2)}, u32[]{:S(2)}) collective-permute-start(f32[1,8,256]{2,1,0:T(8,128)S(1)} %get-tuple-element.142), channel_id=1, source_target_pairs={{64,0},{128,64},{192,128},{256,192},{320,256},{384,320},{448,384},... | collective-permute-start | bytes 24584 | tf_op jit(solution)/shard_map/ppermute | solution.py:22
  291.4 6.5 %collective-permute-start.9 = (f32[1,8,256]{2,1,0:T(8,128)S(1)}, f32[1,8,256]{2,1,0:T(8,128)S(1)}, u32[]{:S(2)}, u32[]{:S(2)}) collective-permute-start(f32[1,8,256]{2,1,0:T(8,128)S(1)} %get-tuple-element.141), channel_id=1, source_target_pairs={{0,64},{64,128},{128,192},{192,256},{256,320},{320,384},{384,448},... | collective-permute-start | bytes 24584 | tf_op jit(solution)/shard_map/ppermute | solution.py:21
  297.9 9.9 %collective-permute-start.10 = (f32[6,1,256]{2,1,0:T(1,128)S(1)}, f32[6,1,256]{2,1,0:T(1,128)S(1)}, u32[]{:S(2)}, u32[]{:S(2)}) collective-permute-start(f32[6,1,256]{2,1,0:T(1,128)S(1)} %get-tuple-element.131), channel_id=1, source_target_pairs={{1,0},{2,1},{3,2},{4,3},{5,4},{6,5},{7,6},{8,7},{9,8},{10,9},{11,1... | collective-permute-start | bytes 18440 | tf_op jit(solution)/shard_map/ppermute | solution.py:22
  301.7 6.7 %collective-permute-start.11 = (f32[6,1,256]{2,1,0:T(1,128)S(1)}, f32[6,1,256]{2,1,0:T(1,128)S(1)}, u32[]{:S(2)}, u32[]{:S(2)}) collective-permute-start(f32[6,1,256]{2,1,0:T(1,128)S(1)} %get-tuple-element.132), channel_id=1, source_target_pairs={{0,1},{1,2},{2,3},{3,4},{4,5},{5,6},{6,7},{7,8},{8,9},{9,10},{10,1... | collective-permute-start | bytes 18440 | tf_op jit(solution)/shard_map/ppermute | solution.py:21
  421.9 19.3 %copy-start.1 = (f32[3,4,8,256]{3,2,1,0:T(8,128)S(1)}, f32[3,4,8,256]{3,2,1,0:T(8,128)}, u32[]{:S(2)}) copy-start(f32[3,4,8,256]{3,2,1,0:T(8,128)} %param.2) | copy-start | bytes 294916
  421.9 7.4 %collective-permute-start.12 = (f32[1,8,256]{2,1,0:T(8,128)S(1)}, f32[1,8,256]{2,1,0:T(8,128)S(1)}, u32[]{:S(2)}, u32[]{:S(2)}) collective-permute-start(f32[1,8,256]{2,1,0:T(8,128)S(1)} %get-tuple-element.135), channel_id=1, source_target_pairs={{0,64},{64,128},{128,192},{192,256},{256,320},{320,384},{384,448},... | collective-permute-start | bytes 24584 | tf_op jit(solution)/shard_map/ppermute | solution.py:21
  425.2 4.9 collective-permute-start.13
  430.1 19.0 %collective-permute-start.14 = (f32[6,1,256]{2,1,0:T(1,128)S(1)}, f32[6,1,256]{2,1,0:T(1,128)S(1)}, u32[]{:S(2)}, u32[]{:S(2)}) collective-permute-start(f32[6,1,256]{2,1,0:T(1,128)S(1)} %get-tuple-element.130), channel_id=1, source_target_pairs={{0,1},{1,2},{2,3},{3,4},{4,5},{5,6},{6,7},{7,8},{8,9},{9,10},{10,1... | collective-permute-start | bytes 18440 | tf_op jit(solution)/shard_map/ppermute | solution.py:21
  439.2 9.9 %collective-permute-start.15 = (f32[6,1,256]{2,1,0:T(1,128)S(1)}, f32[6,1,256]{2,1,0:T(1,128)S(1)}, u32[]{:S(2)}, u32[]{:S(2)}) collective-permute-start(f32[6,1,256]{2,1,0:T(1,128)S(1)} %get-tuple-element.129), channel_id=1, source_target_pairs={{1,0},{2,1},{3,2},{4,3},{5,4},{6,5},{7,6},{8,7},{9,8},{10,9},{11,1... | collective-permute-start | bytes 18440 | tf_op jit(solution)/shard_map/ppermute | solution.py:22
  441.1 15.7 %collective-permute-start.20 = (f32[3,4,8,256]{3,2,1,0:T(8,128)S(1)}, f32[3,4,8,256]{3,2,1,0:T(8,128)S(1)}, u32[]{:S(2)}, u32[]{:S(2)}) collective-permute-start(f32[3,4,8,256]{3,2,1,0:T(8,128)S(1)} %copy-done.1), channel_id=1, source_target_pairs={{0,64},{64,128},{128,192},{192,256},{256,320},{320,384},{384,448},... | collective-permute-start | bytes 294920 | tf_op jit(solution)/shard_map/ppermute | solution.py:21
  443.1 13.8 %collective-permute-start.21 = (f32[3,4,8,256]{3,2,1,0:T(8,128)S(1)}, f32[3,4,8,256]{3,2,1,0:T(8,128)S(1)}, u32[]{:S(2)}, u32[]{:S(2)}) collective-permute-start(f32[3,4,8,256]{3,2,1,0:T(8,128)S(1)} %copy-done.1), channel_id=1, source_target_pairs={{64,0},{128,64},{192,128},{256,192},{320,256},{384,320},{448,384},... | collective-permute-start | bytes 294920 | tf_op jit(solution)/shard_map/ppermute | solution.py:22
  449.5 7.5 %collective-permute-start.16 = (f32[3,2,8,256]{3,2,1,0:T(8,128)S(1)}, f32[3,2,8,256]{3,2,1,0:T(8,128)S(1)}, u32[]{:S(2)}, u32[]{:S(2)}) collective-permute-start(f32[3,2,8,256]{3,2,1,0:T(8,128)S(1)} %get-tuple-element.115), channel_id=1, source_target_pairs={{0,64},{64,128},{128,192},{192,256},{256,320},{320,384},{384,448},... | collective-permute-start | bytes 147464 | tf_op jit(solution)/shard_map/ppermute | solution.py:21
  451.4 6.6 %collective-permute-start.17 = (f32[3,2,8,256]{3,2,1,0:T(8,128)S(1)}, f32[3,2,8,256]{3,2,1,0:T(8,128)S(1)}, u32[]{:S(2)}, u32[]{:S(2)}) collective-permute-start(f32[3,2,8,256]{3,2,1,0:T(8,128)S(1)} %get-tuple-element.116), channel_id=1, source_target_pairs={{64,0},{128,64},{192,128},{256,192},{320,256},{384,320},{448,384},... | collective-permute-start | bytes 147464 | tf_op jit(solution)/shard_map/ppermute | solution.py:22
  458.1 21.1 %collective-permute-start.18 = (f32[3,8,2,256]{3,2,1,0:T(2,128)S(1)}, f32[3,8,2,256]{3,2,1,0:T(2,128)S(1)}, u32[]{:S(2)}, u32[]{:S(2)}) collective-permute-start(f32[3,8,2,256]{3,2,1,0:T(2,128)S(1)} %get-tuple-element.91), channel_id=1, source_target_pairs={{0,1},{1,2},{2,3},{3,4},{4,5},{5,6},{6,7},{7,8},{8,9},{9,10},{10,1... | collective-permute-start | bytes 147464 | tf_op jit(solution)/shard_map/ppermute | solution.py:21
  467.3 11.8 %collective-permute-start.19 = (f32[3,8,2,256]{3,2,1,0:T(2,128)S(1)}, f32[3,8,2,256]{3,2,1,0:T(2,128)S(1)}, u32[]{:S(2)}, u32[]{:S(2)}) collective-permute-start(f32[3,8,2,256]{3,2,1,0:T(2,128)S(1)} %get-tuple-element.92), channel_id=1, source_target_pairs={{1,0},{2,1},{3,2},{4,3},{5,4},{6,5},{7,6},{8,7},{9,8},{10,9},{11,1... | collective-permute-start | bytes 147464 | tf_op jit(solution)/shard_map/ppermute | solution.py:22
  469.3 10.9 %collective-permute-start.22 = (f32[3,12,4,256]{3,2,1,0:T(4,128)S(1)}, f32[3,12,4,256]{3,2,1,0:T(4,128)S(1)}, u32[]{:S(2)}, u32[]{:S(2)}) collective-permute-start(f32[3,12,4,256]{3,2,1,0:T(4,128)S(1)} %get-tuple-element.74), channel_id=1, source_target_pairs={{0,1},{1,2},{2,3},{3,4},{4,5},{5,6},{6,7},{7,8},{8,9},{9,10},{10,1... | collective-permute-start | bytes 442376 | tf_op jit(solution)/shard_map/ppermute | solution.py:21
  477.2 11.3 %collective-permute-start.23 = (f32[3,12,4,256]{3,2,1,0:T(4,128)S(1)}, f32[3,12,4,256]{3,2,1,0:T(4,128)S(1)}, u32[]{:S(2)}, u32[]{:S(2)}) collective-permute-start(f32[3,12,4,256]{3,2,1,0:T(4,128)S(1)} %get-tuple-element.75), channel_id=1, source_target_pairs={{1,0},{2,1},{3,2},{4,3},{5,4},{6,5},{7,6},{8,7},{9,8},{10,9},{11,1... | collective-permute-start | bytes 442376 | tf_op jit(solution)/shard_map/ppermute | solution.py:22
where the time goes:
time: 495 us; the launch traced here: 494 us
  blocking collectives  335 us (68%)
  starting transfers between devices  116 us (23%)
  waiting for transfers between devices  28.7 us (6%)
  other arithmetic  6.83 us (1%)
    psum x2, blocking collectives, squares_sum(): return lax.psum(jnp.sum(residual * residual), ('py', 'pz'))  223 us
    psum x1, blocking collectives, body(): lax.psum(jnp.sum(direction * image_field), ('py', 'pz'))  111 us
    ppermute x12, starting transfers between devices, extended(): before = lax.ppermute(last, axis, up)  61.9 us
    ppermute x12, starting transfers between devices, extended(): after = lax.ppermute(leading, axis, down)  53.6 us
    ppermute x12, waiting for transfers between devices, extended(): after = lax.ppermute(leading, axis, down)  18.4 us
    ppermute x12, waiting for transfers between devices, extended(): before = lax.ppermute(last, axis, up)  10.4 us
  transfers between devices with their start and end apart: 24, of which 9 were waited for; matrix products, arithmetic and copies ran while one was open for 0% of the time, Pallas kernels for 0%

commit v1 on v0

v1 whole, which is shorter than its diff:
```python
import functools

import jax
import jax.numpy as jnp
from jax import lax
from jax.experimental import pallas as pl
from jax.experimental.pallas import tpu as pltpu
from jax.sharding import PartitionSpec as P

smag_coef = 0.1156
time_step = 0.2
strain_floor = 0.25

ROWS = 4
TILE = 8
SIDE = 4
WIDE = TILE + 2 * SIDE
SENT = 9


def rolled(x, shift, axis):
    return pltpu.roll(x, shift % x.shape[axis], axis)


def dx(f):
    n = f.ndim - 1
    return 0.5 * (rolled(f, -1, n) - rolled(f, 1, n))


def dz(f):
    n = f.ndim - 2
    return 0.5 * (rolled(f, -1, n) - rolled(f, 1, n))


def sublane():
    return lax.broadcasted_iota(jnp.int32, (TILE, 256), 0)


def pack_z(cot_ref, vel_ref, prev_ref, next_ref):
    row = sublane()
    for c in range(3):
        for y in range(ROWS):
            cot, vel = cot_ref[c, y], vel_ref[c, y]
            prev_ref[c, y] = jnp.where(row < 5, cot, rolled(vel, 5, 0))
            next_ref[c, y] = jnp.where(row >= 3, cot, rolled(vel, 3, 0))


def side_cot(row, zn, zp):
    return jnp.where(row < SIDE, zn, zp)


def side_vel(row, zn, zp):
    return jnp.where(row < SIDE, rolled(zn, 3, 0), rolled(zp, 5, 0))


def pack_y(cot_ref, vel_ref, zn_ref, zp_ref, prev_ref, next_ref):
    row = sublane()
    for out, order in ((prev_ref, (0, 1, 2, 3)), (next_ref, (3, 2, 1, 0))):
        for c in range(3):
            side = [side_cot(row, zn_ref[c, y], zp_ref[c, y]) for y in order]
            near = side_vel(row, zn_ref[c, order[0]], zp_ref[c, order[0]])
            for d in range(4):
                out[c, d] = cot_ref[c, order[d]]
            out[c, 4] = side[0]
            far = jnp.where(row == 4, rolled(side[3], 5, 0), side[1])
            out[c, 5] = jnp.where(row == 3, rolled(side[3], 3, 0), far)
            mid = jnp.where(row == 5, rolled(near, 6, 0), side[2])
            out[c, 6] = jnp.where(row == 2, rolled(near, 2, 0), mid)
            out[c, 7] = vel_ref[c, order[0]]
            out[c, 8] = vel_ref[c, order[1]]


def joined(a, b):
    return jnp.concatenate([a, b], axis=0)


def cot_frame(refs, row, c, y):
    cot_ref, vel_ref, zn_ref, zp_ref, yn_ref, yp_ref = refs
    if 0 <= y < ROWS:
        return joined(cot_ref[c, y], side_cot(row, zn_ref[c, y], zp_ref[c, y]))
    got, d = (yn_ref, y - ROWS) if y >= ROWS else (yp_ref, -1 - y)
    if d < 3:
        return joined(got[c, d], got[c, 4 + d])
    tile = got[c, 5]
    return joined(got[c, 3], jnp.where(row < SIDE, rolled(tile, 5, 0), rolled(tile, 3, 0)))


def vel_frame(refs, row, c, y):
    cot_ref, vel_ref, zn_ref, zp_ref, yn_ref, yp_ref = refs
    if 0 <= y < ROWS:
        return joined(vel_ref[c, y], side_vel(row, zn_ref[c, y], zp_ref[c, y]))
    got, d = (yn_ref, y - ROWS) if y >= ROWS else (yp_ref, -1 - y)
    if d == 0:
        tile = got[c, 6]
        return joined(got[c, 7], jnp.where(row < SIDE, rolled(tile, 6, 0), rolled(tile, 2, 0)))
    return joined(got[c, 8], got[c, 8])


def along_z_cot(refs, row, frame, y):
    if not 0 <= y < ROWS:
        return dz(frame)
    zn_ref, zp_ref = refs[2], refs[3]
    ends = jnp.where(row < SIDE, zp_ref[2, y], zn_ref[2, y])
    wide = lax.broadcasted_iota(jnp.int32, (WIDE, 256), 0)
    both = joined(ends, ends)
    after = jnp.where(wide == TILE + 3, rolled(both, -1, 0), rolled(frame, -1, 0))
    before = jnp.where(wide == TILE + 4, rolled(both, 1, 0), rolled(frame, 1, 0))
    return 0.5 * (after - before)


def laplace(here, below, above):
    beside = rolled(here, 1, 1) + rolled(here, -1, 1)
    beside = beside + above + below
    beside = beside + rolled(here, 1, 0) + rolled(here, -1, 0)
    return 6.0 * here - beside


def ratio(top, bottom):
    safe = bottom > 0.0
    return jnp.where(safe, top / jnp.where(safe, bottom, 1.0), 0.0)


def total(x):
    return jnp.sum(jnp.sum(x, axis=0, keepdims=True), axis=1, keepdims=True)


def moments(peers, place_ref, cot_ref, vel_ref, zn_ref, zp_ref, yn_ref, yp_ref, out_ref, b_ref, w_ref):
    refs = (cot_ref, vel_ref, zn_ref, zp_ref, yn_ref, yp_ref)
    row = sublane()
    cot_y = {y: cot_frame(refs, row, 1, y) for y in range(-4, 8)}
    b = {}
    for y in range(-3, 7):
        flat = dx(cot_frame(refs, row, 0, y)) + along_z_cot(refs, row, cot_frame(refs, row, 2, y), y)
        b[y] = -(flat + 0.5 * (cot_y[y + 1] - cot_y[y - 1]))
        b_ref[y + 3] = b[y]
    w = {}
    for y in range(-2, 6):
        w[y] = laplace(b[y], b[y - 1], b[y + 1])
        w_ref[y + 2] = w[y]
    m0 = m1 = None
    for y in range(ROWS):
        bc, wc = b[y][:TILE], w[y][:TILE]
        m0 = bc * bc if m0 is None else m0 + bc * bc
        m1 = bc * wc if m1 is None else m1 + bc * wc
    m0, m1 = total(m0), total(m1)
    sigma = ratio(m1, m0)
    spread = third = cross = None
    for y in range(ROWS):
        bc, wc = b[y][:TILE], w[y][:TILE]
        x = laplace(w[y], w[y - 1], w[y + 1])[:TILE]
        v = wc - sigma * bc
        u = x - sigma * wc
        spread = v * v if spread is None else spread + v * v
        third = v * u if third is None else third + v * u
        cross = bc * u if cross is None else cross + bc * u
    spread, third, cross = total(spread), total(third), total(cross)
    line = lax.broadcasted_iota(jnp.int32, (TILE, 128), 0)
    tile = jnp.zeros((TILE, 128), jnp.float32)
    for k, value in enumerate((m0, m1, spread, third, cross)):
        tile = jnp.where(line == k, value, tile)
    place = place_ref[0]
    for j in range(peers):
        ahead = lax.rem(j - place + peers, peers)
        up = jnp.where(ahead < peers // 2, 1.0, 0.0)
        out_ref[j, :, :256] = jnp.where(up > 0.5, cot_ref[1, ROWS - 1], cot_ref[1, 0])
        out_ref[j, :, 256:] = tile


def merged(m0, m1, spread, third, cross):
    own = ratio(m1, m0)

    def over(x):
        return jnp.sum(x, axis=0, keepdims=True)

    all0, all1 = over(m0), over(m1)
    delta = ratio(all1, all0) - own
    all_spread = over(spread + delta * delta * m0)
    all_third = over(third - delta * (spread + cross) + delta * delta * m1)
    all_cross = over(cross - delta * m1)
    return all0, all1, all_spread, all_third, all_cross


def merge(got_ref, out_ref):
    parts = merged(*[got_ref[:, k, 256:] for k in range(5)])
    lane = lax.broadcasted_iota(jnp.int32, (1, 128), 1)
    line = jnp.zeros((1, 128), jnp.float32)
    for k, value in enumerate(parts):
        line = jnp.where(lane == k, value, line)
    for j in range(out_ref.shape[0]):
        out_ref[j] = line


def finish(peers, place_ref, cot_ref, vel_ref, zn_ref, zp_ref, yn_ref, yp_ref, far_ref, b_ref, w_ref, sums_ref, out_ref):
    refs = (cot_ref, vel_ref, zn_ref, zp_ref, yn_ref, yp_ref)
    row = sublane()
    sums = sums_ref[...].reshape(sums_ref.shape[0], 128)
    m0, m1, spread, third, _ = [x[:, :1] for x in merged(*[rolled(sums, -k, 1) for k in range(5)])]
    step0 = m0 / m1
    norm1 = step0 * step0 * spread
    beta = norm1 / m0
    bend = step0 * step0 * third - 2.0 * step0 * beta * spread + beta * beta * m1
    step1 = norm1 / bend
    coef_b = step0 + step1 * (1.0 + beta)
    coef_w = -(step1 * step0)

    place = place_ref[0]
    above = far_ref[lax.rem(place + 2, peers), :, :256]
    below = far_ref[lax.rem(place + peers - 2, peers), :, :256]
    above, below = joined(above, above), joined(below, below)
    cot = {(c, y): cot_frame(refs, row, c, y) for c in range(3) for y in range(-4, 8)}
    b = {y: b_ref[y + 3] for y in range(-3, 7)}
    b[-4] = -(dx(cot[0, -4]) + dz(cot[2, -4]) + 0.5 * (cot[1, -3] - below))
    b[7] = -(dx(cot[0, 7]) + dz(cot[2, 7]) + 0.5 * (above - cot[1, 6]))
    w = {y: w_ref[y + 2] for y in range(-2, 6)}
    w[-3] = laplace(b[-3], b[-4], b[-2])
    w[6] = laplace(b[6], b[5], b[7])
    p = {y: coef_b * b[y] + coef_w * w[y] for y in range(-3, 7)}
    lam = {}
    for y in range(-2, 6):
        lam[0, y] = cot[0, y] - dx(p[y])
        lam[1, y] = cot[1, y] - 0.5 * (p[y + 1] - p[y - 1])
        lam[2, y] = cot[2, y] - dz(p[y])
    vel = {(c, y): vel_frame(refs, row, c, y) for c in range(3) for y in range(-2, 6)}

    flat, upright = {}, {}
    for y in range(-1, 5):
        grad = [[dx(vel[i, y]), 0.5 * (vel[i, y + 1] - vel[i, y - 1]), dz(vel[i, y])] for i in range(3)]
        pull = [[dx(lam[i, y]), 0.5 * (lam[i, y + 1] - lam[i, y - 1]), dz(lam[i, y])] for i in range(3)]
        strain, ebb = {}, {}
        for i in range(3):
            for j in range(i + 1):
                strain[i, j] = grad[i][i] if i == j else 0.5 * (grad[i][j] + grad[j][i])
                ebb[i, j] = pull[i][i] if i == j else 0.5 * (pull[i][j] + pull[j][i])
        squares = strain[0, 0] * strain[0, 0] + strain[1, 1] * strain[1, 1] + strain[2, 2] * strain[2, 2]
        work = strain[0, 0] * ebb[0, 0] + strain[1, 1] * ebb[1, 1] + strain[2, 2] * ebb[2, 2]
        off = strain[1, 0] * strain[1, 0] + strain[2, 0] * strain[2, 0] + strain[2, 1] * strain[2, 1]
        off_work = strain[1, 0] * ebb[1, 0] + strain[2, 0] * ebb[2, 0] + strain[2, 1] * ebb[2, 1]
        inside = 2.0 * (squares + 2.0 * off) + strain_floor
        inverse = lax.rsqrt(inside)
        twice = (2.0 * smag_coef) * (inside * inverse)
        factor = (4.0 * smag_coef) * inverse * (work + 2.0 * off_work)
        stress = {key: twice * ebb[key] + factor * strain[key] for key in strain}

        def both(i, j):
            return stress[max(i, j), min(i, j)] + lam[i, y] * vel[j, y]

        for i in range(3):
            upright[i, y] = both(i, 1)[:TILE]
        if 0 <= y < ROWS:
            for i in range(3):
                carried = lam[0, y] * grad[0][i] + lam[1, y] * grad[1][i] + lam[2, y] * grad[2][i]
                level = dx(both(i, 0)) + dz(both(i, 2))
                flat[i, y] = (lam[i, y] + time_step * (level - carried))[:TILE]
    for i in range(3):
        for y in range(ROWS):
            out_ref[i, y] = flat[i, y] + (0.5 * time_step) * (upright[i, y + 1] - upright[i, y - 1])


def call(kernel, outs, scalars, arrays):
    vmem = pl.BlockSpec(memory_space=pltpu.VMEM)
    smem = pl.BlockSpec(memory_space=pltpu.SMEM)
    return pl.pallas_call(
        kernel,
        out_shape=[jax.ShapeDtypeStruct(s, jnp.float32) for s in outs],
        in_specs=[smem] * len(scalars) + [vmem] * len(arrays),
        out_specs=[vmem] * len(outs),
        compiler_params=pltpu.CompilerParams(vmem_limit_bytes=32 * 1024 * 1024),
    )(*scalars, *arrays)


def both_ways(to_prev, to_next, axis):
    n = lax.axis_size(axis)
    up = [(i, (i + 1) % n) for i in range(n)]
    down = [(j, i) for i, j in up]
    from_next = lax.ppermute(to_prev, axis, down)
    from_prev = lax.ppermute(to_next, axis, up)
    return from_next, from_prev


def body(velocity, cotangent):
    ny, nz = lax.axis_size("py"), lax.axis_size("pz")
    place = lax.axis_index("py").astype(jnp.int32).reshape(1)
    block = (3, ROWS, TILE, 256)
    to_prev, to_next = call(pack_z, [block, block], [], [cotangent, velocity])
    zn, zp = both_ways(to_prev, to_next, "pz")
    sent = (3, SENT, TILE, 256)
    to_prev, to_next = call(pack_y, [sent, sent], [], [cotangent, velocity, zn, zp])
    yn, yp = both_ways(to_prev, to_next, "py")
    held = [cotangent, velocity, zn, zp, yn, yp]
    chunks, b, w = call(
        functools.partial(moments, ny),
        [(ny, TILE, 384), (10, WIDE, 256), (8, WIDE, 256)],
        [place],
        held,
    )
    got = lax.all_to_all(chunks, "py", 0, 0)
    (lines,) = call(merge, [(nz, 1, 128)], [], [got])
    sums = lax.all_to_all(lines, "pz", 0, 0)
    (out,) = call(functools.partial(finish, ny), [block], [place], held + [got, b, w, sums])
    return out


def solution(mesh):
    placed = (P(None, "py", "pz", None), P(None, "py", "pz", None))
    return jax.shard_map(
        body, mesh=mesh, in_specs=placed, out_specs=P(None, "py", "pz", None), check_vma=False
    )
```

time: 495 us -> 81.6 us (0.16)
  the two profiles are of different devices: /device:TPU:47 before, /device:TPU:1 now
where the time goes in v1:
time: 81.6 us; the launch traced here: 81.3 us
  blocking collectives  38.5 us (47%)
  starting transfers between devices  30.5 us (37%)
  waiting for transfers between devices  8.46 us (10%)
  Pallas kernels  1.86 us (2%)
  local copies, waits for them, and re-layouts  1.8 us (2%)
    all_to_all x1, blocking collectives, body(): sums = lax.all_to_all(lines, 'pz', 0, 0)  28.4 us
    ppermute x2, starting transfers between devices, both_ways(): from_next = lax.ppermute(to_prev, axis, down)  26.5 us
    all_to_all x1, blocking collectives, body(): got = lax.all_to_all(chunks, 'py', 0, 0)  10.1 us
    ppermute x2, waiting for transfers between devices, both_ways(): from_prev = lax.ppermute(to_next, axis, up)  7.54 us
    ppermute x2, starting transfers between devices, both_ways(): from_prev = lax.ppermute(to_next, axis, up)  3.97 us
    pallas_call x5, Pallas kernels, call(): pl.pallas_call(kernel, out_shape=[jax.ShapeDtypeStruct(s, jnp.float32) fo...  1.86 us
    unnamed x8, local copies, waits for them, and re-layouts  1.8 us
  transfers between devices with their start and end apart: 4, of which 3 were waited for; matrix products, arithmetic and copies ran while one was open for 0% of the time, Pallas kernels for 0%

profile of v1, /device:TPU:1, one launch (start us, length us, event | category | flops | bytes accessed | tf_op | source)
XLA Modules:
  0.0 81.3 jit_solution(17616106030563050382)
XLA Ops:
  0.0 0.0 copy-start
  0.0 0.9 %copy-done = f32[3,4,8,256]{3,2,1,0:T(8,128)S(1)} copy-done((f32[3,4,8,256]{3,2,1,0:T(8,128)S(1)}, f32[3,4,8,256]{3,2,1,0:T(8,128)}, u32[]{:S(2)}) %copy-start) | copy-done | bytes 98328
  0.9 0.0 copy-start.2
  0.9 0.9 %copy-done.2 = f32[3,4,8,256]{3,2,1,0:T(8,128)S(1)} copy-done((f32[3,4,8,256]{3,2,1,0:T(8,128)S(1)}, f32[3,4,8,256]{3,2,1,0:T(8,128)}, u32[]{:S(2)}) %copy-start.2) | copy-done | bytes 98328
  1.8 16.1 %collective-permute-start = (f32[3,4,8,256]{3,2,1,0:T(8,128)S(1)}, f32[3,4,8,256]{3,2,1,0:T(8,128)S(1)}, u32[]{:S(2)}, u32[]{:S(2)}) collective-permute-start(f32[3,4,8,256]{3,2,1,0:T(8,128)S(1)} %get-tuple-element.12), channel_id=1, source_target_pairs={{1,0},{2,1},{3,2},{4,3},{5,4},{6,5},{7,6},{8,7},{9,8},{10,9},{11,1... | collective-permute-start | bytes 294920 | tf_op jit(solution)/shard_map/ppermute | solution.py:275
  17.9 0.0 copy-start.1
  17.9 0.0 copy-start.3
  17.9 2.1 %collective-permute-start.1 = (f32[3,4,8,256]{3,2,1,0:T(8,128)S(1)}, f32[3,4,8,256]{3,2,1,0:T(8,128)S(1)}, u32[]{:S(2)}, u32[]{:S(2)}) collective-permute-start(f32[3,4,8,256]{3,2,1,0:T(8,128)S(1)} %get-tuple-element.13), channel_id=1, source_target_pairs={{0,1},{1,2},{2,3},{3,4},{4,5},{5,6},{6,7},{7,8},{8,9},{9,10},{10,1... | collective-permute-start | bytes 294920 | tf_op jit(solution)/shard_map/ppermute | solution.py:276
  20.0 0.0 collective-permute-done.zn_ref
  20.0 1.6 %collective-permute-done.1.zp_ref = f32[3,4,8,256]{3,2,1,0:T(8,128)S(1)} collective-permute-done((f32[3,4,8,256]{3,2,1,0:T(8,128)S(1)}, f32[3,4,8,256]{3,2,1,0:T(8,128)S(1)}, u32[]{:S(2)}, u32[]{:S(2)}) %collective-permute-start.1) | collective-permute-done | bytes 98336 | tf_op jit(solution)/shard_map/ppermute | solution.py:276
  21.6 10.5 %collective-permute-start.2 = (f32[3,9,8,256]{3,2,1,0:T(8,128)S(1)}, f32[3,9,8,256]{3,2,1,0:T(8,128)S(1)}, u32[]{:S(2)}, u32[]{:S(2)}) collective-permute-start(f32[3,9,8,256]{3,2,1,0:T(8,128)S(1)} %get-tuple-element.14), channel_id=1, source_target_pairs={{64,0},{128,64},{192,128},{256,192},{320,256},{384,320},{448,384},... | collective-permute-start | bytes 663560 | tf_op jit(solution)/shard_map/ppermute | solution.py:275
  32.1 1.9 %collective-permute-start.3 = (f32[3,9,8,256]{3,2,1,0:T(8,128)S(1)}, f32[3,9,8,256]{3,2,1,0:T(8,128)S(1)}, u32[]{:S(2)}, u32[]{:S(2)}) collective-permute-start(f32[3,9,8,256]{3,2,1,0:T(8,128)S(1)} %get-tuple-element.15), channel_id=1, source_target_pairs={{0,64},{64,128},{128,192},{192,256},{256,320},{320,384},{384,448},... | collective-permute-start | bytes 663560 | tf_op jit(solution)/shard_map/ppermute | solution.py:276
  34.0 0.9 %collective-permute-done.2.yn_ref = f32[3,9,8,256]{3,2,1,0:T(8,128)S(1)} collective-permute-done((f32[3,9,8,256]{3,2,1,0:T(8,128)S(1)}, f32[3,9,8,256]{3,2,1,0:T(8,128)S(1)}, u32[]{:S(2)}, u32[]{:S(2)}) %collective-permute-start.2) | collective-permute-done | bytes 221216 | tf_op jit(solution)/shard_map/ppermute | solution.py:275
  35.0 5.9 %collective-permute-done.3.yp_ref = f32[3,9,8,256]{3,2,1,0:T(8,128)S(1)} collective-permute-done((f32[3,9,8,256]{3,2,1,0:T(8,128)S(1)}, f32[3,9,8,256]{3,2,1,0:T(8,128)S(1)}, u32[]{:S(2)}, u32[]{:S(2)}) %collective-permute-start.3) | collective-permute-done | bytes 221216 | tf_op jit(solution)/shard_map/ppermute | solution.py:276
  40.9 0.0 copy-done.1
  40.9 0.0 copy-done.3
  40.9 0.4 shard_map.30
  41.3 10.1 %all_to_all.10.got_ref.far_ref = f32[16,8,384]{2,1,0:T(8,128)S(1)} all-to-all(f32[16,8,384]{2,1,0:T(8,128)S(1)} %get-tuple-element.16), channel_id=1, replica_groups=mesh['py'=16,'pz'=64] {'py'}, dimensions={0} | all-to-all | bytes 393216 | tf_op jit(solution)/shard_map/all_to_all | solution.py:296
  51.4 0.1 shard_map.31
  51.5 28.4 %all_to_all.11.sums_ref = f32[64,1,128]{2,1,0:T(1,128)S(1)} all-to-all(f32[64,1,128]{2,1,0:T(1,128)S(1)} %shard_map.31), channel_id=1, replica_groups=mesh['py'=16,'pz'=64] {'pz'}, dimensions={0} | all-to-all | bytes 65536 | tf_op jit(solution)/shard_map/all_to_all | solution.py:298
  79.9 1.4 %shard_map.32 = f32[3,4,8,256]{3,2,1,0:T(8,128)} custom-call(s32[1]{0:T(128)} %bitcast.place_ref, f32[3,4,8,256]{3,2,1,0:T(8,128)S(1)} %copy-done.1, f32[3,4,8,256]{3,2,1,0:T(8,128)S(1)} %copy-done.3, f32[3,4,8,256]{3,2,1,0:T(8,128)S(1)} %collective-permute-done.zn_ref, f32[3,4,8,256]{3,2,1,0:T(8,128)S(1)} %collective-permute-done.1.zp_ref, ...), custom_call_target="tpu_custom_call" | custom-call | tf_op jit(solution)/shard_map/pallas_call | solution.py:262
  (2 shorter events, 0.0 us)
Async XLA Ops:
  0.0 0.9 %copy-start = (f32[3,4,8,256]{3,2,1,0:T(8,128)S(1)}, f32[3,4,8,256]{3,2,1,0:T(8,128)}, u32[]{:S(2)}) copy-start(f32[3,4,8,256]{3,2,1,0:T(8,128)} %cot_ref.7) | copy-start | bytes 294916
  0.9 0.9 %copy-start.2 = (f32[3,4,8,256]{3,2,1,0:T(8,128)S(1)}, f32[3,4,8,256]{3,2,1,0:T(8,128)}, u32[]{:S(2)}) copy-start(f32[3,4,8,256]{3,2,1,0:T(8,128)} %vel_ref.7) | copy-start | bytes 294916
  1.8 18.2 %collective-permute-start = (f32[3,4,8,256]{3,2,1,0:T(8,128)S(1)}, f32[3,4,8,256]{3,2,1,0:T(8,128)S(1)}, u32[]{:S(2)}, u32[]{:S(2)}) collective-permute-start(f32[3,4,8,256]{3,2,1,0:T(8,128)S(1)} %get-tuple-element.12), channel_id=1, source_target_pairs={{1,0},{2,1},{3,2},{4,3},{5,4},{6,5},{7,6},{8,7},{9,8},{10,9},{11,1... | collective-permute-start | bytes 294920 | tf_op jit(solution)/shard_map/ppermute | solution.py:275
  17.9 23.0 %copy-start.1 = (f32[3,4,8,256]{3,2,1,0:T(8,128)S(1)}, f32[3,4,8,256]{3,2,1,0:T(8,128)}, u32[]{:S(2)}) copy-start(f32[3,4,8,256]{3,2,1,0:T(8,128)} %cot_ref.7) | copy-start | bytes 294916
  17.9 23.0 %copy-start.3 = (f32[3,4,8,256]{3,2,1,0:T(8,128)S(1)}, f32[3,4,8,256]{3,2,1,0:T(8,128)}, u32[]{:S(2)}) copy-start(f32[3,4,8,256]{3,2,1,0:T(8,128)} %vel_ref.7) | copy-start | bytes 294916
  17.9 3.7 %collective-permute-start.1 = (f32[3,4,8,256]{3,2,1,0:T(8,128)S(1)}, f32[3,4,8,256]{3,2,1,0:T(8,128)S(1)}, u32[]{:S(2)}, u32[]{:S(2)}) collective-permute-start(f32[3,4,8,256]{3,2,1,0:T(8,128)S(1)} %get-tuple-element.13), channel_id=1, source_target_pairs={{0,1},{1,2},{2,3},{3,4},{4,5},{5,6},{6,7},{7,8},{8,9},{9,10},{10,1... | collective-permute-start | bytes 294920 | tf_op jit(solution)/shard_map/ppermute | solution.py:276
  21.6 13.3 %collective-permute-start.2 = (f32[3,9,8,256]{3,2,1,0:T(8,128)S(1)}, f32[3,9,8,256]{3,2,1,0:T(8,128)S(1)}, u32[]{:S(2)}, u32[]{:S(2)}) collective-permute-start(f32[3,9,8,256]{3,2,1,0:T(8,128)S(1)} %get-tuple-element.14), channel_id=1, source_target_pairs={{64,0},{128,64},{192,128},{256,192},{320,256},{384,320},{448,384},... | collective-permute-start | bytes 663560 | tf_op jit(solution)/shard_map/ppermute | solution.py:275
  32.1 8.8 %collective-permute-start.3 = (f32[3,9,8,256]{3,2,1,0:T(8,128)S(1)}, f32[3,9,8,256]{3,2,1,0:T(8,128)S(1)}, u32[]{:S(2)}, u32[]{:S(2)}) collective-permute-start(f32[3,9,8,256]{3,2,1,0:T(8,128)S(1)} %get-tuple-element.15), channel_id=1, source_target_pairs={{0,64},{64,128},{128,192},{192,256},{256,320},{320,384},{384,448},... | collective-permute-start | bytes 663560 | tf_op jit(solution)/shard_map/ppermute | solution.py:276

commit v2 on v1

--- a/solution.py
+++ b/solution.py
@@ -15,7 +15,7 @@
 TILE = 8
 SIDE = 4
 WIDE = TILE + 2 * SIDE
-SENT = 9
+SENT = 20
 
 
 def rolled(x, shift, axis):
@@ -36,7 +36,15 @@
     return lax.broadcasted_iota(jnp.int32, (TILE, 256), 0)
 
 
-def pack_z(cot_ref, vel_ref, prev_ref, next_ref):
+def pack_z(cot_hbm, vel_hbm, prev_ref, next_ref, cot_ref, vel_ref, sems):
+    copies = [
+        pltpu.make_async_copy(cot_hbm, cot_ref, sems.at[0]),
+        pltpu.make_async_copy(vel_hbm, vel_ref, sems.at[1]),
+    ]
+    for copy in copies:
+        copy.start()
+    for copy in copies:
+        copy.wait()
     row = sublane()
     for c in range(3):
         for y in range(ROWS):
@@ -53,25 +61,49 @@
     return jnp.where(row < SIDE, rolled(zn, 3, 0), rolled(zp, 5, 0))
 
 
-def pack_y(cot_ref, vel_ref, zn_ref, zp_ref, prev_ref, next_ref):
-    row = sublane()
-    for out, order in ((prev_ref, (0, 1, 2, 3)), (next_ref, (3, 2, 1, 0))):
-        for c in range(3):
-            side = [side_cot(row, zn_ref[c, y], zp_ref[c, y]) for y in order]
-            near = side_vel(row, zn_ref[c, order[0]], zp_ref[c, order[0]])
-            for d in range(4):
-                out[c, d] = cot_ref[c, order[d]]
-            out[c, 4] = side[0]
-            far = jnp.where(row == 4, rolled(side[3], 5, 0), side[1])
-            out[c, 5] = jnp.where(row == 3, rolled(side[3], 3, 0), far)
-            mid = jnp.where(row == 5, rolled(near, 6, 0), side[2])
-            out[c, 6] = jnp.where(row == 2, rolled(near, 2, 0), mid)
-            out[c, 7] = vel_ref[c, order[0]]
-            out[c, 8] = vel_ref[c, order[1]]
+def put(row, tile, k):
+    return jnp.where(row < SIDE, rolled(tile, k, 0), rolled(tile, -k, 0))
+
+
+def take(row, tile, k):
+    return jnp.where(row < SIDE, rolled(tile, -k, 0), rolled(tile, k, 0))
+
+
+def mixed(row, base, inner):
+    for k, tile in inner:
+        base = jnp.where((row == k) | (row == TILE - 1 - k), put(row, tile, k), base)
+    return base
 
 
 def joined(a, b):
     return jnp.concatenate([a, b], axis=0)
+
+
+def pack_y(cot_ref, vel_ref, zn_ref, zp_ref, prev_ref, next_ref):
+    refs = (cot_ref, vel_ref, zn_ref, zp_ref, None, None)
+    row = sublane()
+    cot = {(c, y): cot_frame(refs, row, c, y) for c in range(3) for y in range(ROWS)}
+    flat = {y: -(dx(cot[0, y]) + along_z_cot(refs, row, cot[2, y], y)) for y in range(ROWS)}
+    low = flat[0] - 0.5 * cot[1, 1]
+    high = flat[3] + 0.5 * cot[1, 2]
+    one = flat[1] - 0.5 * (cot[1, 2] - cot[1, 0])
+    two = flat[2] - 0.5 * (cot[1, 3] - cot[1, 1])
+    for out, part, (d1, d2) in (
+        (prev_ref, (low, one, two, high), (0, 1)),
+        (next_ref, (high, two, one, low), (3, 2)),
+    ):
+        for d in range(4):
+            out[d] = part[d][:TILE]
+        for c in range(3):
+            out[4 + c] = cot_ref[c, d1]
+            out[7 + c] = cot_ref[c, d2]
+            out[10 + c] = vel_ref[c, d1]
+            out[13 + c] = vel_ref[c, d2]
+        vel = [side_vel(row, zn_ref[c, d1], zp_ref[c, d1]) for c in range(3)]
+        out[16] = mixed(row, part[0][TILE:], [(3, part[2][TILE:])])
+        out[17] = mixed(row, part[1][TILE:], [(2, cot[0, d1][TILE:]), (3, cot[2, d1][TILE:])])
+        out[18] = mixed(row, vel[0], [(1, vel[1]), (2, vel[2])])
+        out[19] = cot[1, d1][TILE:]
 
 
 def cot_frame(refs, row, c, y):
@@ -79,10 +111,9 @@
     if 0 <= y < ROWS:
         return joined(cot_ref[c, y], side_cot(row, zn_ref[c, y], zp_ref[c, y]))
     got, d = (yn_ref, y - ROWS) if y >= ROWS else (yp_ref, -1 - y)
-    if d < 3:
-        return joined(got[c, d], got[c, 4 + d])
-    tile = got[c, 5]
-    return joined(got[c, 3], jnp.where(row < SIDE, rolled(tile, 5, 0), rolled(tile, 3, 0)))
+    if d == 1:
+        return joined(got[7 + c], got[7 + c])
+    return joined(got[4 + c], got[19] if c == 1 else take(row, got[17], 2 if c == 0 else 3))
 
 
 def vel_frame(refs, row, c, y):
@@ -90,10 +121,20 @@
     if 0 <= y < ROWS:
         return joined(vel_ref[c, y], side_vel(row, zn_ref[c, y], zp_ref[c, y]))
     got, d = (yn_ref, y - ROWS) if y >= ROWS else (yp_ref, -1 - y)
+    if d == 1:
+        return joined(got[13 + c], got[13 + c])
+    return joined(got[10 + c], take(row, got[18], c))
+
+
+def part_frame(refs, row, y):
+    got, d = (refs[4], y - ROWS) if y >= ROWS else (refs[5], -1 - y)
     if d == 0:
-        tile = got[c, 6]
-        return joined(got[c, 7], jnp.where(row < SIDE, rolled(tile, 6, 0), rolled(tile, 2, 0)))
-    return joined(got[c, 8], got[c, 8])
+        return joined(got[0], got[16])
+    if d == 1:
+        return joined(got[1], got[17])
+    if d == 2:
+        return joined(got[2], take(row, got[16], 3))
+    return joined(got[3], got[3])
 
 
 def along_z_cot(refs, row, frame, y):
@@ -127,11 +168,14 @@
 def moments(peers, place_ref, cot_ref, vel_ref, zn_ref, zp_ref, yn_ref, yp_ref, out_ref, b_ref, w_ref):
     refs = (cot_ref, vel_ref, zn_ref, zp_ref, yn_ref, yp_ref)
     row = sublane()
-    cot_y = {y: cot_frame(refs, row, 1, y) for y in range(-4, 8)}
-    b = {}
-    for y in range(-3, 7):
+    cot_y = {y: cot_frame(refs, row, 1, y) for y in range(-1, 5)}
+    b = {y: part_frame(refs, row, y) for y in (-3, -2, -1, 4, 5, 6)}
+    b[-1] = b[-1] - 0.5 * cot_y[0]
+    b[4] = b[4] + 0.5 * cot_y[3]
+    for y in range(ROWS):
         flat = dx(cot_frame(refs, row, 0, y)) + along_z_cot(refs, row, cot_frame(refs, row, 2, y), y)
         b[y] = -(flat + 0.5 * (cot_y[y + 1] - cot_y[y - 1]))
+    for y in range(-3, 7):
         b_ref[y + 3] = b[y]
     w = {}
     for y in range(-2, 6):
@@ -207,10 +251,10 @@
     above = far_ref[lax.rem(place + 2, peers), :, :256]
     below = far_ref[lax.rem(place + peers - 2, peers), :, :256]
     above, below = joined(above, above), joined(below, below)
-    cot = {(c, y): cot_frame(refs, row, c, y) for c in range(3) for y in range(-4, 8)}
+    cot = {(c, y): cot_frame(refs, row, c, y) for c in range(3) for y in range(-2, 6)}
     b = {y: b_ref[y + 3] for y in range(-3, 7)}
-    b[-4] = -(dx(cot[0, -4]) + dz(cot[2, -4]) + 0.5 * (cot[1, -3] - below))
-    b[7] = -(dx(cot[0, 7]) + dz(cot[2, 7]) + 0.5 * (above - cot[1, 6]))
+    b[-4] = part_frame(refs, row, -4) + 0.5 * below
+    b[7] = part_frame(refs, row, 7) - 0.5 * above
     w = {y: w_ref[y + 2] for y in range(-2, 6)}
     w[-3] = laplace(b[-3], b[-4], b[-2])
     w[6] = laplace(b[6], b[5], b[7])
@@ -256,14 +300,16 @@
             out_ref[i, y] = flat[i, y] + (0.5 * time_step) * (upright[i, y + 1] - upright[i, y - 1])
 
 
-def call(kernel, outs, scalars, arrays):
+def call(kernel, outs, scalars, arrays, place=pltpu.VMEM, scratch=()):
     vmem = pl.BlockSpec(memory_space=pltpu.VMEM)
+    given = pl.BlockSpec(memory_space=place)
     smem = pl.BlockSpec(memory_space=pltpu.SMEM)
     return pl.pallas_call(
         kernel,
         out_shape=[jax.ShapeDtypeStruct(s, jnp.float32) for s in outs],
-        in_specs=[smem] * len(scalars) + [vmem] * len(arrays),
+        in_specs=[smem] * len(scalars) + [given] * len(arrays),
         out_specs=[vmem] * len(outs),
+        scratch_shapes=list(scratch),
         compiler_params=pltpu.CompilerParams(vmem_limit_bytes=32 * 1024 * 1024),
     )(*scalars, *arrays)
 
@@ -281,9 +327,12 @@
     ny, nz = lax.axis_size("py"), lax.axis_size("pz")
     place = lax.axis_index("py").astype(jnp.int32).reshape(1)
     block = (3, ROWS, TILE, 256)
-    to_prev, to_next = call(pack_z, [block, block], [], [cotangent, velocity])
+    dmas = [pltpu.SemaphoreType.DMA((2,))]
+    to_prev, to_next, cotangent, velocity = call(
+        pack_z, [block] * 4, [], [cotangent, velocity], pl.ANY, dmas
+    )
     zn, zp = both_ways(to_prev, to_next, "pz")
-    sent = (3, SENT, TILE, 256)
+    sent = (SENT, TILE, 256)
     to_prev, to_next = call(pack_y, [sent, sent], [], [cotangent, velocity, zn, zp])
     yn, yp = both_ways(to_prev, to_next, "py")
     held = [cotangent, velocity, zn, zp, yn, yp]

time: 81.6 us -> 81 us (level)
    unnamed x8 -> x4, local copies, waits for them, and re-layouts: 1.8 us -> 1.78 us
where the time goes in v2:
time: 81 us; the launch traced here: 80.6 us
  blocking collectives  38.4 us (47%)
  starting transfers between devices  30.4 us (38%)
  waiting for transfers between devices  7.85 us (10%)
  Pallas kernels  2.15 us (3%)
  local copies, waits for them, and re-layouts  1.78 us (2%)
    all_to_all x1, blocking collectives, body(): sums = lax.all_to_all(lines, 'pz', 0, 0)  28.2 us
    ppermute x2, starting transfers between devices, both_ways(): from_next = lax.ppermute(to_prev, axis, down)  26.5 us
    all_to_all x1, blocking collectives, body(): got = lax.all_to_all(chunks, 'py', 0, 0)  10.1 us
    ppermute x2, waiting for transfers between devices, both_ways(): from_prev = lax.ppermute(to_next, axis, up)  7.54 us
    ppermute x2, starting transfers between devices, both_ways(): from_prev = lax.ppermute(to_next, axis, up)  3.84 us
    pallas_call x5, Pallas kernels, call(): pl.pallas_call(kernel, out_shape=[jax.ShapeDtypeStruct(s, jnp.float32) fo...  2.15 us
    unnamed x4, local copies, waits for them, and re-layouts  1.78 us
  transfers between devices with their start and end apart: 4, of which 3 were waited for; matrix products, arithmetic and copies ran while one was open for 0% of the time, Pallas kernels for 0%

profile of v2, /device:TPU:1, one launch (start us, length us, event | category | flops | bytes accessed | tf_op | source)
XLA Modules:
  0.0 80.6 jit_solution(12569232550871164400)
XLA Ops:
  0.0 0.0 copy-start
  0.0 0.9 %copy-done = f32[3,4,8,256]{3,2,1,0:T(8,128)S(1)} copy-done((f32[3,4,8,256]{3,2,1,0:T(8,128)S(1)}, f32[3,4,8,256]{3,2,1,0:T(8,128)}, u32[]{:S(2)}) %copy-start) | copy-done | bytes 98328
  0.9 0.0 copy-start.1
  0.9 0.9 %copy-done.1 = f32[3,4,8,256]{3,2,1,0:T(8,128)S(1)} copy-done((f32[3,4,8,256]{3,2,1,0:T(8,128)S(1)}, f32[3,4,8,256]{3,2,1,0:T(8,128)}, u32[]{:S(2)}) %copy-start.1) | copy-done | bytes 98328
  1.8 0.3 shard_map.28
  2.0 16.1 %collective-permute-start = (f32[3,4,8,256]{3,2,1,0:T(8,128)S(1)}, f32[3,4,8,256]{3,2,1,0:T(8,128)S(1)}, u32[]{:S(2)}, u32[]{:S(2)}) collective-permute-start(f32[3,4,8,256]{3,2,1,0:T(8,128)S(1)} %get-tuple-element.16), channel_id=1, source_target_pairs={{1,0},{2,1},{3,2},{4,3},{5,4},{6,5},{7,6},{8,7},{9,8},{10,9},{11,1... | collective-permute-start | bytes 294920 | tf_op jit(solution)/shard_map/ppermute | solution.py:321
  18.1 1.9 %collective-permute-start.1 = (f32[3,4,8,256]{3,2,1,0:T(8,128)S(1)}, f32[3,4,8,256]{3,2,1,0:T(8,128)S(1)}, u32[]{:S(2)}, u32[]{:S(2)}) collective-permute-start(f32[3,4,8,256]{3,2,1,0:T(8,128)S(1)} %get-tuple-element.17), channel_id=1, source_target_pairs={{0,1},{1,2},{2,3},{3,4},{4,5},{5,6},{6,7},{7,8},{8,9},{9,10},{10,1... | collective-permute-start | bytes 294920 | tf_op jit(solution)/shard_map/ppermute | solution.py:322
  20.0 0.0 collective-permute-done.zn_ref
  20.1 1.6 %collective-permute-done.1.zp_ref = f32[3,4,8,256]{3,2,1,0:T(8,128)S(1)} collective-permute-done((f32[3,4,8,256]{3,2,1,0:T(8,128)S(1)}, f32[3,4,8,256]{3,2,1,0:T(8,128)S(1)}, u32[]{:S(2)}, u32[]{:S(2)}) %collective-permute-start.1) | collective-permute-done | bytes 98336 | tf_op jit(solution)/shard_map/ppermute | solution.py:322
  21.7 0.1 shard_map.29
  21.8 10.5 %collective-permute-start.2 = (f32[20,8,256]{2,1,0:T(8,128)S(1)}, f32[20,8,256]{2,1,0:T(8,128)S(1)}, u32[]{:S(2)}, u32[]{:S(2)}) collective-permute-start(f32[20,8,256]{2,1,0:T(8,128)S(1)} %get-tuple-element.18), channel_id=1, source_target_pairs={{64,0},{128,64},{192,128},{256,192},{320,256},{384,320},{448,384},... | collective-permute-start | bytes 491528 | tf_op jit(solution)/shard_map/ppermute | solution.py:321
  32.3 1.9 %collective-permute-start.3 = (f32[20,8,256]{2,1,0:T(8,128)S(1)}, f32[20,8,256]{2,1,0:T(8,128)S(1)}, u32[]{:S(2)}, u32[]{:S(2)}) collective-permute-start(f32[20,8,256]{2,1,0:T(8,128)S(1)} %get-tuple-element.19), channel_id=1, source_target_pairs={{0,64},{64,128},{128,192},{192,256},{256,320},{320,384},{384,448},... | collective-permute-start | bytes 491528 | tf_op jit(solution)/shard_map/ppermute | solution.py:322
  34.2 0.3 collective-permute-done.2.yn_ref
  34.5 5.9 %collective-permute-done.3.yp_ref = f32[20,8,256]{2,1,0:T(8,128)S(1)} collective-permute-done((f32[20,8,256]{2,1,0:T(8,128)S(1)}, f32[20,8,256]{2,1,0:T(8,128)S(1)}, u32[]{:S(2)}, u32[]{:S(2)}) %collective-permute-start.3) | collective-permute-done | bytes 163872 | tf_op jit(solution)/shard_map/ppermute | solution.py:322
  40.4 0.4 shard_map.30
  40.8 10.1 %all_to_all.10.got_ref.far_ref = f32[16,8,384]{2,1,0:T(8,128)S(1)} all-to-all(f32[16,8,384]{2,1,0:T(8,128)S(1)} %get-tuple-element.20), channel_id=1, replica_groups=mesh['py'=16,'pz'=64] {'py'}, dimensions={0} | all-to-all | bytes 393216 | tf_op jit(solution)/shard_map/all_to_all | solution.py:345
  50.9 0.1 shard_map.31
  51.0 28.2 %all_to_all.11.sums_ref = f32[64,1,128]{2,1,0:T(1,128)S(1)} all-to-all(f32[64,1,128]{2,1,0:T(1,128)S(1)} %shard_map.31), channel_id=1, replica_groups=mesh['py'=16,'pz'=64] {'pz'}, dimensions={0} | all-to-all | bytes 65536 | tf_op jit(solution)/shard_map/all_to_all | solution.py:347
  79.3 1.4 %shard_map.32 = f32[3,4,8,256]{3,2,1,0:T(8,128)} custom-call(s32[1]{0:T(128)} %bitcast.place_ref, f32[3,4,8,256]{3,2,1,0:T(8,128)S(1)} %get-tuple-element.14.cot_ref, f32[3,4,8,256]{3,2,1,0:T(8,128)S(1)} %get-tuple-element.15.vel_ref, f32[3,4,8,256]{3,2,1,0:T(8,128)S(1)} %collective-permute-done.zn_ref, f32[3,4,8,256]{3,2,1,0:T(8,128)S(1)} %collective-permute-done.1.zp_ref, ...), custom_call_target="tpu_custom_call" | custom-call | tf_op jit(solution)/shard_map/pallas_call | solution.py:307
Async XLA Ops:
  0.0 0.9 %copy-start = (f32[3,4,8,256]{3,2,1,0:T(8,128)S(1)}, f32[3,4,8,256]{3,2,1,0:T(8,128)}, u32[]{:S(2)}) copy-start(f32[3,4,8,256]{3,2,1,0:T(8,128)} %cot_hbm.1) | copy-start | bytes 294916
  0.9 0.9 %copy-start.1 = (f32[3,4,8,256]{3,2,1,0:T(8,128)S(1)}, f32[3,4,8,256]{3,2,1,0:T(8,128)}, u32[]{:S(2)}) copy-start(f32[3,4,8,256]{3,2,1,0:T(8,128)} %vel_hbm.1) | copy-start | bytes 294916
  2.0 18.0 %collective-permute-start = (f32[3,4,8,256]{3,2,1,0:T(8,128)S(1)}, f32[3,4,8,256]{3,2,1,0:T(8,128)S(1)}, u32[]{:S(2)}, u32[]{:S(2)}) collective-permute-start(f32[3,4,8,256]{3,2,1,0:T(8,128)S(1)} %get-tuple-element.16), channel_id=1, source_target_pairs={{1,0},{2,1},{3,2},{4,3},{5,4},{6,5},{7,6},{8,7},{9,8},{10,9},{11,1... | collective-permute-start | bytes 294920 | tf_op jit(solution)/shard_map/ppermute | solution.py:321
  18.1 3.5 %collective-permute-start.1 = (f32[3,4,8,256]{3,2,1,0:T(8,128)S(1)}, f32[3,4,8,256]{3,2,1,0:T(8,128)S(1)}, u32[]{:S(2)}, u32[]{:S(2)}) collective-permute-start(f32[3,4,8,256]{3,2,1,0:T(8,128)S(1)} %get-tuple-element.17), channel_id=1, source_target_pairs={{0,1},{1,2},{2,3},{3,4},{4,5},{5,6},{6,7},{7,8},{8,9},{9,10},{10,1... | collective-permute-start | bytes 294920 | tf_op jit(solution)/shard_map/ppermute | solution.py:322
  21.8 12.7 %collective-permute-start.2 = (f32[20,8,256]{2,1,0:T(8,128)S(1)}, f32[20,8,256]{2,1,0:T(8,128)S(1)}, u32[]{:S(2)}, u32[]{:S(2)}) collective-permute-start(f32[20,8,256]{2,1,0:T(8,128)S(1)} %get-tuple-element.18), channel_id=1, source_target_pairs={{64,0},{128,64},{192,128},{256,192},{320,256},{384,320},{448,384},... | collective-permute-start | bytes 491528 | tf_op jit(solution)/shard_map/ppermute | solution.py:321
  32.3 8.2 %collective-permute-start.3 = (f32[20,8,256]{2,1,0:T(8,128)S(1)}, f32[20,8,256]{2,1,0:T(8,128)S(1)}, u32[]{:S(2)}, u32[]{:S(2)}) collective-permute-start(f32[20,8,256]{2,1,0:T(8,128)S(1)} %get-tuple-element.19), channel_id=1, source_target_pairs={{0,64},{64,128},{128,192},{192,256},{256,320},{320,384},{384,448},... | collective-permute-start | bytes 491528 | tf_op jit(solution)/shard_map/ppermute | solution.py:322

commit v3 on v2

--- a/solution.py
+++ b/solution.py
@@ -36,7 +36,7 @@
     return lax.broadcasted_iota(jnp.int32, (TILE, 256), 0)
 
 
-def pack_z(cot_hbm, vel_hbm, prev_ref, next_ref, cot_ref, vel_ref, sems):
+def pack_z(odd_ref, cot_hbm, vel_hbm, cross_ref, core_ref, cot_ref, vel_ref, sems):
     copies = [
         pltpu.make_async_copy(cot_hbm, cot_ref, sems.at[0]),
         pltpu.make_async_copy(vel_hbm, vel_ref, sems.at[1]),
@@ -46,11 +46,14 @@
     for copy in copies:
         copy.wait()
     row = sublane()
+    even = odd_ref[0] == 0
     for c in range(3):
         for y in range(ROWS):
             cot, vel = cot_ref[c, y], vel_ref[c, y]
-            prev_ref[c, y] = jnp.where(row < 5, cot, rolled(vel, 5, 0))
-            next_ref[c, y] = jnp.where(row >= 3, cot, rolled(vel, 3, 0))
+            to_prev = jnp.where(row < 5, cot, rolled(vel, 5, 0))
+            to_next = jnp.where(row >= 3, cot, rolled(vel, 3, 0))
+            cross_ref[c, y] = jnp.where(even, to_prev, to_next)
+            core_ref[c, y] = jnp.where(even, to_next, to_prev)
 
 
 def side_cot(row, zn, zp):
@@ -79,7 +82,13 @@
     return jnp.concatenate([a, b], axis=0)
 
 
-def pack_y(cot_ref, vel_ref, zn_ref, zp_ref, prev_ref, next_ref):
+def pack_y(odd_ref, cot_ref, vel_ref, cross_ref, core_ref, prev_ref, next_ref, zn_ref, zp_ref):
+    even = odd_ref[0] == 0
+    for c in range(3):
+        for y in range(ROWS):
+            cross, core = cross_ref[c, y], core_ref[c, y]
+            zn_ref[c, y] = jnp.where(even, core, cross)
+            zp_ref[c, y] = jnp.where(even, cross, core)
     refs = (cot_ref, vel_ref, zn_ref, zp_ref, None, None)
     row = sublane()
     cot = {(c, y): cot_frame(refs, row, c, y) for c in range(3) for y in range(ROWS)}
@@ -328,12 +337,16 @@
     place = lax.axis_index("py").astype(jnp.int32).reshape(1)
     block = (3, ROWS, TILE, 256)
     dmas = [pltpu.SemaphoreType.DMA((2,))]
-    to_prev, to_next, cotangent, velocity = call(
-        pack_z, [block] * 4, [], [cotangent, velocity], pl.ANY, dmas
+    odd = lax.rem(lax.axis_index("pz"), 2).astype(jnp.int32).reshape(1)
+    cross, core, cotangent, velocity = call(
+        pack_z, [block] * 4, [odd], [cotangent, velocity], pltpu.HBM, dmas
     )
-    zn, zp = both_ways(to_prev, to_next, "pz")
+    cross = lax.ppermute(cross, "pz", [(i, (i + 1 if i % 2 else i - 1) % nz) for i in range(nz)])
+    core = lax.ppermute(core, "pz", [(i, i ^ 1) for i in range(nz)])
     sent = (SENT, TILE, 256)
-    to_prev, to_next = call(pack_y, [sent, sent], [], [cotangent, velocity, zn, zp])
+    to_prev, to_next, zn, zp = call(
+        pack_y, [sent, sent, block, block], [odd], [cotangent, velocity, cross, core]
+    )
     yn, yp = both_ways(to_prev, to_next, "py")
     held = [cotangent, velocity, zn, zp, yn, yp]
     chunks, b, w = call(

time: 81 us -> 75.6 us (0.933)
  blocking collectives: 38.4 us -> 32 us
    ppermute x0 -> x2, starting transfers between devices: none -> 18 us  [the longest x1 13.5 us: body(): core = lax.ppermute(core, 'pz', [(i, i ^ 1) for i in range(nz)])]
    ppermute x2 -> x1, starting transfers between devices: 26.5 us -> 11.3 us  [both_ways(): from_next = lax.ppermute(to_prev, axis, down)]
    all_to_all x1, blocking collectives: 28.2 us -> 21.7 us  [body(): sums = lax.all_to_all(lines, 'pz', 0, 0)]
    ppermute x2 -> x1, starting transfers between devices: 3.84 us -> 1.92 us  [both_ways(): from_prev = lax.ppermute(to_next, axis, up)]
    ppermute x2 -> x1, waiting for transfers between devices: 7.54 us -> 5.9 us  [both_ways(): from_prev = lax.ppermute(to_next, axis, up)]
    ppermute x2 -> x1, waiting for transfers between devices: 0.31 us -> 1.27 us  [both_ways(): from_next = lax.ppermute(to_prev, axis, down)]
    ppermute x0 -> x2, waiting for transfers between devices: none -> 0.91 us  [the longest x1 0.91 us: body(): core = lax.ppermute(core, 'pz', [(i, i ^ 1) for i in range(nz)])]
where the time goes in v3:
time: 75.6 us; the launch traced here: 75.3 us
  blocking collectives  32 us (42%)
  starting transfers between devices  31.2 us (41%)
  waiting for transfers between devices  8.09 us (11%)
  Pallas kernels  2.16 us (3%)
  local copies, waits for them, and re-layouts  1.78 us (2%)
    all_to_all x1, blocking collectives, body(): sums = lax.all_to_all(lines, 'pz', 0, 0)  21.7 us
    ppermute x1, starting transfers between devices, body(): core = lax.ppermute(core, 'pz', [(i, i ^ 1) for i in range(nz)])  13.5 us
    ppermute x1, starting transfers between devices, both_ways(): from_next = lax.ppermute(to_prev, axis, down)  11.3 us
    all_to_all x1, blocking collectives, body(): got = lax.all_to_all(chunks, 'py', 0, 0)  10.3 us
    ppermute x1, waiting for transfers between devices, both_ways(): from_prev = lax.ppermute(to_next, axis, up)  5.9 us
    ppermute x1, starting transfers between devices, body(): lax.ppermute(cross, 'pz', [(i, (i + 1 if i % 2 else i - 1) % nz) for i in...  4.51 us
    pallas_call x5, Pallas kernels, call(): pl.pallas_call(kernel, out_shape=[jax.ShapeDtypeStruct(s, jnp.float32) fo...  2.16 us
    ppermute x1, starting transfers between devices, both_ways(): from_prev = lax.ppermute(to_next, axis, up)  1.92 us
  transfers between devices with their start and end apart: 4, of which 3 were waited for; matrix products, arithmetic and copies ran while one was open for 0% of the time, Pallas kernels for 0%

profile of v3, /device:TPU:1, one launch (start us, length us, event | category | flops | bytes accessed | tf_op | source)
XLA Modules:
  0.0 75.3 jit_solution(11998459000331047363)
XLA Ops:
  0.0 0.0 copy-start
  0.0 0.9 %copy-done = f32[3,4,8,256]{3,2,1,0:T(8,128)S(1)} copy-done((f32[3,4,8,256]{3,2,1,0:T(8,128)S(1)}, f32[3,4,8,256]{3,2,1,0:T(8,128)}, u32[]{:S(2)}) %copy-start) | copy-done | bytes 98328
  0.9 0.0 copy-start.1
  0.9 0.9 %copy-done.1 = f32[3,4,8,256]{3,2,1,0:T(8,128)S(1)} copy-done((f32[3,4,8,256]{3,2,1,0:T(8,128)S(1)}, f32[3,4,8,256]{3,2,1,0:T(8,128)}, u32[]{:S(2)}) %copy-start.1) | copy-done | bytes 98328
  1.8 0.3 shard_map.28
  2.1 4.5 %collective-permute-start = (f32[3,4,8,256]{3,2,1,0:T(8,128)S(1)}, f32[3,4,8,256]{3,2,1,0:T(8,128)S(1)}, u32[]{:S(2)}, u32[]{:S(2)}) collective-permute-start(f32[3,4,8,256]{3,2,1,0:T(8,128)S(1)} %get-tuple-element.18), channel_id=1, source_target_pairs={{0,63},{1,2},{2,1},{3,4},{4,3},{5,6},{6,5},{7,8},{8,7},{9,10},{10,... | collective-permute-start | bytes 294920 | tf_op jit(solution)/shard_map/ppermute | solution.py:344
  6.6 13.5 %collective-permute-start.1 = (f32[3,4,8,256]{3,2,1,0:T(8,128)S(1)}, f32[3,4,8,256]{3,2,1,0:T(8,128)S(1)}, u32[]{:S(2)}, u32[]{:S(2)}) collective-permute-start(f32[3,4,8,256]{3,2,1,0:T(8,128)S(1)} %get-tuple-element.19), channel_id=1, source_target_pairs={{0,1},{1,0},{2,3},{3,2},{4,5},{5,4},{6,7},{7,6},{8,9},{9,8},{10,11... | collective-permute-start | bytes 294920 | tf_op jit(solution)/shard_map/ppermute | solution.py:345
  20.1 0.0 collective-permute-done.cross_ref
  20.1 0.9 %collective-permute-done.1.core_ref = f32[3,4,8,256]{3,2,1,0:T(8,128)S(1)} collective-permute-done((f32[3,4,8,256]{3,2,1,0:T(8,128)S(1)}, f32[3,4,8,256]{3,2,1,0:T(8,128)S(1)}, u32[]{:S(2)}, u32[]{:S(2)}) %collective-permute-start.1) | collective-permute-done | bytes 98336 | tf_op jit(solution)/shard_map/ppermute | solution.py:345
  21.0 0.1 shard_map.29
  21.1 11.3 %collective-permute-start.2 = (f32[20,8,256]{2,1,0:T(8,128)S(1)}, f32[20,8,256]{2,1,0:T(8,128)S(1)}, u32[]{:S(2)}, u32[]{:S(2)}) collective-permute-start(f32[20,8,256]{2,1,0:T(8,128)S(1)} %get-tuple-element.22), channel_id=1, source_target_pairs={{64,0},{128,64},{192,128},{256,192},{320,256},{384,320},{448,384},... | collective-permute-start | bytes 491528 | tf_op jit(solution)/shard_map/ppermute | solution.py:330
  32.4 1.9 %collective-permute-start.3 = (f32[20,8,256]{2,1,0:T(8,128)S(1)}, f32[20,8,256]{2,1,0:T(8,128)S(1)}, u32[]{:S(2)}, u32[]{:S(2)}) collective-permute-start(f32[20,8,256]{2,1,0:T(8,128)S(1)} %get-tuple-element.23), channel_id=1, source_target_pairs={{0,64},{64,128},{128,192},{192,256},{256,320},{320,384},{384,448},... | collective-permute-start | bytes 491528 | tf_op jit(solution)/shard_map/ppermute | solution.py:331
  34.3 1.3 %collective-permute-done.2.yn_ref = f32[20,8,256]{2,1,0:T(8,128)S(1)} collective-permute-done((f32[20,8,256]{2,1,0:T(8,128)S(1)}, f32[20,8,256]{2,1,0:T(8,128)S(1)}, u32[]{:S(2)}, u32[]{:S(2)}) %collective-permute-start.2) | collective-permute-done | bytes 163872 | tf_op jit(solution)/shard_map/ppermute | solution.py:330
  35.6 5.9 %collective-permute-done.3.yp_ref = f32[20,8,256]{2,1,0:T(8,128)S(1)} collective-permute-done((f32[20,8,256]{2,1,0:T(8,128)S(1)}, f32[20,8,256]{2,1,0:T(8,128)S(1)}, u32[]{:S(2)}, u32[]{:S(2)}) %collective-permute-start.3) | collective-permute-done | bytes 163872 | tf_op jit(solution)/shard_map/ppermute | solution.py:331
  41.5 0.4 shard_map.30
  41.9 10.3 %all_to_all.10.got_ref.far_ref = f32[16,8,384]{2,1,0:T(8,128)S(1)} all-to-all(f32[16,8,384]{2,1,0:T(8,128)S(1)} %get-tuple-element.24), channel_id=1, replica_groups=mesh['py'=16,'pz'=64] {'py'}, dimensions={0} | all-to-all | bytes 393216 | tf_op jit(solution)/shard_map/all_to_all | solution.py:358
  52.1 0.1 shard_map.31
  52.2 21.7 %all_to_all.11.sums_ref = f32[64,1,128]{2,1,0:T(1,128)S(1)} all-to-all(f32[64,1,128]{2,1,0:T(1,128)S(1)} %shard_map.31), channel_id=1, replica_groups=mesh['py'=16,'pz'=64] {'pz'}, dimensions={0} | all-to-all | bytes 65536 | tf_op jit(solution)/shard_map/all_to_all | solution.py:360
  73.9 1.4 %shard_map.32 = f32[3,4,8,256]{3,2,1,0:T(8,128)} custom-call(s32[1]{0:T(128)} %bitcast.place_ref, f32[3,4,8,256]{3,2,1,0:T(8,128)S(1)} %get-tuple-element.16.cot_ref, f32[3,4,8,256]{3,2,1,0:T(8,128)S(1)} %get-tuple-element.17.vel_ref, f32[3,4,8,256]{3,2,1,0:T(8,128)S(1)} %get-tuple-element.20.zn_ref, f32[3,4,8,256]{3,2,1,0:T(8,128)S(1)} %get-tuple-element.21.zp_ref, ...), custom_call_target="tpu_custom_call" | custom-call | tf_op jit(solution)/shard_map/pallas_call | solution.py:316
Async XLA Ops:
  0.0 0.9 %copy-start = (f32[3,4,8,256]{3,2,1,0:T(8,128)S(1)}, f32[3,4,8,256]{3,2,1,0:T(8,128)}, u32[]{:S(2)}) copy-start(f32[3,4,8,256]{3,2,1,0:T(8,128)} %cot_hbm.1) | copy-start | bytes 294916
  0.9 0.9 %copy-start.1 = (f32[3,4,8,256]{3,2,1,0:T(8,128)S(1)}, f32[3,4,8,256]{3,2,1,0:T(8,128)}, u32[]{:S(2)}) copy-start(f32[3,4,8,256]{3,2,1,0:T(8,128)} %vel_hbm.1) | copy-start | bytes 294916
  2.1 18.0 %collective-permute-start = (f32[3,4,8,256]{3,2,1,0:T(8,128)S(1)}, f32[3,4,8,256]{3,2,1,0:T(8,128)S(1)}, u32[]{:S(2)}, u32[]{:S(2)}) collective-permute-start(f32[3,4,8,256]{3,2,1,0:T(8,128)S(1)} %get-tuple-element.18), channel_id=1, source_target_pairs={{0,63},{1,2},{2,1},{3,4},{4,3},{5,6},{6,5},{7,8},{8,7},{9,10},{10,... | collective-permute-start | bytes 294920 | tf_op jit(solution)/shard_map/ppermute | solution.py:344
  6.6 14.4 %collective-permute-start.1 = (f32[3,4,8,256]{3,2,1,0:T(8,128)S(1)}, f32[3,4,8,256]{3,2,1,0:T(8,128)S(1)}, u32[]{:S(2)}, u32[]{:S(2)}) collective-permute-start(f32[3,4,8,256]{3,2,1,0:T(8,128)S(1)} %get-tuple-element.19), channel_id=1, source_target_pairs={{0,1},{1,0},{2,3},{3,2},{4,5},{5,4},{6,7},{7,6},{8,9},{9,8},{10,11... | collective-permute-start | bytes 294920 | tf_op jit(solution)/shard_map/ppermute | solution.py:345
  21.1 14.5 %collective-permute-start.2 = (f32[20,8,256]{2,1,0:T(8,128)S(1)}, f32[20,8,256]{2,1,0:T(8,128)S(1)}, u32[]{:S(2)}, u32[]{:S(2)}) collective-permute-start(f32[20,8,256]{2,1,0:T(8,128)S(1)} %get-tuple-element.22), channel_id=1, source_target_pairs={{64,0},{128,64},{192,128},{256,192},{320,256},{384,320},{448,384},... | collective-permute-start | bytes 491528 | tf_op jit(solution)/shard_map/ppermute | solution.py:330
  32.4 9.1 %collective-permute-start.3 = (f32[20,8,256]{2,1,0:T(8,128)S(1)}, f32[20,8,256]{2,1,0:T(8,128)S(1)}, u32[]{:S(2)}, u32[]{:S(2)}) collective-permute-start(f32[20,8,256]{2,1,0:T(8,128)S(1)} %get-tuple-element.23), channel_id=1, source_target_pairs={{0,64},{64,128},{128,192},{192,256},{256,320},{320,384},{384,448},... | collective-permute-start | bytes 491528 | tf_op jit(solution)/shard_map/ppermute | solution.py:331

commit v4 on v3

--- a/solution.py
+++ b/solution.py
@@ -82,7 +82,7 @@
     return jnp.concatenate([a, b], axis=0)
 
 
-def pack_y(odd_ref, cot_ref, vel_ref, cross_ref, core_ref, prev_ref, next_ref, zn_ref, zp_ref):
+def pack_y(odd_ref, place_ref, cot_ref, vel_ref, cross_ref, core_ref, first_ref, second_ref, zn_ref, zp_ref):
     even = odd_ref[0] == 0
     for c in range(3):
         for y in range(ROWS):
@@ -97,9 +97,10 @@
     high = flat[3] + 0.5 * cot[1, 2]
     one = flat[1] - 0.5 * (cot[1, 2] - cot[1, 0])
     two = flat[2] - 0.5 * (cot[1, 3] - cot[1, 1])
+    to_prev, to_next = {}, {}
     for out, part, (d1, d2) in (
-        (prev_ref, (low, one, two, high), (0, 1)),
-        (next_ref, (high, two, one, low), (3, 2)),
+        (to_prev, (low, one, two, high), (0, 1)),
+        (to_next, (high, two, one, low), (3, 2)),
     ):
         for d in range(4):
             out[d] = part[d][:TILE]
@@ -113,6 +114,10 @@
         out[17] = mixed(row, part[1][TILE:], [(2, cot[0, d1][TILE:]), (3, cot[2, d1][TILE:])])
         out[18] = mixed(row, vel[0], [(1, vel[1]), (2, vel[2])])
         out[19] = cot[1, d1][TILE:]
+    level = lax.rem(place_ref[0], 2) == 0
+    for k in range(SENT):
+        first_ref[k] = jnp.where(level, to_prev[k], to_next[k])
+        second_ref[k] = jnp.where(level, to_next[k], to_prev[k])
 
 
 def cot_frame(refs, row, c, y):
@@ -174,7 +179,14 @@
     return jnp.sum(jnp.sum(x, axis=0, keepdims=True), axis=1, keepdims=True)
 
 
-def moments(peers, place_ref, cot_ref, vel_ref, zn_ref, zp_ref, yn_ref, yp_ref, out_ref, b_ref, w_ref):
+def moments(
+    peers, place_ref, cot_ref, vel_ref, zn_ref, zp_ref, first_ref, second_ref, out_ref, b_ref, w_ref, yn_ref, yp_ref
+):
+    level = lax.rem(place_ref[0], 2) == 0
+    for k in range(SENT):
+        first, second = first_ref[k], second_ref[k]
+        yn_ref[k] = jnp.where(level, second, first)
+        yp_ref[k] = jnp.where(level, first, second)
     refs = (cot_ref, vel_ref, zn_ref, zp_ref, yn_ref, yp_ref)
     row = sublane()
     cot_y = {y: cot_frame(refs, row, 1, y) for y in range(-1, 5)}
@@ -323,13 +335,13 @@
     )(*scalars, *arrays)
 
 
-def both_ways(to_prev, to_next, axis):
+def swap_across(x, axis):
     n = lax.axis_size(axis)
-    up = [(i, (i + 1) % n) for i in range(n)]
-    down = [(j, i) for i, j in up]
-    from_next = lax.ppermute(to_prev, axis, down)
-    from_prev = lax.ppermute(to_next, axis, up)
-    return from_next, from_prev
+    return lax.ppermute(x, axis, [(i, (i + 1 if i % 2 else i - 1) % n) for i in range(n)])
+
+
+def swap_within(x, axis):
+    return lax.ppermute(x, axis, [(i, i ^ 1) for i in range(lax.axis_size(axis))])
 
 
 def body(velocity, cotangent):
@@ -341,20 +353,21 @@
     cross, core, cotangent, velocity = call(
         pack_z, [block] * 4, [odd], [cotangent, velocity], pltpu.HBM, dmas
     )
-    cross = lax.ppermute(cross, "pz", [(i, (i + 1 if i % 2 else i - 1) % nz) for i in range(nz)])
-    core = lax.ppermute(core, "pz", [(i, i ^ 1) for i in range(nz)])
+    cross = swap_across(cross, "pz")
+    core = swap_within(core, "pz")
     sent = (SENT, TILE, 256)
-    to_prev, to_next, zn, zp = call(
-        pack_y, [sent, sent, block, block], [odd], [cotangent, velocity, cross, core]
+    first, second, zn, zp = call(
+        pack_y, [sent, sent, block, block], [odd, place], [cotangent, velocity, cross, core]
     )
-    yn, yp = both_ways(to_prev, to_next, "py")
+    first = swap_across(first, "py")
+    second = swap_within(second, "py")
+    chunks, b, w, yn, yp = call(
+        functools.partial(moments, ny),
+        [(ny, TILE, 384), (10, WIDE, 256), (8, WIDE, 256), sent, sent],
+        [place],
+        [cotangent, velocity, zn, zp, first, second],
+    )
     held = [cotangent, velocity, zn, zp, yn, yp]
-    chunks, b, w = call(
-        functools.partial(moments, ny),
-        [(ny, TILE, 384), (10, WIDE, 256), (8, WIDE, 256)],
-        [place],
-        held,
-    )
     got = lax.all_to_all(chunks, "py", 0, 0)
     (lines,) = call(merge, [(nz, 1, 128)], [], [got])
     sums = lax.all_to_all(lines, "pz", 0, 0)

time: 75.6 us -> 73.6 us (0.974)
  waiting for transfers between devices: 8.09 us -> 5.98 us
    ppermute x4, waiting for transfers between devices: 8.09 us -> 5.98 us  [the longest x2 3.63 us: swap_within(): lax.ppermute(x, axis, [(i, i ^ 1) for i in range(lax.axis_size(axis))])]
where the time goes in v4:
time: 73.6 us; the launch traced here: 73.2 us
  blocking collectives  32 us (43%)
  starting transfers between devices  31.2 us (42%)
  waiting for transfers between devices  5.98 us (8%)
  Pallas kernels  2.17 us (3%)
  local copies, waits for them, and re-layouts  1.78 us (2%)
    all_to_all x1, blocking collectives, body(): sums = lax.all_to_all(lines, 'pz', 0, 0)  21.7 us
    ppermute x2, starting transfers between devices, swap_across(): lax.ppermute(x, axis, [(i, (i + 1 if i % 2 else i - 1) % n) for i in rang...  15.8 us
    ppermute x2, starting transfers between devices, swap_within(): lax.ppermute(x, axis, [(i, i ^ 1) for i in range(lax.axis_size(axis))])  15.4 us
    all_to_all x1, blocking collectives, body(): got = lax.all_to_all(chunks, 'py', 0, 0)  10.3 us
    ppermute x2, waiting for transfers between devices, swap_within(): lax.ppermute(x, axis, [(i, i ^ 1) for i in range(lax.axis_size(axis))])  3.63 us
    ppermute x2, waiting for transfers between devices, swap_across(): lax.ppermute(x, axis, [(i, (i + 1 if i % 2 else i - 1) % n) for i in rang...  2.35 us
    pallas_call x5, Pallas kernels, call(): pl.pallas_call(kernel, out_shape=[jax.ShapeDtypeStruct(s, jnp.float32) fo...  2.17 us
    unnamed x4, local copies, waits for them, and re-layouts  1.78 us
  transfers between devices with their start and end apart: 4, of which 3 were waited for; matrix products, arithmetic and copies ran while one was open for 0% of the time, Pallas kernels for 0%

profile of v4, /device:TPU:1, one launch (start us, length us, event | category | flops | bytes accessed | tf_op | source)
XLA Modules:
  0.0 73.2 jit_solution(6179289457332322513)
XLA Ops:
  0.0 0.0 copy-start
  0.0 0.9 %copy-done = f32[3,4,8,256]{3,2,1,0:T(8,128)S(1)} copy-done((f32[3,4,8,256]{3,2,1,0:T(8,128)S(1)}, f32[3,4,8,256]{3,2,1,0:T(8,128)}, u32[]{:S(2)}) %copy-start) | copy-done | bytes 98328
  0.9 0.0 copy-start.1
  0.9 0.9 %copy-done.1 = f32[3,4,8,256]{3,2,1,0:T(8,128)S(1)} copy-done((f32[3,4,8,256]{3,2,1,0:T(8,128)S(1)}, f32[3,4,8,256]{3,2,1,0:T(8,128)}, u32[]{:S(2)}) %copy-start.1) | copy-done | bytes 98328
  1.8 0.3 shard_map.28
  2.1 4.5 %collective-permute-start = (f32[3,4,8,256]{3,2,1,0:T(8,128)S(1)}, f32[3,4,8,256]{3,2,1,0:T(8,128)S(1)}, u32[]{:S(2)}, u32[]{:S(2)}) collective-permute-start(f32[3,4,8,256]{3,2,1,0:T(8,128)S(1)} %get-tuple-element.20), channel_id=1, source_target_pairs={{0,63},{1,2},{2,1},{3,4},{4,3},{5,6},{6,5},{7,8},{8,7},{9,10},{10,... | collective-permute-start | bytes 294920 | tf_op jit(solution)/shard_map/ppermute | solution.py:340
  6.6 13.5 %collective-permute-start.1 = (f32[3,4,8,256]{3,2,1,0:T(8,128)S(1)}, f32[3,4,8,256]{3,2,1,0:T(8,128)S(1)}, u32[]{:S(2)}, u32[]{:S(2)}) collective-permute-start(f32[3,4,8,256]{3,2,1,0:T(8,128)S(1)} %get-tuple-element.21), channel_id=1, source_target_pairs={{0,1},{1,0},{2,3},{3,2},{4,5},{5,4},{6,7},{7,6},{8,9},{9,8},{10,11... | collective-permute-start | bytes 294920 | tf_op jit(solution)/shard_map/ppermute | solution.py:344
  20.1 0.0 collective-permute-done.cross_ref
  20.1 0.9 %collective-permute-done.1.core_ref = f32[3,4,8,256]{3,2,1,0:T(8,128)S(1)} collective-permute-done((f32[3,4,8,256]{3,2,1,0:T(8,128)S(1)}, f32[3,4,8,256]{3,2,1,0:T(8,128)S(1)}, u32[]{:S(2)}, u32[]{:S(2)}) %collective-permute-start.1) | collective-permute-done | bytes 98336 | tf_op jit(solution)/shard_map/ppermute | solution.py:344
  21.0 0.1 shard_map.29
  21.1 11.3 %collective-permute-start.2 = (f32[20,8,256]{2,1,0:T(8,128)S(1)}, f32[20,8,256]{2,1,0:T(8,128)S(1)}, u32[]{:S(2)}, u32[]{:S(2)}) collective-permute-start(f32[20,8,256]{2,1,0:T(8,128)S(1)} %get-tuple-element.24), channel_id=1, source_target_pairs={{0,960},{64,128},{128,64},{192,256},{256,192},{320,384},{384,320},... | collective-permute-start | bytes 491528 | tf_op jit(solution)/shard_map/ppermute | solution.py:340
  32.4 1.9 %collective-permute-start.3 = (f32[20,8,256]{2,1,0:T(8,128)S(1)}, f32[20,8,256]{2,1,0:T(8,128)S(1)}, u32[]{:S(2)}, u32[]{:S(2)}) collective-permute-start(f32[20,8,256]{2,1,0:T(8,128)S(1)} %get-tuple-element.25), channel_id=1, source_target_pairs={{0,64},{64,0},{128,192},{192,128},{256,320},{320,256},{384,448},{4... | collective-permute-start | bytes 491528 | tf_op jit(solution)/shard_map/ppermute | solution.py:344
  34.3 2.3 %collective-permute-done.2.first_ref = f32[20,8,256]{2,1,0:T(8,128)S(1)} collective-permute-done((f32[20,8,256]{2,1,0:T(8,128)S(1)}, f32[20,8,256]{2,1,0:T(8,128)S(1)}, u32[]{:S(2)}, u32[]{:S(2)}) %collective-permute-start.2) | collective-permute-done | bytes 163872 | tf_op jit(solution)/shard_map/ppermute | solution.py:340
  36.7 2.7 %collective-permute-done.3.second_ref = f32[20,8,256]{2,1,0:T(8,128)S(1)} collective-permute-done((f32[20,8,256]{2,1,0:T(8,128)S(1)}, f32[20,8,256]{2,1,0:T(8,128)S(1)}, u32[]{:S(2)}, u32[]{:S(2)}) %collective-permute-start.3) | collective-permute-done | bytes 163872 | tf_op jit(solution)/shard_map/ppermute | solution.py:344
  39.4 0.4 shard_map.30
  39.8 10.3 %all_to_all.10.got_ref.far_ref = f32[16,8,384]{2,1,0:T(8,128)S(1)} all-to-all(f32[16,8,384]{2,1,0:T(8,128)S(1)} %get-tuple-element.28), channel_id=1, replica_groups=mesh['py'=16,'pz'=64] {'py'}, dimensions={0} | all-to-all | bytes 393216 | tf_op jit(solution)/shard_map/all_to_all | solution.py:371
  50.0 0.1 shard_map.31
  50.1 21.7 %all_to_all.11.sums_ref = f32[64,1,128]{2,1,0:T(1,128)S(1)} all-to-all(f32[64,1,128]{2,1,0:T(1,128)S(1)} %shard_map.31), channel_id=1, replica_groups=mesh['py'=16,'pz'=64] {'pz'}, dimensions={0} | all-to-all | bytes 65536 | tf_op jit(solution)/shard_map/all_to_all | solution.py:373
  71.8 1.4 %shard_map.32 = f32[3,4,8,256]{3,2,1,0:T(8,128)} custom-call(s32[1]{0:T(128)} %bitcast.place_ref, f32[3,4,8,256]{3,2,1,0:T(8,128)S(1)} %get-tuple-element.18.cot_ref, f32[3,4,8,256]{3,2,1,0:T(8,128)S(1)} %get-tuple-element.19.vel_ref, f32[3,4,8,256]{3,2,1,0:T(8,128)S(1)} %get-tuple-element.22.zn_ref, f32[3,4,8,256]{3,2,1,0:T(8,128)S(1)} %get-tuple-element.23.zp_ref, ...), custom_call_target="tpu_custom_call" | custom-call | tf_op jit(solution)/shard_map/pallas_call | solution.py:328
Async XLA Ops:
  0.0 0.9 %copy-start = (f32[3,4,8,256]{3,2,1,0:T(8,128)S(1)}, f32[3,4,8,256]{3,2,1,0:T(8,128)}, u32[]{:S(2)}) copy-start(f32[3,4,8,256]{3,2,1,0:T(8,128)} %cot_hbm.1) | copy-start | bytes 294916
  0.9 0.9 %copy-start.1 = (f32[3,4,8,256]{3,2,1,0:T(8,128)S(1)}, f32[3,4,8,256]{3,2,1,0:T(8,128)}, u32[]{:S(2)}) copy-start(f32[3,4,8,256]{3,2,1,0:T(8,128)} %vel_hbm.1) | copy-start | bytes 294916
  2.1 18.0 %collective-permute-start = (f32[3,4,8,256]{3,2,1,0:T(8,128)S(1)}, f32[3,4,8,256]{3,2,1,0:T(8,128)S(1)}, u32[]{:S(2)}, u32[]{:S(2)}) collective-permute-start(f32[3,4,8,256]{3,2,1,0:T(8,128)S(1)} %get-tuple-element.20), channel_id=1, source_target_pairs={{0,63},{1,2},{2,1},{3,4},{4,3},{5,6},{6,5},{7,8},{8,7},{9,10},{10,... | collective-permute-start | bytes 294920 | tf_op jit(solution)/shard_map/ppermute | solution.py:340
  6.6 14.4 %collective-permute-start.1 = (f32[3,4,8,256]{3,2,1,0:T(8,128)S(1)}, f32[3,4,8,256]{3,2,1,0:T(8,128)S(1)}, u32[]{:S(2)}, u32[]{:S(2)}) collective-permute-start(f32[3,4,8,256]{3,2,1,0:T(8,128)S(1)} %get-tuple-element.21), channel_id=1, source_target_pairs={{0,1},{1,0},{2,3},{3,2},{4,5},{5,4},{6,7},{7,6},{8,9},{9,8},{10,11... | collective-permute-start | bytes 294920 | tf_op jit(solution)/shard_map/ppermute | solution.py:344
  21.1 15.6 %collective-permute-start.2 = (f32[20,8,256]{2,1,0:T(8,128)S(1)}, f32[20,8,256]{2,1,0:T(8,128)S(1)}, u32[]{:S(2)}, u32[]{:S(2)}) collective-permute-start(f32[20,8,256]{2,1,0:T(8,128)S(1)} %get-tuple-element.24), channel_id=1, source_target_pairs={{0,960},{64,128},{128,64},{192,256},{256,192},{320,384},{384,320},... | collective-permute-start | bytes 491528 | tf_op jit(solution)/shard_map/ppermute | solution.py:340
  32.4 7.0 %collective-permute-start.3 = (f32[20,8,256]{2,1,0:T(8,128)S(1)}, f32[20,8,256]{2,1,0:T(8,128)S(1)}, u32[]{:S(2)}, u32[]{:S(2)}) collective-permute-start(f32[20,8,256]{2,1,0:T(8,128)S(1)} %get-tuple-element.25), channel_id=1, source_target_pairs={{0,64},{64,0},{128,192},{192,128},{256,320},{320,256},{384,448},{4... | collective-permute-start | bytes 491528 | tf_op jit(solution)/shard_map/ppermute | solution.py:344

commit v5 on v4

--- a/solution.py
+++ b/solution.py
@@ -1,4 +1,4 @@
-import functools
+import math
 
 import jax
 import jax.numpy as jnp
@@ -36,20 +36,13 @@
     return lax.broadcasted_iota(jnp.int32, (TILE, 256), 0)
 
 
-def pack_z(odd_ref, cot_hbm, vel_hbm, cross_ref, core_ref, cot_ref, vel_ref, sems):
-    copies = [
-        pltpu.make_async_copy(cot_hbm, cot_ref, sems.at[0]),
-        pltpu.make_async_copy(vel_hbm, vel_ref, sems.at[1]),
-    ]
-    for copy in copies:
-        copy.start()
-    for copy in copies:
-        copy.wait()
+def pack_z(odd_ref, both_ref, cross_ref, core_ref, cot_ref, vel_ref):
     row = sublane()
     even = odd_ref[0] == 0
     for c in range(3):
         for y in range(ROWS):
-            cot, vel = cot_ref[c, y], vel_ref[c, y]
+            cot, vel = both_ref[c, y], both_ref[3 + c, y]
+            cot_ref[c, y], vel_ref[c, y] = cot, vel
             to_prev = jnp.where(row < 5, cot, rolled(vel, 5, 0))
             to_next = jnp.where(row >= 3, cot, rolled(vel, 3, 0))
             cross_ref[c, y] = jnp.where(even, to_prev, to_next)
@@ -82,7 +75,7 @@
     return jnp.concatenate([a, b], axis=0)
 
 
-def pack_y(odd_ref, place_ref, cot_ref, vel_ref, cross_ref, core_ref, first_ref, second_ref, zn_ref, zp_ref):
+def pack_y(odd_ref, place_ref, cot_ref, vel_ref, cross_ref, core_ref, first_ref, second_ref, zn_ref, zp_ref, far1_ref, far2_ref):
     even = odd_ref[0] == 0
     for c in range(3):
         for y in range(ROWS):
@@ -118,6 +111,9 @@
     for k in range(SENT):
         first_ref[k] = jnp.where(level, to_prev[k], to_next[k])
         second_ref[k] = jnp.where(level, to_next[k], to_prev[k])
+    lower = lax.rem(place_ref[0], 4) < 2
+    far1_ref[...] = jnp.where(lower, cot_ref[1, 0], cot_ref[1, ROWS - 1])
+    far2_ref[...] = jnp.where(lower, cot_ref[1, ROWS - 1], cot_ref[1, 0])
 
 
 def cot_frame(refs, row, c, y):
@@ -180,7 +176,7 @@
 
 
 def moments(
-    peers, place_ref, cot_ref, vel_ref, zn_ref, zp_ref, first_ref, second_ref, out_ref, b_ref, w_ref, yn_ref, yp_ref
+    place_ref, cot_ref, vel_ref, zn_ref, zp_ref, first_ref, second_ref, out_ref, b_ref, w_ref, yn_ref, yp_ref
 ):
     level = lax.rem(place_ref[0], 2) == 0
     for k in range(SENT):
@@ -219,16 +215,21 @@
         third = v * u if third is None else third + v * u
         cross = bc * u if cross is None else cross + bc * u
     spread, third, cross = total(spread), total(third), total(cross)
-    line = lax.broadcasted_iota(jnp.int32, (TILE, 128), 0)
-    tile = jnp.zeros((TILE, 128), jnp.float32)
-    for k, value in enumerate((m0, m1, spread, third, cross)):
-        tile = jnp.where(line == k, value, tile)
-    place = place_ref[0]
-    for j in range(peers):
-        ahead = lax.rem(j - place + peers, peers)
-        up = jnp.where(ahead < peers // 2, 1.0, 0.0)
-        out_ref[j, :, :256] = jnp.where(up > 0.5, cot_ref[1, ROWS - 1], cot_ref[1, 0])
-        out_ref[j, :, 256:] = tile
+    spread_out((m0, m1, spread, third, cross), out_ref)
+
+
+def spread_out(parts, out_ref):
+    lane = lax.broadcasted_iota(jnp.int32, (1, 128), 1)
+    line = jnp.zeros((1, 128), jnp.float32)
+    for k, value in enumerate(parts):
+        line = jnp.where(lane == k, value, line)
+    for j in range(out_ref.shape[0]):
+        out_ref[j] = line
+
+
+def gathered(got_ref):
+    lines = got_ref[...].reshape(got_ref.shape[0], 128)
+    return [x[:, :1] for x in merged(*[rolled(lines, -k, 1) for k in range(5)])]
 
 
 def merged(m0, m1, spread, third, cross):
@@ -246,20 +247,15 @@
 
 
 def merge(got_ref, out_ref):
-    parts = merged(*[got_ref[:, k, 256:] for k in range(5)])
-    lane = lax.broadcasted_iota(jnp.int32, (1, 128), 1)
-    line = jnp.zeros((1, 128), jnp.float32)
-    for k, value in enumerate(parts):
-        line = jnp.where(lane == k, value, line)
-    for j in range(out_ref.shape[0]):
-        out_ref[j] = line
-
-
-def finish(peers, place_ref, cot_ref, vel_ref, zn_ref, zp_ref, yn_ref, yp_ref, far_ref, b_ref, w_ref, sums_ref, out_ref):
+    spread_out(gathered(got_ref), out_ref)
+
+
+def finish(
+    place_ref, cot_ref, vel_ref, zn_ref, zp_ref, yn_ref, yp_ref, far1_ref, far2_ref, b_ref, w_ref, sums_ref, out_ref
+):
     refs = (cot_ref, vel_ref, zn_ref, zp_ref, yn_ref, yp_ref)
     row = sublane()
-    sums = sums_ref[...].reshape(sums_ref.shape[0], 128)
-    m0, m1, spread, third, _ = [x[:, :1] for x in merged(*[rolled(sums, -k, 1) for k in range(5)])]
+    m0, m1, spread, third, _ = gathered(sums_ref)
     step0 = m0 / m1
     norm1 = step0 * step0 * spread
     beta = norm1 / m0
@@ -268,9 +264,9 @@
     coef_b = step0 + step1 * (1.0 + beta)
     coef_w = -(step1 * step0)
 
-    place = place_ref[0]
-    above = far_ref[lax.rem(place + 2, peers), :, :256]
-    below = far_ref[lax.rem(place + peers - 2, peers), :, :256]
+    lower = lax.rem(place_ref[0], 4) < 2
+    above = jnp.where(lower, far2_ref[...], far1_ref[...])
+    below = jnp.where(lower, far1_ref[...], far2_ref[...])
     above, below = joined(above, above), joined(below, below)
     cot = {(c, y): cot_frame(refs, row, c, y) for c in range(3) for y in range(-2, 6)}
     b = {y: b_ref[y + 3] for y in range(-3, 7)}
@@ -321,62 +317,76 @@
             out_ref[i, y] = flat[i, y] + (0.5 * time_step) * (upright[i, y + 1] - upright[i, y - 1])
 
 
-def call(kernel, outs, scalars, arrays, place=pltpu.VMEM, scratch=()):
+def call(kernel, outs, scalars, arrays):
     vmem = pl.BlockSpec(memory_space=pltpu.VMEM)
-    given = pl.BlockSpec(memory_space=place)
     smem = pl.BlockSpec(memory_space=pltpu.SMEM)
     return pl.pallas_call(
         kernel,
         out_shape=[jax.ShapeDtypeStruct(s, jnp.float32) for s in outs],
-        in_specs=[smem] * len(scalars) + [given] * len(arrays),
+        in_specs=[smem] * len(scalars) + [vmem] * len(arrays),
         out_specs=[vmem] * len(outs),
-        scratch_shapes=list(scratch),
         compiler_params=pltpu.CompilerParams(vmem_limit_bytes=32 * 1024 * 1024),
     )(*scalars, *arrays)
 
 
-def swap_across(x, axis):
-    n = lax.axis_size(axis)
-    return lax.ppermute(x, axis, [(i, (i + 1 if i % 2 else i - 1) % n) for i in range(n)])
-
-
-def swap_within(x, axis):
-    return lax.ppermute(x, axis, [(i, i ^ 1) for i in range(lax.axis_size(axis))])
+PY = ("y_low", "z")
+PZ = ("y_high", "x", "core")
+STEPS = (("z", "core"), ("y_high", "y_low", "x"))
+
+
+def size(axes):
+    return math.prod(lax.axis_size(axis) for axis in axes)
+
+
+def swap_across(x, axes, reach=1):
+    n = size(axes)
+    return lax.ppermute(x, axes, [(i, (i + (reach if i // reach % 2 else -reach)) % n) for i in range(n)])
+
+
+def swap_within(x, axes, reach=1):
+    return lax.ppermute(x, axes, [(i, i ^ reach) for i in range(size(axes))])
 
 
 def body(velocity, cotangent):
-    ny, nz = lax.axis_size("py"), lax.axis_size("pz")
-    place = lax.axis_index("py").astype(jnp.int32).reshape(1)
+    place = lax.axis_index(PY).astype(jnp.int32).reshape(1)
+    odd = lax.axis_index("core").astype(jnp.int32).reshape(1)
     block = (3, ROWS, TILE, 256)
-    dmas = [pltpu.SemaphoreType.DMA((2,))]
-    odd = lax.rem(lax.axis_index("pz"), 2).astype(jnp.int32).reshape(1)
     cross, core, cotangent, velocity = call(
-        pack_z, [block] * 4, [odd], [cotangent, velocity], pltpu.HBM, dmas
+        pack_z, [block] * 4, [odd], [jnp.concatenate([cotangent, velocity], axis=0)]
     )
-    cross = swap_across(cross, "pz")
-    core = swap_within(core, "pz")
+    cross = swap_across(cross, PZ)
+    core = swap_within(core, PZ)
     sent = (SENT, TILE, 256)
-    first, second, zn, zp = call(
-        pack_y, [sent, sent, block, block], [odd, place], [cotangent, velocity, cross, core]
+    far = (TILE, 256)
+    first, second, zn, zp, far1, far2 = call(
+        pack_y,
+        [sent, sent, block, block, far, far],
+        [odd, place],
+        [cotangent, velocity, cross, core],
     )
-    first = swap_across(first, "py")
-    second = swap_within(second, "py")
-    chunks, b, w, yn, yp = call(
-        functools.partial(moments, ny),
-        [(ny, TILE, 384), (10, WIDE, 256), (8, WIDE, 256), sent, sent],
+    first = swap_across(first, PY)
+    second = swap_within(second, PY)
+    far1 = swap_across(far1, PY, 2)
+    far2 = swap_within(far2, PY, 2)
+    lines, b, w, yn, yp = call(
+        moments,
+        [(size(STEPS[0]), 1, 128), (10, WIDE, 256), (8, WIDE, 256), sent, sent],
         [place],
         [cotangent, velocity, zn, zp, first, second],
     )
-    held = [cotangent, velocity, zn, zp, yn, yp]
-    got = lax.all_to_all(chunks, "py", 0, 0)
-    (lines,) = call(merge, [(nz, 1, 128)], [], [got])
-    sums = lax.all_to_all(lines, "pz", 0, 0)
-    (out,) = call(functools.partial(finish, ny), [block], [place], held + [got, b, w, sums])
+    got = lax.all_to_all(lines, STEPS[0], 0, 0)
+    (lines,) = call(merge, [(size(STEPS[1]), 1, 128)], [], [got])
+    sums = lax.all_to_all(lines, STEPS[1], 0, 0)
+    held = [cotangent, velocity, zn, zp, yn, yp, far1, far2]
+    (out,) = call(finish, [block], [place], held + [b, w, sums])
     return out
 
 
 def solution(mesh):
-    placed = (P(None, "py", "pz", None), P(None, "py", "pz", None))
-    return jax.shard_map(
-        body, mesh=mesh, in_specs=placed, out_specs=P(None, "py", "pz", None), check_vma=False
-    )
+    ny, nz = mesh.shape["py"], mesh.shape["pz"]
+    x = min(8, nz // 2)
+    shape = (2, ny // 2, nz // (2 * x), x, 2)
+    names = ("y_low", "z", "y_high", "x", "core")
+    fine = jax.sharding.Mesh(mesh.devices.reshape(shape), names)
+    placed = P(None, PY, PZ, None)
+    return jax.shard_map(body, mesh=fine, in_specs=(placed, placed), out_specs=placed, check_vma=False)

time: 73.6 us -> 70.9 us (0.963)
  blocking collectives: 32 us -> 11 us
  starting transfers between devices: 31.2 us -> 44 us
  waiting for transfers between devices: 5.98 us -> 11.9 us
  local copies, waits for them, and re-layouts: 1.78 us -> 0 us
  other arithmetic: 0 us -> 0.95 us
    all_to_all x2 -> x1, blocking collectives: 32 us -> 11 us  [body(): got = lax.all_to_all(lines, STEPS[0], 0, 0)]
    all_to_all x0 -> x1, starting transfers between devices: none -> 7.9 us  [body(): sums = lax.all_to_all(lines, STEPS[1], 0, 0)]
    ppermute x4 -> x6, starting transfers between devices: 31.2 us -> 36.1 us  [the longest x3 18.7 us: swap_across(): lax.ppermute(x, axes, [(i, (i + (reach if i // reach % 2 else -reach)) %...]
    ppermute x4 -> x6, waiting for transfers between devices: 5.98 us -> 9.64 us  [the longest x3 5.17 us: swap_across(): lax.ppermute(x, axes, [(i, (i + (reach if i // reach % 2 else -reach)) %...]
    all_to_all x0 -> x1, waiting for transfers between devices: none -> 2.23 us  [body(): sums = lax.all_to_all(lines, STEPS[1], 0, 0)]
    unnamed x4 -> x0, local copies, waits for them, and re-layouts: 1.78 us -> none
    concatenate x0 -> x1, other arithmetic: none -> 0.95 us  [body(): jnp.concatenate([cotangent, velocity], axis=0)]
  transfers between devices with their start and end apart: 4 -> 7, of which waited for: 3 -> 6; matrix products, arithmetic and copies ran while one was open for 0% -> 0% of each run, Pallas kernels for 0% -> 0%
where the time goes in v5:
time: 70.9 us; the launch traced here: 70.5 us
  starting transfers between devices  44 us (62%)
  waiting for transfers between devices  11.9 us (17%)
  blocking collectives  11 us (16%)
  Pallas kernels  2.66 us (4%)
  other arithmetic  0.95 us (1%)
    ppermute x3, starting transfers between devices, swap_across(): lax.ppermute(x, axes, [(i, (i + (reach if i // reach % 2 else -reach)) %...  18.7 us
    ppermute x3, starting transfers between devices, swap_within(): return lax.ppermute(x, axes, [(i, i ^ reach) for i in range(size(axes))])  17.3 us
    all_to_all x1, blocking collectives, body(): got = lax.all_to_all(lines, STEPS[0], 0, 0)  11 us
    all_to_all x1, starting transfers between devices, body(): sums = lax.all_to_all(lines, STEPS[1], 0, 0)  7.9 us
    ppermute x3, waiting for transfers between devices, swap_across(): lax.ppermute(x, axes, [(i, (i + (reach if i // reach % 2 else -reach)) %...  5.17 us
    ppermute x3, waiting for transfers between devices, swap_within(): return lax.ppermute(x, axes, [(i, i ^ reach) for i in range(size(axes))])  4.46 us
    pallas_call x5, Pallas kernels, call(): pl.pallas_call(kernel, out_shape=[jax.ShapeDtypeStruct(s, jnp.float32) fo...  2.66 us
    all_to_all x1, waiting for transfers between devices, body(): sums = lax.all_to_all(lines, STEPS[1], 0, 0)  2.23 us
  transfers between devices with their start and end apart: 7, of which 6 were waited for; matrix products, arithmetic and copies ran while one was open for 0% of the time, Pallas kernels for 0%

profile of v5, /device:TPU:1, one launch (start us, length us, event | category | flops | bytes accessed | tf_op | source)
XLA Modules:
  0.0 70.5 jit_solution(910669419015133392)
XLA Ops:
  0.0 1.0 %pad_maximum_fusion.both_ref = f32[6,4,8,256]{3,2,1,0:T(8,128)S(1)} fusion(f32[3,4,8,256]{3,2,1,0:T(8,128)} %param.2, f32[3,4,8,256]{3,2,1,0:T(8,128)} %param.3), kind=kLoop, calls=%fused_computation | loop fusion | flops 49152 | bytes 393216 | tf_op jit(solution)/shard_map/concatenate | solution.py:355
  1.0 4.5 %collective-permute-start = (f32[3,4,8,256]{3,2,1,0:T(8,128)S(1)}, f32[3,4,8,256]{3,2,1,0:T(8,128)S(1)}, u32[]{:S(2)}, u32[]{:S(2)}) collective-permute-start(f32[3,4,8,256]{3,2,1,0:T(8,128)S(1)} %get-tuple-element.22), channel_id=1, source_target_pairs={{0,63},{1,2},{2,1},{3,4},{4,3},{5,6},{6,5},{7,8},{8,7},{9,10},{10,... | collective-permute-start | bytes 294920 | tf_op jit(solution)/shard_map/ppermute | solution.py:343
  5.5 13.5 %collective-permute-start.1 = (f32[3,4,8,256]{3,2,1,0:T(8,128)S(1)}, f32[3,4,8,256]{3,2,1,0:T(8,128)S(1)}, u32[]{:S(2)}, u32[]{:S(2)}) collective-permute-start(f32[3,4,8,256]{3,2,1,0:T(8,128)S(1)} %get-tuple-element.23), channel_id=1, source_target_pairs={{0,1},{1,0},{2,3},{3,2},{4,5},{5,4},{6,7},{7,6},{8,9},{9,8},{10,11... | collective-permute-start | bytes 294920 | tf_op jit(solution)/shard_map/ppermute | solution.py:347
  19.0 0.0 collective-permute-done.cross_ref
  19.0 0.9 %collective-permute-done.1.core_ref = f32[3,4,8,256]{3,2,1,0:T(8,128)S(1)} collective-permute-done((f32[3,4,8,256]{3,2,1,0:T(8,128)S(1)}, f32[3,4,8,256]{3,2,1,0:T(8,128)S(1)}, u32[]{:S(2)}, u32[]{:S(2)}) %collective-permute-start.1) | collective-permute-done | bytes 98336 | tf_op jit(solution)/shard_map/ppermute | solution.py:347
  19.9 0.1 shard_map.29
  20.0 11.3 %collective-permute-start.2 = (f32[20,8,256]{2,1,0:T(8,128)S(1)}, f32[20,8,256]{2,1,0:T(8,128)S(1)}, u32[]{:S(2)}, u32[]{:S(2)}) collective-permute-start(f32[20,8,256]{2,1,0:T(8,128)S(1)} %get-tuple-element.26), channel_id=1, source_target_pairs={{0,960},{64,128},{128,64},{192,256},{256,192},{320,384},{384,320},... | collective-permute-start | bytes 491528 | tf_op jit(solution)/shard_map/ppermute | solution.py:343
  31.3 1.9 %collective-permute-start.3 = (f32[20,8,256]{2,1,0:T(8,128)S(1)}, f32[20,8,256]{2,1,0:T(8,128)S(1)}, u32[]{:S(2)}, u32[]{:S(2)}) collective-permute-start(f32[20,8,256]{2,1,0:T(8,128)S(1)} %get-tuple-element.27), channel_id=1, source_target_pairs={{0,64},{64,0},{128,192},{192,128},{256,320},{320,256},{384,448},{4... | collective-permute-start | bytes 491528 | tf_op jit(solution)/shard_map/ppermute | solution.py:347
  33.3 2.3 %collective-permute-done.2.first_ref = f32[20,8,256]{2,1,0:T(8,128)S(1)} collective-permute-done((f32[20,8,256]{2,1,0:T(8,128)S(1)}, f32[20,8,256]{2,1,0:T(8,128)S(1)}, u32[]{:S(2)}, u32[]{:S(2)}) %collective-permute-start.2) | collective-permute-done | bytes 163872 | tf_op jit(solution)/shard_map/ppermute | solution.py:343
  35.6 2.7 %collective-permute-done.3.second_ref = f32[20,8,256]{2,1,0:T(8,128)S(1)} collective-permute-done((f32[20,8,256]{2,1,0:T(8,128)S(1)}, f32[20,8,256]{2,1,0:T(8,128)S(1)}, u32[]{:S(2)}, u32[]{:S(2)}) %collective-permute-start.3) | collective-permute-done | bytes 163872 | tf_op jit(solution)/shard_map/ppermute | solution.py:347
  38.3 0.4 shard_map.30
  38.7 11.0 %all_to_all.10.got_ref = f32[16,1,128]{2,1,0:T(1,128)S(1)} all-to-all(f32[16,1,128]{2,1,0:T(1,128)S(1)} %get-tuple-element.34), channel_id=1, replica_groups=mesh['y_low'=2,'z'=8,'y_high'=4,'x'=8,'core'=2] {'z','core'}, dimensions={0} | all-to-all | bytes 16384 | tf_op jit(solution)/shard_map/all_to_all | solution.py:377
  49.6 0.8 %shard_map.31 = f32[64,1,128]{2,1,0:T(1,128)} custom-call(f32[16,1,128]{2,1,0:T(1,128)S(1)} %all_to_all.10.got_ref), custom_call_target="tpu_custom_call" | custom-call | tf_op jit(solution)/shard_map/pallas_call | solution.py:323
  50.4 7.9 %all-to-all-start.1 = ((f32[64,1,128]{2,1,0:T(1,128)}), f32[64,1,128]{2,1,0:T(1,128)S(1)}, u32[]{:S(2)}, u32[]{:S(2)}) async-start(f32[64,1,128]{2,1,0:T(1,128)} %shard_map.31), calls=%async_computation.1 | async-start | bytes 65536 | tf_op jit(solution)/shard_map/all_to_all | solution.py:379
  58.4 2.9 %collective-permute-start.4 = (f32[8,256]{1,0:T(8,128)S(1)}, f32[8,256]{1,0:T(8,128)S(1)}, u32[]{:S(2)}, u32[]{:S(2)}) collective-permute-start(f32[8,256]{1,0:T(8,128)S(1)} %get-tuple-element.30), channel_id=1, source_target_pairs={{0,896},{64,960},{128,256},{192,320},{256,128},{320,192},{384,512}... | collective-permute-start | bytes 24584 | tf_op jit(solution)/shard_map/ppermute | solution.py:343
  61.3 1.9 %collective-permute-start.5 = (f32[8,256]{1,0:T(8,128)S(1)}, f32[8,256]{1,0:T(8,128)S(1)}, u32[]{:S(2)}, u32[]{:S(2)}) collective-permute-start(f32[8,256]{1,0:T(8,128)S(1)} %get-tuple-element.31), channel_id=1, source_target_pairs={{0,128},{64,192},{128,0},{192,64},{256,384},{320,448},{384,256},{4... | collective-permute-start | bytes 24584 | tf_op jit(solution)/shard_map/ppermute | solution.py:347
  63.2 2.8 %collective-permute-done.4.far1_ref = f32[8,256]{1,0:T(8,128)S(1)} collective-permute-done((f32[8,256]{1,0:T(8,128)S(1)}, f32[8,256]{1,0:T(8,128)S(1)}, u32[]{:S(2)}, u32[]{:S(2)}) %collective-permute-start.4) | collective-permute-done | bytes 8224 | tf_op jit(solution)/shard_map/ppermute | solution.py:343
  66.1 0.8 %collective-permute-done.5.far2_ref = f32[8,256]{1,0:T(8,128)S(1)} collective-permute-done((f32[8,256]{1,0:T(8,128)S(1)}, f32[8,256]{1,0:T(8,128)S(1)}, u32[]{:S(2)}, u32[]{:S(2)}) %collective-permute-start.5) | collective-permute-done | bytes 8224 | tf_op jit(solution)/shard_map/ppermute | solution.py:347
  66.9 2.2 %all-to-all-done.1.sums_ref = f32[64,1,128]{2,1,0:T(1,128)S(1)} async-done(((f32[64,1,128]{2,1,0:T(1,128)}), f32[64,1,128]{2,1,0:T(1,128)S(1)}, u32[]{:S(2)}, u32[]{:S(2)}) %all-to-all-start.1) | async-done | bytes 32800 | tf_op jit(solution)/shard_map/all_to_all | solution.py:379
  69.1 1.3 %shard_map.32 = f32[3,4,8,256]{3,2,1,0:T(8,128)} custom-call(s32[1]{0:T(128)} %bitcast.place_ref, f32[3,4,8,256]{3,2,1,0:T(8,128)S(1)} %get-tuple-element.20.cot_ref, f32[3,4,8,256]{3,2,1,0:T(8,128)S(1)} %get-tuple-element.21.vel_ref, f32[3,4,8,256]{3,2,1,0:T(8,128)S(1)} %get-tuple-element.24.zn_ref, f32[3,4,8,256]{3,2,1,0:T(8,128)S(1)} %get-tuple-element.25.zp_ref, ...), custom_call_target="tpu_custom_call" | custom-call | tf_op jit(solution)/shard_map/pallas_call | solution.py:323
  (1 shorter events, 0.0 us)
Async XLA Ops:
  1.0 18.0 %collective-permute-start = (f32[3,4,8,256]{3,2,1,0:T(8,128)S(1)}, f32[3,4,8,256]{3,2,1,0:T(8,128)S(1)}, u32[]{:S(2)}, u32[]{:S(2)}) collective-permute-start(f32[3,4,8,256]{3,2,1,0:T(8,128)S(1)} %get-tuple-element.22), channel_id=1, source_target_pairs={{0,63},{1,2},{2,1},{3,4},{4,3},{5,6},{6,5},{7,8},{8,7},{9,10},{10,... | collective-permute-start | bytes 294920 | tf_op jit(solution)/shard_map/ppermute | solution.py:343
  5.5 14.4 %collective-permute-start.1 = (f32[3,4,8,256]{3,2,1,0:T(8,128)S(1)}, f32[3,4,8,256]{3,2,1,0:T(8,128)S(1)}, u32[]{:S(2)}, u32[]{:S(2)}) collective-permute-start(f32[3,4,8,256]{3,2,1,0:T(8,128)S(1)} %get-tuple-element.23), channel_id=1, source_target_pairs={{0,1},{1,0},{2,3},{3,2},{4,5},{5,4},{6,7},{7,6},{8,9},{9,8},{10,11... | collective-permute-start | bytes 294920 | tf_op jit(solution)/shard_map/ppermute | solution.py:347
  20.0 15.6 %collective-permute-start.2 = (f32[20,8,256]{2,1,0:T(8,128)S(1)}, f32[20,8,256]{2,1,0:T(8,128)S(1)}, u32[]{:S(2)}, u32[]{:S(2)}) collective-permute-start(f32[20,8,256]{2,1,0:T(8,128)S(1)} %get-tuple-element.26), channel_id=1, source_target_pairs={{0,960},{64,128},{128,64},{192,256},{256,192},{320,384},{384,320},... | collective-permute-start | bytes 491528 | tf_op jit(solution)/shard_map/ppermute | solution.py:343
  31.3 7.0 %collective-permute-start.3 = (f32[20,8,256]{2,1,0:T(8,128)S(1)}, f32[20,8,256]{2,1,0:T(8,128)S(1)}, u32[]{:S(2)}, u32[]{:S(2)}) collective-permute-start(f32[20,8,256]{2,1,0:T(8,128)S(1)} %get-tuple-element.27), channel_id=1, source_target_pairs={{0,64},{64,0},{128,192},{192,128},{256,320},{320,256},{384,448},{4... | collective-permute-start | bytes 491528 | tf_op jit(solution)/shard_map/ppermute | solution.py:347
  50.4 18.7 %all-to-all-start.1 = ((f32[64,1,128]{2,1,0:T(1,128)}), f32[64,1,128]{2,1,0:T(1,128)S(1)}, u32[]{:S(2)}, u32[]{:S(2)}) async-start(f32[64,1,128]{2,1,0:T(1,128)} %shard_map.31), calls=%async_computation.1 | async-start | bytes 65536 | tf_op jit(solution)/shard_map/all_to_all | solution.py:379
  58.4 7.7 %collective-permute-start.4 = (f32[8,256]{1,0:T(8,128)S(1)}, f32[8,256]{1,0:T(8,128)S(1)}, u32[]{:S(2)}, u32[]{:S(2)}) collective-permute-start(f32[8,256]{1,0:T(8,128)S(1)} %get-tuple-element.30), channel_id=1, source_target_pairs={{0,896},{64,960},{128,256},{192,320},{256,128},{320,192},{384,512}... | collective-permute-start | bytes 24584 | tf_op jit(solution)/shard_map/ppermute | solution.py:343
  61.3 5.6 %collective-permute-start.5 = (f32[8,256]{1,0:T(8,128)S(1)}, f32[8,256]{1,0:T(8,128)S(1)}, u32[]{:S(2)}, u32[]{:S(2)}) collective-permute-start(f32[8,256]{1,0:T(8,128)S(1)} %get-tuple-element.31), channel_id=1, source_target_pairs={{0,128},{64,192},{128,0},{192,64},{256,384},{320,448},{384,256},{4... | collective-permute-start | bytes 24584 | tf_op jit(solution)/shard_map/ppermute | solution.py:347

commit v6 on v5

v6 whole, which is shorter than its diff:
```python
import math

import jax
import jax.numpy as jnp
from jax import lax
from jax.experimental import pallas as pl
from jax.experimental.pallas import tpu as pltpu
from jax.sharding import PartitionSpec as P

smag_coef = 0.1156
time_step = 0.2
strain_floor = 0.25

ROWS = 4
TILE = 8
SIDE = 4
WIDE = TILE + 2 * SIDE
SOON = 6
LATE = 14


def rolled(x, shift, axis):
    return pltpu.roll(x, shift % x.shape[axis], axis)


def dx(f):
    n = f.ndim - 1
    return 0.5 * (rolled(f, -1, n) - rolled(f, 1, n))


def dz(f):
    n = f.ndim - 2
    return 0.5 * (rolled(f, -1, n) - rolled(f, 1, n))


def sublane():
    return lax.broadcasted_iota(jnp.int32, (TILE, 256), 0)


def pack_z(odd_ref, both_ref, cross_ref, core_ref, cot_ref, vel_ref):
    row = sublane()
    even = odd_ref[0] == 0
    for c in range(3):
        for y in range(ROWS):
            cot, vel = both_ref[c, y], both_ref[3 + c, y]
            cot_ref[c, y], vel_ref[c, y] = cot, vel
            to_prev = jnp.where(row < 5, cot, rolled(vel, 5, 0))
            to_next = jnp.where(row >= 3, cot, rolled(vel, 3, 0))
            cross_ref[c, y] = jnp.where(even, to_prev, to_next)
            core_ref[c, y] = jnp.where(even, to_next, to_prev)


def side_cot(row, zn, zp):
    return jnp.where(row < SIDE, zn, zp)


def side_vel(row, zn, zp):
    return jnp.where(row < SIDE, rolled(zn, 3, 0), rolled(zp, 5, 0))


def put(row, tile, k):
    return jnp.where(row < SIDE, rolled(tile, k, 0), rolled(tile, -k, 0))


def take(row, tile, k):
    return jnp.where(row < SIDE, rolled(tile, -k, 0), rolled(tile, k, 0))


def mixed(row, base, inner):
    for k, tile in inner:
        base = jnp.where((row == k) | (row == TILE - 1 - k), put(row, tile, k), base)
    return base


def joined(a, b):
    return jnp.concatenate([a, b], axis=0)


def own_parts(refs, row):
    flat, cot_y = {}, {}
    for y in range(ROWS):
        flat[y] = -(dx(cot_frame(refs, row, 0, y)) + along_z_cot(refs, row, cot_frame(refs, row, 2, y), y))
        cot_y[y] = cot_frame(refs, row, 1, y)
    return flat, cot_y


def paired(place_ref, to_prev, to_next, first_ref, second_ref):
    even = lax.rem(place_ref[0], 2) == 0
    for k in range(first_ref.shape[0]):
        first_ref[k] = jnp.where(even, to_prev[k], to_next[k])
        second_ref[k] = jnp.where(even, to_next[k], to_prev[k])


def unpaired(place_ref, first_ref, second_ref):
    even = lax.rem(place_ref[0], 2) == 0
    tiles = range(first_ref.shape[0])
    after = [jnp.where(even, second_ref[k], first_ref[k]) for k in tiles]
    before = [jnp.where(even, first_ref[k], second_ref[k]) for k in tiles]
    return after, before


def pack_y(odd_ref, place_ref, cot_ref, vel_ref, cross_ref, core_ref, first_ref, second_ref, zn_ref, zp_ref):
    even = odd_ref[0] == 0
    for c in range(3):
        for y in range(ROWS):
            cross, core = cross_ref[c, y], core_ref[c, y]
            zn_ref[c, y] = jnp.where(even, core, cross)
            zp_ref[c, y] = jnp.where(even, cross, core)
    refs = (cot_ref, vel_ref, zn_ref, zp_ref)
    row = sublane()
    flat, cot_y = own_parts(refs, row)
    low = flat[0] - 0.5 * cot_y[1]
    high = flat[3] + 0.5 * cot_y[2]
    one = flat[1] - 0.5 * (cot_y[2] - cot_y[0])
    two = flat[2] - 0.5 * (cot_y[3] - cot_y[1])
    to_prev, to_next = [], []
    for out, part, edge in ((to_prev, (low, one, two), 0), (to_next, (high, two, one), 3)):
        side_x = side_cot(row, zn_ref[0, edge], zp_ref[0, edge])
        side_z = side_cot(row, zn_ref[2, edge], zp_ref[2, edge])
        out.append(part[0][:TILE])
        out.append(part[1][:TILE])
        out.append(cot_y[edge][:TILE])
        out.append(mixed(row, part[0][TILE:], [(3, part[2][TILE:])]))
        out.append(mixed(row, part[1][TILE:], [(2, side_x), (3, side_z)]))
        out.append(cot_y[edge][TILE:])
    paired(place_ref, to_prev, to_next, first_ref, second_ref)


def pack_late(place_ref, refs, row, b, first_ref, second_ref):
    cot_ref, vel_ref, zn_ref, zp_ref = refs
    to_prev, to_next = [], []
    for out, d1, d2, d3, d4 in ((to_prev, 0, 1, 2, 3), (to_next, 3, 2, 1, 0)):
        out += [b[d3][:TILE], b[d4][:TILE], cot_ref[0, d1], cot_ref[2, d1]]
        out += [cot_ref[c, d2] for c in range(3)]
        out += [vel_ref[c, d1] for c in range(3)]
        out += [vel_ref[c, d2] for c in range(3)]
        vel = [side_vel(row, zn_ref[c, d1], zp_ref[c, d1]) for c in range(3)]
        out.append(mixed(row, vel[0], [(1, vel[1]), (2, vel[2])]))
    paired(place_ref, to_prev, to_next, first_ref, second_ref)


def cot_frame(refs, row, c, y):
    cot_ref, _, zn_ref, zp_ref = refs
    return joined(cot_ref[c, y], side_cot(row, zn_ref[c, y], zp_ref[c, y]))


def vel_frame(refs, row, c, y):
    _, vel_ref, zn_ref, zp_ref = refs
    return joined(vel_ref[c, y], side_vel(row, zn_ref[c, y], zp_ref[c, y]))


def along_z_cot(refs, row, frame, y):
    if not 0 <= y < ROWS:
        return dz(frame)
    zn_ref, zp_ref = refs[2], refs[3]
    ends = jnp.where(row < SIDE, zp_ref[2, y], zn_ref[2, y])
    wide = lax.broadcasted_iota(jnp.int32, (WIDE, 256), 0)
    both = joined(ends, ends)
    after = jnp.where(wide == TILE + 3, rolled(both, -1, 0), rolled(frame, -1, 0))
    before = jnp.where(wide == TILE + 4, rolled(both, 1, 0), rolled(frame, 1, 0))
    return 0.5 * (after - before)


def laplace(here, below, above):
    beside = rolled(here, 1, 1) + rolled(here, -1, 1)
    beside = beside + above + below
    beside = beside + rolled(here, 1, 0) + rolled(here, -1, 0)
    return 6.0 * here - beside


def ratio(top, bottom):
    safe = bottom > 0.0
    return jnp.where(safe, top / jnp.where(safe, bottom, 1.0), 0.0)


def total(x):
    return jnp.sum(jnp.sum(x, axis=0, keepdims=True), axis=1, keepdims=True)


def moments(
    place_ref,
    cot_ref,
    vel_ref,
    zn_ref,
    zp_ref,
    first_ref,
    second_ref,
    out_ref,
    b_ref,
    w_ref,
):
    refs = (cot_ref, vel_ref, zn_ref, zp_ref)
    row = sublane()
    after, before = unpaired(place_ref, first_ref, second_ref)
    flat, cot_y = own_parts(refs, row)
    cot_y[-1], cot_y[4] = joined(before[2], before[5]), joined(after[2], after[5])
    b = {y: flat[y] - 0.5 * (cot_y[y + 1] - cot_y[y - 1]) for y in range(ROWS)}
    b[-1] = joined(before[0], before[3]) - 0.5 * cot_y[0]
    b[4] = joined(after[0], after[3]) + 0.5 * cot_y[3]
    b[-2] = joined(before[1], before[4])
    b[5] = joined(after[1], after[4])
    w = {y: laplace(b[y], b[y - 1], b[y + 1]) for y in range(-1, 5)}
    m0 = m1 = None
    for y in range(ROWS):
        bc, wc = b[y][:TILE], w[y][:TILE]
        m0 = bc * bc if m0 is None else m0 + bc * bc
        m1 = bc * wc if m1 is None else m1 + bc * wc
    m0, m1 = total(m0), total(m1)
    sigma = ratio(m1, m0)
    spread = third = cross = None
    for y in range(ROWS):
        bc, wc = b[y][:TILE], w[y][:TILE]
        x = laplace(w[y], w[y - 1], w[y + 1])[:TILE]
        v = wc - sigma * bc
        u = x - sigma * wc
        spread = v * v if spread is None else spread + v * v
        third = v * u if third is None else third + v * u
        cross = bc * u if cross is None else cross + bc * u
    spread, third, cross = total(spread), total(third), total(cross)
    spread_out((m0, m1, spread, third, cross), out_ref)
    for y in range(-2, 6):
        b_ref[y + 2] = b[y]
    for y in range(-1, 5):
        w_ref[y + 1] = w[y]


def spread_out(parts, out_ref):
    lane = lax.broadcasted_iota(jnp.int32, (1, 128), 1)
    line = jnp.zeros((1, 128), jnp.float32)
    for k, value in enumerate(parts):
        line = jnp.where(lane == k, value, line)
    for j in range(out_ref.shape[0]):
        out_ref[j] = line


def gathered(got_ref):
    lines = got_ref[...].reshape(got_ref.shape[0], 128)
    return [x[:, :1] for x in merged(*[rolled(lines, -k, 1) for k in range(5)])]


def merged(m0, m1, spread, third, cross):
    own = ratio(m1, m0)

    def over(x):
        return jnp.sum(x, axis=0, keepdims=True)

    all0, all1 = over(m0), over(m1)
    delta = ratio(all1, all0) - own
    all_spread = over(spread + delta * delta * m0)
    all_third = over(third - delta * (spread + cross) + delta * delta * m1)
    all_cross = over(cross - delta * m1)
    return all0, all1, all_spread, all_third, all_cross


def merge(place_ref, got_ref, cot_ref, vel_ref, zn_ref, zp_ref, b_ref, out_ref, late1_ref, late2_ref):
    spread_out(gathered(got_ref), out_ref)
    b = {y: b_ref[y + 2] for y in range(ROWS)}
    pack_late(place_ref, (cot_ref, vel_ref, zn_ref, zp_ref), sublane(), b, late1_ref, late2_ref)


def slope(vel, y, grad_ref, inverse_ref, at):
    grad = [[dx(vel[i, y]), 0.5 * (vel[i, y + 1] - vel[i, y - 1]), dz(vel[i, y])] for i in range(3)]
    inside = None
    for i in range(3):
        for j in range(3):
            grad_ref[at, 3 * i + j] = grad[i][j]
        for j in range(i + 1):
            strain = grad[i][i] if i == j else 0.5 * (grad[i][j] + grad[j][i])
            square = (1.0 if i == j else 2.0) * (strain * strain)
            inside = square if inside is None else inside + square
    inverse_ref[at] = lax.rsqrt(2.0 * inside + strain_floor)


INNER = (1, 2)
OUTER = (-1, 0, 3, 4)


def inner_slopes(cot_ref, vel_ref, zn_ref, zp_ref, lines_ref, grad_ref, inverse_ref):
    refs = (cot_ref, vel_ref, zn_ref, zp_ref)
    row = sublane()
    vel = {(c, y): vel_frame(refs, row, c, y) for c in range(3) for y in range(ROWS)}
    for at, y in enumerate(INNER):
        slope(vel, y, grad_ref, inverse_ref, at)


def outer_slopes(place_ref, cot_ref, vel_ref, zn_ref, zp_ref, late1_ref, late2_ref, grad_ref, inverse_ref):
    refs = (cot_ref, vel_ref, zn_ref, zp_ref)
    row = sublane()
    vel = {(c, y): vel_frame(refs, row, c, y) for c in range(3) for y in range(ROWS)}
    late = unpaired(place_ref, late1_ref, late2_ref)
    for got, edge, step in ((late[0], ROWS - 1, 1), (late[1], 0, -1)):
        for c in range(3):
            vel[c, edge + step] = joined(got[7 + c], take(row, got[13], c))
            vel[c, edge + 2 * step] = joined(got[10 + c], got[10 + c])
    for at, y in enumerate(OUTER):
        slope(vel, y, grad_ref, inverse_ref, at)


def finish(
    place_ref,
    cot_ref,
    vel_ref,
    zn_ref,
    zp_ref,
    first_ref,
    second_ref,
    late1_ref,
    late2_ref,
    b_ref,
    w_ref,
    inner_grad_ref,
    inner_inverse_ref,
    outer_grad_ref,
    outer_inverse_ref,
    sums_ref,
    out_ref,
):
    refs = (cot_ref, vel_ref, zn_ref, zp_ref)
    row = sublane()
    m0, m1, spread, third, _ = gathered(sums_ref)
    step0 = m0 / m1
    norm1 = step0 * step0 * spread
    beta = norm1 / m0
    bend = step0 * step0 * third - 2.0 * step0 * beta * spread + beta * beta * m1
    step1 = norm1 / bend
    coef_b = step0 + step1 * (1.0 + beta)
    coef_w = -(step1 * step0)

    b = {y: b_ref[y + 2] for y in range(-2, 6)}
    w = {y: w_ref[y + 1] for y in range(-1, 5)}
    cot = {(c, y): cot_frame(refs, row, c, y) for c in range(3) for y in range(ROWS)}
    vel = {(c, y): vel_frame(refs, row, c, y) for c in range(3) for y in range(ROWS)}
    soon = unpaired(place_ref, first_ref, second_ref)
    late = unpaired(place_ref, late1_ref, late2_ref)
    for side, edge, step in ((0, ROWS - 1, 1), (1, 0, -1)):
        near, got = soon[side], late[side]
        y1, y2, y3, y4 = [edge + step * d for d in range(1, 5)]
        b[y3] = joined(got[0], take(row, near[3], 3))
        b[y4] = joined(got[1], got[1])
        cot[0, y1] = joined(got[2], take(row, near[4], 2))
        cot[1, y1] = joined(near[2], near[5])
        cot[2, y1] = joined(got[3], take(row, near[4], 3))
        for c in range(3):
            cot[c, y2] = joined(got[4 + c], got[4 + c])
            vel[c, y1] = joined(got[7 + c], take(row, got[13], c))
            vel[c, y2] = joined(got[10 + c], got[10 + c])
    for y in (-3, -2, 5, 6):
        w[y] = laplace(b[y], b[y - 1], b[y + 1])
    p = {y: coef_b * b[y] + coef_w * w[y] for y in range(-3, 7)}
    lam = {}
    for y in range(-2, 6):
        lam[0, y] = cot[0, y] - dx(p[y])
        lam[1, y] = cot[1, y] - 0.5 * (p[y + 1] - p[y - 1])
        lam[2, y] = cot[2, y] - dz(p[y])

    flat, upright = {}, {}
    for y in range(-1, 5):
        grad_ref, inverse_ref, rows = (
            (inner_grad_ref, inner_inverse_ref, INNER)
            if y in INNER
            else (outer_grad_ref, outer_inverse_ref, OUTER)
        )
        at = rows.index(y)
        grad = [[grad_ref[at, 3 * i + j] for j in range(3)] for i in range(3)]
        pull = [[dx(lam[i, y]), 0.5 * (lam[i, y + 1] - lam[i, y - 1]), dz(lam[i, y])] for i in range(3)]
        strain, ebb = {}, {}
        for i in range(3):
            for j in range(i + 1):
                strain[i, j] = grad[i][i] if i == j else 0.5 * (grad[i][j] + grad[j][i])
                ebb[i, j] = pull[i][i] if i == j else 0.5 * (pull[i][j] + pull[j][i])
        work = strain[0, 0] * ebb[0, 0] + strain[1, 1] * ebb[1, 1] + strain[2, 2] * ebb[2, 2]
        off_work = strain[1, 0] * ebb[1, 0] + strain[2, 0] * ebb[2, 0] + strain[2, 1] * ebb[2, 1]
        inverse = inverse_ref[at]
        twice = (2.0 * smag_coef) / inverse
        factor = (4.0 * smag_coef) * inverse * (work + 2.0 * off_work)
        stress = {key: twice * ebb[key] + factor * strain[key] for key in strain}

        def both(i, j):
            return stress[max(i, j), min(i, j)] + lam[i, y] * vel[j, y]

        for i in range(3):
            upright[i, y] = both(i, 1)[:TILE]
        if 0 <= y < ROWS:
            for i in range(3):
                carried = lam[0, y] * grad[0][i] + lam[1, y] * grad[1][i] + lam[2, y] * grad[2][i]
                level = dx(both(i, 0)) + dz(both(i, 2))
                flat[i, y] = (lam[i, y] + time_step * (level - carried))[:TILE]
    for i in range(3):
        for y in range(ROWS):
            out_ref[i, y] = flat[i, y] + (0.5 * time_step) * (upright[i, y + 1] - upright[i, y - 1])


def call(kernel, outs, scalars, arrays, cost=None):
    vmem = pl.BlockSpec(memory_space=pltpu.VMEM)
    smem = pl.BlockSpec(memory_space=pltpu.SMEM)
    return pl.pallas_call(
        kernel,
        out_shape=[jax.ShapeDtypeStruct(s, jnp.float32) for s in outs],
        in_specs=[smem] * len(scalars) + [vmem] * len(arrays),
        out_specs=[vmem] * len(outs),
        cost_estimate=cost and pl.CostEstimate(flops=cost, bytes_accessed=2_000_000, transcendentals=100_000),
        compiler_params=pltpu.CompilerParams(vmem_limit_bytes=32 * 1024 * 1024),
    )(*scalars, *arrays)


PY = ("y_low", "z")
PZ = ("y_high", "x", "core")
STEPS = (("z", "core"), ("y_high", "y_low", "x"))


def size(axes):
    return math.prod(lax.axis_size(axis) for axis in axes)


def swap_across(x, axes):
    n = size(axes)
    return lax.ppermute(x, axes, [(i, (i + 1 if i % 2 else i - 1) % n) for i in range(n)])


def swap_within(x, axes):
    return lax.ppermute(x, axes, [(i, i ^ 1) for i in range(size(axes))])


def body(velocity, cotangent):
    place = lax.axis_index(PY).astype(jnp.int32).reshape(1)
    odd = lax.axis_index("core").astype(jnp.int32).reshape(1)
    block = (3, ROWS, TILE, 256)
    cross, core, cotangent, velocity = call(
        pack_z, [block] * 4, [odd], [jnp.concatenate([cotangent, velocity], axis=0)]
    )
    cross = swap_across(cross, PZ)
    core = swap_within(core, PZ)
    soon, later = (SOON, TILE, 256), (LATE, TILE, 256)
    first, second, zn, zp = call(
        pack_y, [soon, soon, block, block], [odd, place], [cotangent, velocity, cross, core]
    )
    held = [cotangent, velocity, zn, zp, swap_across(first, PY), swap_within(second, PY)]
    lines, b, w = call(
        moments,
        [(size(STEPS[0]), 1, 128), (8, WIDE, 256), (6, WIDE, 256)],
        [place],
        held,
    )
    got = lax.all_to_all(lines, STEPS[0], 0, 0)
    lines, late1, late2 = call(
        merge, [(size(STEPS[1]), 1, 128), later, later], [place], [got] + held[:4] + [b]
    )
    sums = lax.all_to_all(lines, STEPS[1], 0, 0)
    late = [swap_across(late1, PY), swap_within(late2, PY)]
    inner = call(inner_slopes, [(2, 9, WIDE, 256), (2, WIDE, 256)], [], held[:4] + [lines], 4_000_000_000)
    outer = call(outer_slopes, [(4, 9, WIDE, 256), (4, WIDE, 256)], [place], held[:4] + late, 4_000_000)
    (out,) = call(finish, [block], [place], held + late + [b, w, *inner, *outer, sums])
    return out


def solution(mesh):
    ny, nz = mesh.shape["py"], mesh.shape["pz"]
    x = min(8, nz // 2)
    shape = (2, ny // 2, nz // (2 * x), x, 2)
    names = ("y_low", "z", "y_high", "x", "core")
    fine = jax.sharding.Mesh(mesh.devices.reshape(shape), names)
    placed = P(None, PY, PZ, None)
    return jax.shard_map(body, mesh=fine, in_specs=(placed, placed), out_specs=placed, check_vma=False)
```

time: 70.9 us -> 69.6 us (0.982)
  waiting for transfers between devices: 11.9 us -> 8.63 us
  Pallas kernels: 2.66 us -> 3.67 us
    ppermute x6, waiting for transfers between devices: 9.64 us -> 6.81 us  [the longest x3 4.48 us: swap_within(): return lax.ppermute(x, axes, [(i, i ^ 1) for i in range(size(axes))])]
    pallas_call x5 -> x7, Pallas kernels: 2.66 us -> 3.67 us  [call(): pl.pallas_call(kernel, out_shape=[jax.ShapeDtypeStruct(s, jnp.float32) fo...]
  transfers between devices with their start and end apart: 7 -> 7, of which waited for: 6 -> 5; matrix products, arithmetic and copies ran while one was open for 0% -> 0% of each run, Pallas kernels for 0% -> 2%
where the time goes in v6:
time: 69.6 us; the launch traced here: 69.2 us
  starting transfers between devices  44.6 us (64%)
  blocking collectives  11.2 us (16%)
  waiting for transfers between devices  8.63 us (12%)
  Pallas kernels  3.67 us (5%)
  other arithmetic  0.95 us (1%)
    ppermute x3, starting transfers between devices, swap_across(): lax.ppermute(x, axes, [(i, (i + 1 if i % 2 else i - 1) % n) for i in rang...  18.7 us
    ppermute x3, starting transfers between devices, swap_within(): return lax.ppermute(x, axes, [(i, i ^ 1) for i in range(size(axes))])  17.3 us
    all_to_all x1, blocking collectives, body(): got = lax.all_to_all(lines, STEPS[0], 0, 0)  11.2 us
    all_to_all x1, starting transfers between devices, body(): sums = lax.all_to_all(lines, STEPS[1], 0, 0)  8.56 us
    ppermute x3, waiting for transfers between devices, swap_within(): return lax.ppermute(x, axes, [(i, i ^ 1) for i in range(size(axes))])  4.48 us
    pallas_call x7, Pallas kernels, call(): pl.pallas_call(kernel, out_shape=[jax.ShapeDtypeStruct(s, jnp.float32) fo...  3.67 us
    ppermute x3, waiting for transfers between devices, swap_across(): lax.ppermute(x, axes, [(i, (i + 1 if i % 2 else i - 1) % n) for i in rang...  2.33 us
    all_to_all x1, waiting for transfers between devices, body(): sums = lax.all_to_all(lines, STEPS[1], 0, 0)  1.82 us
  transfers between devices with their start and end apart: 7, of which 5 were waited for; matrix products, arithmetic and copies ran while one was open for 0% of the time, Pallas kernels for 2%

profile of v6, /device:TPU:1, one launch (start us, length us, event | category | flops | bytes accessed | tf_op | source)
XLA Modules:
  0.0 69.2 jit_solution(11907286782456649750)
XLA Ops:
  0.0 1.0 %pad_maximum_fusion.both_ref = f32[6,4,8,256]{3,2,1,0:T(8,128)S(1)} fusion(f32[3,4,8,256]{3,2,1,0:T(8,128)} %param.2, f32[3,4,8,256]{3,2,1,0:T(8,128)} %param.3), kind=kLoop, calls=%fused_computation | loop fusion | flops 49152 | bytes 393216 | tf_op jit(solution)/shard_map/concatenate | solution.py:429
  1.0 4.5 %collective-permute-start = (f32[3,4,8,256]{3,2,1,0:T(8,128)S(1)}, f32[3,4,8,256]{3,2,1,0:T(8,128)S(1)}, u32[]{:S(2)}, u32[]{:S(2)}) collective-permute-start(f32[3,4,8,256]{3,2,1,0:T(8,128)S(1)} %get-tuple-element.25), channel_id=1, source_target_pairs={{0,63},{1,2},{2,1},{3,4},{4,3},{5,6},{6,5},{7,8},{8,7},{9,10},{10,... | collective-permute-start | bytes 294920 | tf_op jit(solution)/shard_map/ppermute | solution.py:417
  5.5 13.5 %collective-permute-start.1 = (f32[3,4,8,256]{3,2,1,0:T(8,128)S(1)}, f32[3,4,8,256]{3,2,1,0:T(8,128)S(1)}, u32[]{:S(2)}, u32[]{:S(2)}) collective-permute-start(f32[3,4,8,256]{3,2,1,0:T(8,128)S(1)} %get-tuple-element.26), channel_id=1, source_target_pairs={{0,1},{1,0},{2,3},{3,2},{4,5},{5,4},{6,7},{7,6},{8,9},{9,8},{10,11... | collective-permute-start | bytes 294920 | tf_op jit(solution)/shard_map/ppermute | solution.py:421
  19.0 0.0 collective-permute-done.cross_ref
  19.0 0.9 %collective-permute-done.1.core_ref = f32[3,4,8,256]{3,2,1,0:T(8,128)S(1)} collective-permute-done((f32[3,4,8,256]{3,2,1,0:T(8,128)S(1)}, f32[3,4,8,256]{3,2,1,0:T(8,128)S(1)}, u32[]{:S(2)}, u32[]{:S(2)}) %collective-permute-start.1) | collective-permute-done | bytes 98336 | tf_op jit(solution)/shard_map/ppermute | solution.py:421
  19.9 0.1 shard_map.29
  20.0 11.3 %collective-permute-start.2 = (f32[6,8,256]{2,1,0:T(8,128)S(1)}, f32[6,8,256]{2,1,0:T(8,128)S(1)}, u32[]{:S(2)}, u32[]{:S(2)}) collective-permute-start(f32[6,8,256]{2,1,0:T(8,128)S(1)} %get-tuple-element.29), channel_id=1, source_target_pairs={{0,960},{64,128},{128,64},{192,256},{256,192},{320,384},{384,320},... | collective-permute-start | bytes 147464 | tf_op jit(solution)/shard_map/ppermute | solution.py:417
  31.3 1.9 %collective-permute-start.3 = (f32[6,8,256]{2,1,0:T(8,128)S(1)}, f32[6,8,256]{2,1,0:T(8,128)S(1)}, u32[]{:S(2)}, u32[]{:S(2)}) collective-permute-start(f32[6,8,256]{2,1,0:T(8,128)S(1)} %get-tuple-element.30), channel_id=1, source_target_pairs={{0,64},{64,0},{128,192},{192,128},{256,320},{320,256},{384,448},{4... | collective-permute-start | bytes 147464 | tf_op jit(solution)/shard_map/ppermute | solution.py:421
  33.3 0.0 collective-permute-done.2.first_ref
  33.3 2.9 %collective-permute-done.3.second_ref = f32[6,8,256]{2,1,0:T(8,128)S(1)} collective-permute-done((f32[6,8,256]{2,1,0:T(8,128)S(1)}, f32[6,8,256]{2,1,0:T(8,128)S(1)}, u32[]{:S(2)}, u32[]{:S(2)}) %collective-permute-start.3) | collective-permute-done | bytes 49184 | tf_op jit(solution)/shard_map/ppermute | solution.py:421
  36.2 0.4 shard_map.30
  36.5 11.2 %all_to_all.10.got_ref = f32[16,1,128]{2,1,0:T(1,128)S(1)} all-to-all(f32[16,1,128]{2,1,0:T(1,128)S(1)} %get-tuple-element.31), channel_id=1, replica_groups=mesh['y_low'=2,'z'=8,'y_high'=4,'x'=8,'core'=2] {'z','core'}, dimensions={0} | all-to-all | bytes 16384 | tf_op jit(solution)/shard_map/all_to_all | solution.py:444
  47.7 0.8 %shard_map.31 = (f32[64,1,128]{2,1,0:T(1,128)}, f32[14,8,256]{2,1,0:T(8,128)S(1)}, f32[14,8,256]{2,1,0:T(8,128)S(1)}) custom-call(s32[1]{0:T(128)} %bitcast.place_ref, f32[16,1,128]{2,1,0:T(1,128)S(1)} %all_to_all.10.got_ref, f32[3,4,8,256]{3,2,1,0:T(8,128)S(1)} %get-tuple-element.23.cot_ref, f32[3,4,8,256]{3,2,1,0:T(8,128)S(1)} %get-tuple-element.24.vel_ref, ...), custom_call_target="tpu_custom_call" | custom-call | tf_op jit(solution)/shard_map/pallas_call | solution.py:396
  48.6 8.6 %all-to-all-start.1 = ((f32[64,1,128]{2,1,0:T(1,128)}), f32[64,1,128]{2,1,0:T(1,128)S(1)}, u32[]{:S(2)}, u32[]{:S(2)}) async-start(f32[64,1,128]{2,1,0:T(1,128)} %get-tuple-element.36.lines_ref), calls=%async_computation.1 | async-start | bytes 65536 | tf_op jit(solution)/shard_map/all_to_all | solution.py:448
  57.1 2.9 %collective-permute-start.4 = (f32[14,8,256]{2,1,0:T(8,128)S(1)}, f32[14,8,256]{2,1,0:T(8,128)S(1)}, u32[]{:S(2)}, u32[]{:S(2)}) collective-permute-start(f32[14,8,256]{2,1,0:T(8,128)S(1)} %get-tuple-element.33), channel_id=1, source_target_pairs={{0,960},{64,128},{128,64},{192,256},{256,192},{320,384},{384,320},... | collective-permute-start | bytes 344072 | tf_op jit(solution)/shard_map/ppermute | solution.py:417
  60.1 1.9 %collective-permute-start.5 = (f32[14,8,256]{2,1,0:T(8,128)S(1)}, f32[14,8,256]{2,1,0:T(8,128)S(1)}, u32[]{:S(2)}, u32[]{:S(2)}) collective-permute-start(f32[14,8,256]{2,1,0:T(8,128)S(1)} %get-tuple-element.34), channel_id=1, source_target_pairs={{0,64},{64,0},{128,192},{192,128},{256,320},{320,256},{384,448},{4... | collective-permute-start | bytes 344072 | tf_op jit(solution)/shard_map/ppermute | solution.py:421
  62.0 0.9 %shard_map.32 = (f32[2,9,16,256]{3,2,1,0:T(8,128)S(1)}, f32[2,16,256]{2,1,0:T(8,128)S(1)}) custom-call(f32[3,4,8,256]{3,2,1,0:T(8,128)S(1)} %get-tuple-element.23.cot_ref, f32[3,4,8,256]{3,2,1,0:T(8,128)S(1)} %get-tuple-element.24.vel_ref, f32[3,4,8,256]{3,2,1,0:T(8,128)S(1)} %get-tuple-element.27.zn_ref, f32[3,4,8,256]{3,2,1,0:T(8,128)S(1)} %get-tuple-element.28.zp_ref, ...), custom_call_target="tpu_custom_call" | custom-call | flops 4000000000 | bytes 2000000 | tf_op jit(solution)/shard_map/pallas_call | solution.py:396
  62.9 2.3 %collective-permute-done.4.late1_ref = f32[14,8,256]{2,1,0:T(8,128)S(1)} collective-permute-done((f32[14,8,256]{2,1,0:T(8,128)S(1)}, f32[14,8,256]{2,1,0:T(8,128)S(1)}, u32[]{:S(2)}, u32[]{:S(2)}) %collective-permute-start.4) | collective-permute-done | bytes 114720 | tf_op jit(solution)/shard_map/ppermute | solution.py:417
  65.2 0.7 collective-permute-done.5.late2_ref
  65.9 0.2 shard_map.33
  66.1 1.8 %all-to-all-done.1.sums_ref = f32[64,1,128]{2,1,0:T(1,128)S(1)} async-done(((f32[64,1,128]{2,1,0:T(1,128)}), f32[64,1,128]{2,1,0:T(1,128)S(1)}, u32[]{:S(2)}, u32[]{:S(2)}) %all-to-all-start.1) | async-done | bytes 32800 | tf_op jit(solution)/shard_map/all_to_all | solution.py:448
  67.9 1.3 %shard_map.34 = f32[3,4,8,256]{3,2,1,0:T(8,128)} custom-call(s32[1]{0:T(128)} %bitcast.place_ref, f32[3,4,8,256]{3,2,1,0:T(8,128)S(1)} %get-tuple-element.23.cot_ref, f32[3,4,8,256]{3,2,1,0:T(8,128)S(1)} %get-tuple-element.24.vel_ref, f32[3,4,8,256]{3,2,1,0:T(8,128)S(1)} %get-tuple-element.27.zn_ref, f32[3,4,8,256]{3,2,1,0:T(8,128)S(1)} %get-tuple-element.28.zp_ref, ...), custom_call_target="tpu_custom_call" | custom-call | tf_op jit(solution)/shard_map/pallas_call | solution.py:396
  (1 shorter events, 0.0 us)
Async XLA Ops:
  1.0 18.0 %collective-permute-start = (f32[3,4,8,256]{3,2,1,0:T(8,128)S(1)}, f32[3,4,8,256]{3,2,1,0:T(8,128)S(1)}, u32[]{:S(2)}, u32[]{:S(2)}) collective-permute-start(f32[3,4,8,256]{3,2,1,0:T(8,128)S(1)} %get-tuple-element.25), channel_id=1, source_target_pairs={{0,63},{1,2},{2,1},{3,4},{4,3},{5,6},{6,5},{7,8},{8,7},{9,10},{10,... | collective-permute-start | bytes 294920 | tf_op jit(solution)/shard_map/ppermute | solution.py:417
  5.5 14.4 %collective-permute-start.1 = (f32[3,4,8,256]{3,2,1,0:T(8,128)S(1)}, f32[3,4,8,256]{3,2,1,0:T(8,128)S(1)}, u32[]{:S(2)}, u32[]{:S(2)}) collective-permute-start(f32[3,4,8,256]{3,2,1,0:T(8,128)S(1)} %get-tuple-element.26), channel_id=1, source_target_pairs={{0,1},{1,0},{2,3},{3,2},{4,5},{5,4},{6,7},{7,6},{8,9},{9,8},{10,11... | collective-permute-start | bytes 294920 | tf_op jit(solution)/shard_map/ppermute | solution.py:421
  20.0 13.2 %collective-permute-start.2 = (f32[6,8,256]{2,1,0:T(8,128)S(1)}, f32[6,8,256]{2,1,0:T(8,128)S(1)}, u32[]{:S(2)}, u32[]{:S(2)}) collective-permute-start(f32[6,8,256]{2,1,0:T(8,128)S(1)} %get-tuple-element.29), channel_id=1, source_target_pairs={{0,960},{64,128},{128,64},{192,256},{256,192},{320,384},{384,320},... | collective-permute-start | bytes 147464 | tf_op jit(solution)/shard_map/ppermute | solution.py:417
  31.3 4.8 %collective-permute-start.3 = (f32[6,8,256]{2,1,0:T(8,128)S(1)}, f32[6,8,256]{2,1,0:T(8,128)S(1)}, u32[]{:S(2)}, u32[]{:S(2)}) collective-permute-start(f32[6,8,256]{2,1,0:T(8,128)S(1)} %get-tuple-element.30), channel_id=1, source_target_pairs={{0,64},{64,0},{128,192},{192,128},{256,320},{320,256},{384,448},{4... | collective-permute-start | bytes 147464 | tf_op jit(solution)/shard_map/ppermute | solution.py:421
  48.6 19.3 %all-to-all-start.1 = ((f32[64,1,128]{2,1,0:T(1,128)}), f32[64,1,128]{2,1,0:T(1,128)S(1)}, u32[]{:S(2)}, u32[]{:S(2)}) async-start(f32[64,1,128]{2,1,0:T(1,128)} %get-tuple-element.36.lines_ref), calls=%async_computation.1 | async-start | bytes 65536 | tf_op jit(solution)/shard_map/all_to_all | solution.py:448
  57.1 8.1 %collective-permute-start.4 = (f32[14,8,256]{2,1,0:T(8,128)S(1)}, f32[14,8,256]{2,1,0:T(8,128)S(1)}, u32[]{:S(2)}, u32[]{:S(2)}) collective-permute-start(f32[14,8,256]{2,1,0:T(8,128)S(1)} %get-tuple-element.33), channel_id=1, source_target_pairs={{0,960},{64,128},{128,64},{192,256},{256,192},{320,384},{384,320},... | collective-permute-start | bytes 344072 | tf_op jit(solution)/shard_map/ppermute | solution.py:417
  60.1 5.8 %collective-permute-start.5 = (f32[14,8,256]{2,1,0:T(8,128)S(1)}, f32[14,8,256]{2,1,0:T(8,128)S(1)}, u32[]{:S(2)}, u32[]{:S(2)}) collective-permute-start(f32[14,8,256]{2,1,0:T(8,128)S(1)} %get-tuple-element.34), channel_id=1, source_target_pairs={{0,64},{64,0},{128,192},{192,128},{256,320},{320,256},{384,448},{4... | collective-permute-start | bytes 344072 | tf_op jit(solution)/shard_map/ppermute | solution.py:421

commit v7 on v6

--- a/solution.py
+++ b/solution.py
@@ -188,6 +188,8 @@
     out_ref,
     b_ref,
     w_ref,
+    late1_ref,
+    late2_ref,
 ):
     refs = (cot_ref, vel_ref, zn_ref, zp_ref)
     row = sublane()
@@ -222,6 +224,7 @@
         b_ref[y + 2] = b[y]
     for y in range(-1, 5):
         w_ref[y + 1] = w[y]
+    pack_late(place_ref, refs, row, b, late1_ref, late2_ref)
 
 
 def spread_out(parts, out_ref):
@@ -252,10 +255,8 @@
     return all0, all1, all_spread, all_third, all_cross
 
 
-def merge(place_ref, got_ref, cot_ref, vel_ref, zn_ref, zp_ref, b_ref, out_ref, late1_ref, late2_ref):
+def merge(got_ref, out_ref):
     spread_out(gathered(got_ref), out_ref)
-    b = {y: b_ref[y + 2] for y in range(ROWS)}
-    pack_late(place_ref, (cot_ref, vel_ref, zn_ref, zp_ref), sublane(), b, late1_ref, late2_ref)
 
 
 def slope(vel, y, grad_ref, inverse_ref, at):
@@ -405,7 +406,7 @@
 
 PY = ("y_low", "z")
 PZ = ("y_high", "x", "core")
-STEPS = (("z", "core"), ("y_high", "y_low", "x"))
+STEPS = (("y_high", "y_low", "x"), ("z", "core"))
 
 
 def size(axes):
@@ -435,20 +436,18 @@
         pack_y, [soon, soon, block, block], [odd, place], [cotangent, velocity, cross, core]
     )
     held = [cotangent, velocity, zn, zp, swap_across(first, PY), swap_within(second, PY)]
-    lines, b, w = call(
+    lines, b, w, late1, late2 = call(
         moments,
-        [(size(STEPS[0]), 1, 128), (8, WIDE, 256), (6, WIDE, 256)],
+        [(size(STEPS[0]), 1, 128), (8, WIDE, 256), (6, WIDE, 256), later, later],
         [place],
         held,
     )
     got = lax.all_to_all(lines, STEPS[0], 0, 0)
-    lines, late1, late2 = call(
-        merge, [(size(STEPS[1]), 1, 128), later, later], [place], [got] + held[:4] + [b]
-    )
-    sums = lax.all_to_all(lines, STEPS[1], 0, 0)
     late = [swap_across(late1, PY), swap_within(late2, PY)]
     inner = call(inner_slopes, [(2, 9, WIDE, 256), (2, WIDE, 256)], [], held[:4] + [lines], 4_000_000_000)
     outer = call(outer_slopes, [(4, 9, WIDE, 256), (4, WIDE, 256)], [place], held[:4] + late, 4_000_000)
+    (lines,) = call(merge, [(size(STEPS[1]), 1, 128)], [], [got])
+    sums = lax.all_to_all(lines, STEPS[1], 0, 0)
     (out,) = call(finish, [block], [place], held + late + [b, w, *inner, *outer, sums])
     return out
 

time: 69.6 us -> 72.5 us (1.042)
  blocking collectives: 11.2 us -> 0 us
  waiting for transfers between devices: 8.63 us -> 16 us
  starting transfers between devices: 44.6 us -> 50.7 us
    all_to_all x1 -> x0, blocking collectives: 11.2 us -> none  [body(): got = lax.all_to_all(lines, STEPS[0], 0, 0)]
    all_to_all x0 -> x1, starting transfers between devices: none -> 8.25 us  [body(): got = lax.all_to_all(lines, STEPS[0], 0, 0)]
    all_to_all x0 -> x1, waiting for transfers between devices: none -> 6.23 us  [body(): got = lax.all_to_all(lines, STEPS[0], 0, 0)]
    all_to_all x1, waiting for transfers between devices: 1.82 us -> 5.94 us  [body(): sums = lax.all_to_all(lines, STEPS[1], 0, 0)]
    ppermute x3, waiting for transfers between devices: 2.33 us -> 0.01 us  [swap_across(): lax.ppermute(x, axes, [(i, (i + 1 if i % 2 else i - 1) % n) for i in rang...]
    all_to_all x1, starting transfers between devices: 8.56 us -> 6.76 us  [body(): sums = lax.all_to_all(lines, STEPS[1], 0, 0)]
  transfers between devices with their start and end apart: 7 -> 8, of which waited for: 5 -> 4; matrix products, arithmetic and copies ran while one was open for 0% -> 0% of each run, Pallas kernels for 2% -> 3%
where the time goes in v7:
time: 72.5 us; the launch traced here: 72 us
  starting transfers between devices  50.7 us (70%)
  waiting for transfers between devices  16 us (22%)
  Pallas kernels  4.26 us (6%)
  other arithmetic  0.95 us (1%)
    ppermute x3, starting transfers between devices, swap_across(): lax.ppermute(x, axes, [(i, (i + 1 if i % 2 else i - 1) % n) for i in rang...  18.4 us
    ppermute x3, starting transfers between devices, swap_within(): return lax.ppermute(x, axes, [(i, i ^ 1) for i in range(size(axes))])  17.3 us
    all_to_all x1, starting transfers between devices, body(): got = lax.all_to_all(lines, STEPS[0], 0, 0)  8.25 us
    all_to_all x1, starting transfers between devices, body(): sums = lax.all_to_all(lines, STEPS[1], 0, 0)  6.76 us
    all_to_all x1, waiting for transfers between devices, body(): got = lax.all_to_all(lines, STEPS[0], 0, 0)  6.23 us
    all_to_all x1, waiting for transfers between devices, body(): sums = lax.all_to_all(lines, STEPS[1], 0, 0)  5.94 us
    pallas_call x7, Pallas kernels, call(): pl.pallas_call(kernel, out_shape=[jax.ShapeDtypeStruct(s, jnp.float32) fo...  4.26 us
    ppermute x3, waiting for transfers between devices, swap_within(): return lax.ppermute(x, axes, [(i, i ^ 1) for i in range(size(axes))])  3.8 us
  transfers between devices with their start and end apart: 8, of which 4 were waited for; matrix products, arithmetic and copies ran while one was open for 0% of the time, Pallas kernels for 3%

profile of v7, /device:TPU:1, one launch (start us, length us, event | category | flops | bytes accessed | tf_op | source)
XLA Modules:
  0.0 72.0 jit_solution(13627115605571075117)
XLA Ops:
  0.0 1.0 %pad_maximum_fusion.both_ref = f32[6,4,8,256]{3,2,1,0:T(8,128)S(1)} fusion(f32[3,4,8,256]{3,2,1,0:T(8,128)} %param.2, f32[3,4,8,256]{3,2,1,0:T(8,128)} %param.3), kind=kLoop, calls=%fused_computation | loop fusion | flops 49152 | bytes 393216 | tf_op jit(solution)/shard_map/concatenate | solution.py:430
  1.0 4.5 %collective-permute-start = (f32[3,4,8,256]{3,2,1,0:T(8,128)S(1)}, f32[3,4,8,256]{3,2,1,0:T(8,128)S(1)}, u32[]{:S(2)}, u32[]{:S(2)}) collective-permute-start(f32[3,4,8,256]{3,2,1,0:T(8,128)S(1)} %get-tuple-element.24), channel_id=1, source_target_pairs={{0,63},{1,2},{2,1},{3,4},{4,3},{5,6},{6,5},{7,8},{8,7},{9,10},{10,... | collective-permute-start | bytes 294920 | tf_op jit(solution)/shard_map/ppermute | solution.py:418
  5.5 13.5 %collective-permute-start.1 = (f32[3,4,8,256]{3,2,1,0:T(8,128)S(1)}, f32[3,4,8,256]{3,2,1,0:T(8,128)S(1)}, u32[]{:S(2)}, u32[]{:S(2)}) collective-permute-start(f32[3,4,8,256]{3,2,1,0:T(8,128)S(1)} %get-tuple-element.25), channel_id=1, source_target_pairs={{0,1},{1,0},{2,3},{3,2},{4,5},{5,4},{6,7},{7,6},{8,9},{9,8},{10,11... | collective-permute-start | bytes 294920 | tf_op jit(solution)/shard_map/ppermute | solution.py:422
  19.0 0.0 collective-permute-done.cross_ref
  19.0 0.9 %collective-permute-done.1.core_ref = f32[3,4,8,256]{3,2,1,0:T(8,128)S(1)} collective-permute-done((f32[3,4,8,256]{3,2,1,0:T(8,128)S(1)}, f32[3,4,8,256]{3,2,1,0:T(8,128)S(1)}, u32[]{:S(2)}, u32[]{:S(2)}) %collective-permute-start.1) | collective-permute-done | bytes 98336 | tf_op jit(solution)/shard_map/ppermute | solution.py:422
  19.9 0.1 shard_map.29
  20.0 11.3 %collective-permute-start.2 = (f32[6,8,256]{2,1,0:T(8,128)S(1)}, f32[6,8,256]{2,1,0:T(8,128)S(1)}, u32[]{:S(2)}, u32[]{:S(2)}) collective-permute-start(f32[6,8,256]{2,1,0:T(8,128)S(1)} %get-tuple-element.28), channel_id=1, source_target_pairs={{0,960},{64,128},{128,64},{192,256},{256,192},{320,384},{384,320},... | collective-permute-start | bytes 147464 | tf_op jit(solution)/shard_map/ppermute | solution.py:418
  31.3 1.9 %collective-permute-start.3 = (f32[6,8,256]{2,1,0:T(8,128)S(1)}, f32[6,8,256]{2,1,0:T(8,128)S(1)}, u32[]{:S(2)}, u32[]{:S(2)}) collective-permute-start(f32[6,8,256]{2,1,0:T(8,128)S(1)} %get-tuple-element.29), channel_id=1, source_target_pairs={{0,64},{64,0},{128,192},{192,128},{256,320},{320,256},{384,448},{4... | collective-permute-start | bytes 147464 | tf_op jit(solution)/shard_map/ppermute | solution.py:422
  33.3 0.0 collective-permute-done.2.first_ref
  33.3 2.9 %collective-permute-done.3.second_ref = f32[6,8,256]{2,1,0:T(8,128)S(1)} collective-permute-done((f32[6,8,256]{2,1,0:T(8,128)S(1)}, f32[6,8,256]{2,1,0:T(8,128)S(1)}, u32[]{:S(2)}, u32[]{:S(2)}) %collective-permute-start.3) | collective-permute-done | bytes 49184 | tf_op jit(solution)/shard_map/ppermute | solution.py:422
  36.2 1.0 %shard_map.30 = (f32[64,1,128]{2,1,0:T(1,128)}, f32[8,16,256]{2,1,0:T(8,128)S(1)}, f32[6,16,256]{2,1,0:T(8,128)S(1)}, f32[14,8,256]{2,1,0:T(8,128)S(1)}, f32[14,8,256]{2,1,0:T(8,128)S(1)}) custom-call(s32[1]{0:T(128)} %bitcast.place_ref, f32[3,4,8,256]{3,2,1,0:T(8,128)S(1)} %get-tuple-element.22.cot_ref, f32[3,4,8,256]{3,2,1,0:T(8,128)S(1)} %get-tuple-element.23.vel_ref, ...), custom_call_target="tpu_custom_call" | custom-call | tf_op jit(solution)/shard_map/pallas_call | solution.py:397
  37.2 8.3 %all-to-all-start = ((f32[64,1,128]{2,1,0:T(1,128)}), f32[64,1,128]{2,1,0:T(1,128)S(1)}, u32[]{:S(2)}, u32[]{:S(2)}) async-start(f32[64,1,128]{2,1,0:T(1,128)} %get-tuple-element.34.lines_ref), calls=%async_computation | async-start | bytes 65536 | tf_op jit(solution)/shard_map/all_to_all | solution.py:445
  45.4 2.6 %collective-permute-start.4 = (f32[14,8,256]{2,1,0:T(8,128)S(1)}, f32[14,8,256]{2,1,0:T(8,128)S(1)}, u32[]{:S(2)}, u32[]{:S(2)}) collective-permute-start(f32[14,8,256]{2,1,0:T(8,128)S(1)} %get-tuple-element.30), channel_id=1, source_target_pairs={{0,960},{64,128},{128,64},{192,256},{256,192},{320,384},{384,320},... | collective-permute-start | bytes 344072 | tf_op jit(solution)/shard_map/ppermute | solution.py:418
  48.0 1.9 %collective-permute-start.5 = (f32[14,8,256]{2,1,0:T(8,128)S(1)}, f32[14,8,256]{2,1,0:T(8,128)S(1)}, u32[]{:S(2)}, u32[]{:S(2)}) collective-permute-start(f32[14,8,256]{2,1,0:T(8,128)S(1)} %get-tuple-element.31), channel_id=1, source_target_pairs={{0,64},{64,0},{128,192},{192,128},{256,320},{320,256},{384,448},{4... | collective-permute-start | bytes 344072 | tf_op jit(solution)/shard_map/ppermute | solution.py:422
  50.0 6.2 %all-to-all-done.got_ref = f32[64,1,128]{2,1,0:T(1,128)S(1)} async-done(((f32[64,1,128]{2,1,0:T(1,128)}), f32[64,1,128]{2,1,0:T(1,128)S(1)}, u32[]{:S(2)}, u32[]{:S(2)}) %all-to-all-start) | async-done | bytes 32800 | tf_op jit(solution)/shard_map/all_to_all | solution.py:445
  56.2 0.8 %shard_map.33 = f32[16,1,128]{2,1,0:T(1,128)} custom-call(f32[64,1,128]{2,1,0:T(1,128)S(1)} %all-to-all-done.got_ref), custom_call_target="tpu_custom_call" | custom-call | tf_op jit(solution)/shard_map/pallas_call | solution.py:397
  57.0 6.8 %all-to-all-start.1 = ((f32[16,1,128]{2,1,0:T(1,128)}), f32[16,1,128]{2,1,0:T(1,128)S(1)}, u32[]{:S(2)}, u32[]{:S(2)}) async-start(f32[16,1,128]{2,1,0:T(1,128)} %shard_map.33), calls=%async_computation.1 | async-start | bytes 16384 | tf_op jit(solution)/shard_map/all_to_all | solution.py:450
  63.7 0.9 %shard_map.31 = (f32[2,9,16,256]{3,2,1,0:T(8,128)S(1)}, f32[2,16,256]{2,1,0:T(8,128)S(1)}) custom-call(f32[3,4,8,256]{3,2,1,0:T(8,128)S(1)} %get-tuple-element.22.cot_ref, f32[3,4,8,256]{3,2,1,0:T(8,128)S(1)} %get-tuple-element.23.vel_ref, f32[3,4,8,256]{3,2,1,0:T(8,128)S(1)} %get-tuple-element.26.zn_ref, f32[3,4,8,256]{3,2,1,0:T(8,128)S(1)} %get-tuple-element.27.zp_ref, ...), custom_call_target="tpu_custom_call" | custom-call | flops 4000000000 | bytes 2000000 | tf_op jit(solution)/shard_map/pallas_call | solution.py:397
  64.6 0.0 collective-permute-done.4.late1_ref
  64.6 0.0 collective-permute-done.5.late2_ref
  64.6 0.2 shard_map.32
  64.8 5.9 %all-to-all-done.1.sums_ref = f32[16,1,128]{2,1,0:T(1,128)S(1)} async-done(((f32[16,1,128]{2,1,0:T(1,128)}), f32[16,1,128]{2,1,0:T(1,128)S(1)}, u32[]{:S(2)}, u32[]{:S(2)}) %all-to-all-start.1) | async-done | bytes 8224 | tf_op jit(solution)/shard_map/all_to_all | solution.py:450
  70.8 1.3 %shard_map.34 = f32[3,4,8,256]{3,2,1,0:T(8,128)} custom-call(s32[1]{0:T(128)} %bitcast.place_ref, f32[3,4,8,256]{3,2,1,0:T(8,128)S(1)} %get-tuple-element.22.cot_ref, f32[3,4,8,256]{3,2,1,0:T(8,128)S(1)} %get-tuple-element.23.vel_ref, f32[3,4,8,256]{3,2,1,0:T(8,128)S(1)} %get-tuple-element.26.zn_ref, f32[3,4,8,256]{3,2,1,0:T(8,128)S(1)} %get-tuple-element.27.zp_ref, ...), custom_call_target="tpu_custom_call" | custom-call | tf_op jit(solution)/shard_map/pallas_call | solution.py:397
  (1 shorter events, 0.0 us)
Async XLA Ops:
  1.0 18.0 %collective-permute-start = (f32[3,4,8,256]{3,2,1,0:T(8,128)S(1)}, f32[3,4,8,256]{3,2,1,0:T(8,128)S(1)}, u32[]{:S(2)}, u32[]{:S(2)}) collective-permute-start(f32[3,4,8,256]{3,2,1,0:T(8,128)S(1)} %get-tuple-element.24), channel_id=1, source_target_pairs={{0,63},{1,2},{2,1},{3,4},{4,3},{5,6},{6,5},{7,8},{8,7},{9,10},{10,... | collective-permute-start | bytes 294920 | tf_op jit(solution)/shard_map/ppermute | solution.py:418
  5.5 14.4 %collective-permute-start.1 = (f32[3,4,8,256]{3,2,1,0:T(8,128)S(1)}, f32[3,4,8,256]{3,2,1,0:T(8,128)S(1)}, u32[]{:S(2)}, u32[]{:S(2)}) collective-permute-start(f32[3,4,8,256]{3,2,1,0:T(8,128)S(1)} %get-tuple-element.25), channel_id=1, source_target_pairs={{0,1},{1,0},{2,3},{3,2},{4,5},{5,4},{6,7},{7,6},{8,9},{9,8},{10,11... | collective-permute-start | bytes 294920 | tf_op jit(solution)/shard_map/ppermute | solution.py:422
  20.0 13.2 %collective-permute-start.2 = (f32[6,8,256]{2,1,0:T(8,128)S(1)}, f32[6,8,256]{2,1,0:T(8,128)S(1)}, u32[]{:S(2)}, u32[]{:S(2)}) collective-permute-start(f32[6,8,256]{2,1,0:T(8,128)S(1)} %get-tuple-element.28), channel_id=1, source_target_pairs={{0,960},{64,128},{128,64},{192,256},{256,192},{320,384},{384,320},... | collective-permute-start | bytes 147464 | tf_op jit(solution)/shard_map/ppermute | solution.py:418
  31.3 4.8 %collective-permute-start.3 = (f32[6,8,256]{2,1,0:T(8,128)S(1)}, f32[6,8,256]{2,1,0:T(8,128)S(1)}, u32[]{:S(2)}, u32[]{:S(2)}) collective-permute-start(f32[6,8,256]{2,1,0:T(8,128)S(1)} %get-tuple-element.29), channel_id=1, source_target_pairs={{0,64},{64,0},{128,192},{192,128},{256,320},{320,256},{384,448},{4... | collective-permute-start | bytes 147464 | tf_op jit(solution)/shard_map/ppermute | solution.py:422
  37.2 19.0 %all-to-all-start = ((f32[64,1,128]{2,1,0:T(1,128)}), f32[64,1,128]{2,1,0:T(1,128)S(1)}, u32[]{:S(2)}, u32[]{:S(2)}) async-start(f32[64,1,128]{2,1,0:T(1,128)} %get-tuple-element.34.lines_ref), calls=%async_computation | async-start | bytes 65536 | tf_op jit(solution)/shard_map/all_to_all | solution.py:445
  45.4 19.2 %collective-permute-start.4 = (f32[14,8,256]{2,1,0:T(8,128)S(1)}, f32[14,8,256]{2,1,0:T(8,128)S(1)}, u32[]{:S(2)}, u32[]{:S(2)}) collective-permute-start(f32[14,8,256]{2,1,0:T(8,128)S(1)} %get-tuple-element.30), channel_id=1, source_target_pairs={{0,960},{64,128},{128,64},{192,256},{256,192},{320,384},{384,320},... | collective-permute-start | bytes 344072 | tf_op jit(solution)/shard_map/ppermute | solution.py:418
  48.0 16.6 %collective-permute-start.5 = (f32[14,8,256]{2,1,0:T(8,128)S(1)}, f32[14,8,256]{2,1,0:T(8,128)S(1)}, u32[]{:S(2)}, u32[]{:S(2)}) collective-permute-start(f32[14,8,256]{2,1,0:T(8,128)S(1)} %get-tuple-element.31), channel_id=1, source_target_pairs={{0,64},{64,0},{128,192},{192,128},{256,320},{320,256},{384,448},{4... | collective-permute-start | bytes 344072 | tf_op jit(solution)/shard_map/ppermute | solution.py:422
  57.0 13.8 %all-to-all-start.1 = ((f32[16,1,128]{2,1,0:T(1,128)}), f32[16,1,128]{2,1,0:T(1,128)S(1)}, u32[]{:S(2)}, u32[]{:S(2)}) async-start(f32[16,1,128]{2,1,0:T(1,128)} %shard_map.33), calls=%async_computation.1 | async-start | bytes 16384 | tf_op jit(solution)/shard_map/all_to_all | solution.py:450

commit v8 on v6

--- a/solution.py
+++ b/solution.py
@@ -408,6 +408,15 @@
 STEPS = (("z", "core"), ("y_high", "y_low", "x"))
 
 
+def to_all(rows, axes):
+    sizes = [lax.axis_size(axis) for axis in axes]
+    order = [0]
+    for n in sizes:
+        middle = n // 2 if n > 2 else 0
+        order = [i * n + (k + middle) % n for i in order for k in range(n)]
+    return lax.all_to_all(rows, axes, 0, 0, axis_index_groups=[order])
+
+
 def size(axes):
     return math.prod(lax.axis_size(axis) for axis in axes)
 
@@ -441,11 +450,11 @@
         [place],
         held,
     )
-    got = lax.all_to_all(lines, STEPS[0], 0, 0)
+    got = to_all(lines, STEPS[0])
     lines, late1, late2 = call(
         merge, [(size(STEPS[1]), 1, 128), later, later], [place], [got] + held[:4] + [b]
     )
-    sums = lax.all_to_all(lines, STEPS[1], 0, 0)
+    sums = to_all(lines, STEPS[1])
     late = [swap_across(late1, PY), swap_within(late2, PY)]
     inner = call(inner_slopes, [(2, 9, WIDE, 256), (2, WIDE, 256)], [], held[:4] + [lines], 4_000_000_000)
     outer = call(outer_slopes, [(4, 9, WIDE, 256), (4, WIDE, 256)], [place], held[:4] + late, 4_000_000)

time: 69.6 us -> 73 us (1.049); the launches traced: 69.2 us -> 71.7 us
  starting transfers between devices: 44.6 us -> 50 us
  waiting for transfers between devices: 8.63 us -> 6.52 us
    all_to_all x1, starting transfers between devices: 8.56 us -> 12.5 us  [to_all(): return lax.all_to_all(rows, axes, 0, 0, axis_index_groups=[order])]
    ppermute x3, waiting for transfers between devices: 2.33 us -> 0.46 us  [swap_across(): lax.ppermute(x, axes, [(i, (i + 1 if i % 2 else i - 1) % n) for i in rang...]
    all_to_all x1, waiting for transfers between devices: 1.82 us -> 0.01 us  [to_all(): return lax.all_to_all(rows, axes, 0, 0, axis_index_groups=[order])]
    ppermute x3, waiting for transfers between devices: 4.48 us -> 6.05 us  [swap_within(): return lax.ppermute(x, axes, [(i, i ^ 1) for i in range(size(axes))])]
    ppermute x3, starting transfers between devices: 18.7 us -> 20.1 us  [swap_across(): lax.ppermute(x, axes, [(i, (i + 1 if i % 2 else i - 1) % n) for i in rang...]
    all_to_all x1, blocking collectives: 11.2 us -> 10.5 us  [to_all(): return lax.all_to_all(rows, axes, 0, 0, axis_index_groups=[order])]
  transfers between devices with their start and end apart: 7 -> 7, of which waited for: 5 -> 4; matrix products, arithmetic and copies ran while one was open for 0% -> 0% of each run, Pallas kernels for 2% -> 2%
where the time goes in v8:
time: 73 us; the launch traced here: 71.7 us
  starting transfers between devices  50 us (68%)
  blocking collectives  10.5 us (14%)
  waiting for transfers between devices  6.52 us (9%)
  Pallas kernels  3.68 us (5%)
  other arithmetic  0.95 us (1%)
    ppermute x3, starting transfers between devices, swap_across(): lax.ppermute(x, axes, [(i, (i + 1 if i % 2 else i - 1) % n) for i in rang...  20.1 us
    ppermute x3, starting transfers between devices, swap_within(): return lax.ppermute(x, axes, [(i, i ^ 1) for i in range(size(axes))])  17.3 us
    all_to_all x1, starting transfers between devices, to_all(): return lax.all_to_all(rows, axes, 0, 0, axis_index_groups=[order])  12.5 us
    all_to_all x1, blocking collectives, to_all(): return lax.all_to_all(rows, axes, 0, 0, axis_index_groups=[order])  10.5 us
    ppermute x3, waiting for transfers between devices, swap_within(): return lax.ppermute(x, axes, [(i, i ^ 1) for i in range(size(axes))])  6.05 us
    pallas_call x7, Pallas kernels, call(): pl.pallas_call(kernel, out_shape=[jax.ShapeDtypeStruct(s, jnp.float32) fo...  3.68 us
  transfers between devices with their start and end apart: 7, of which 4 were waited for; matrix products, arithmetic and copies ran while one was open for 0% of the time, Pallas kernels for 2%

profile of v8, /device:TPU:1, one launch (start us, length us, event | category | flops | bytes accessed | tf_op | source)
XLA Modules:
  0.0 71.7 jit_solution(15898829664122249656)
XLA Ops:
  0.0 1.0 %pad_maximum_fusion.both_ref = f32[6,4,8,256]{3,2,1,0:T(8,128)S(1)} fusion(f32[3,4,8,256]{3,2,1,0:T(8,128)} %param.2, f32[3,4,8,256]{3,2,1,0:T(8,128)} %param.3), kind=kLoop, calls=%fused_computation | loop fusion | flops 49152 | bytes 393216 | tf_op jit(solution)/shard_map/concatenate | solution.py:438
  1.0 4.5 %collective-permute-start = (f32[3,4,8,256]{3,2,1,0:T(8,128)S(1)}, f32[3,4,8,256]{3,2,1,0:T(8,128)S(1)}, u32[]{:S(2)}, u32[]{:S(2)}) collective-permute-start(f32[3,4,8,256]{3,2,1,0:T(8,128)S(1)} %get-tuple-element.25), channel_id=1, source_target_pairs={{0,63},{1,2},{2,1},{3,4},{4,3},{5,6},{6,5},{7,8},{8,7},{9,10},{10,... | collective-permute-start | bytes 294920 | tf_op jit(solution)/shard_map/ppermute | solution.py:426
  5.5 13.5 %collective-permute-start.1 = (f32[3,4,8,256]{3,2,1,0:T(8,128)S(1)}, f32[3,4,8,256]{3,2,1,0:T(8,128)S(1)}, u32[]{:S(2)}, u32[]{:S(2)}) collective-permute-start(f32[3,4,8,256]{3,2,1,0:T(8,128)S(1)} %get-tuple-element.26), channel_id=1, source_target_pairs={{0,1},{1,0},{2,3},{3,2},{4,5},{5,4},{6,7},{7,6},{8,9},{9,8},{10,11... | collective-permute-start | bytes 294920 | tf_op jit(solution)/shard_map/ppermute | solution.py:430
  19.0 0.0 collective-permute-done.cross_ref
  19.0 0.9 %collective-permute-done.1.core_ref = f32[3,4,8,256]{3,2,1,0:T(8,128)S(1)} collective-permute-done((f32[3,4,8,256]{3,2,1,0:T(8,128)S(1)}, f32[3,4,8,256]{3,2,1,0:T(8,128)S(1)}, u32[]{:S(2)}, u32[]{:S(2)}) %collective-permute-start.1) | collective-permute-done | bytes 98336 | tf_op jit(solution)/shard_map/ppermute | solution.py:430
  19.9 0.1 shard_map.29
  20.0 11.3 %collective-permute-start.2 = (f32[6,8,256]{2,1,0:T(8,128)S(1)}, f32[6,8,256]{2,1,0:T(8,128)S(1)}, u32[]{:S(2)}, u32[]{:S(2)}) collective-permute-start(f32[6,8,256]{2,1,0:T(8,128)S(1)} %get-tuple-element.29), channel_id=1, source_target_pairs={{0,960},{64,128},{128,64},{192,256},{256,192},{320,384},{384,320},... | collective-permute-start | bytes 147464 | tf_op jit(solution)/shard_map/ppermute | solution.py:426
  31.3 1.9 %collective-permute-start.3 = (f32[6,8,256]{2,1,0:T(8,128)S(1)}, f32[6,8,256]{2,1,0:T(8,128)S(1)}, u32[]{:S(2)}, u32[]{:S(2)}) collective-permute-start(f32[6,8,256]{2,1,0:T(8,128)S(1)} %get-tuple-element.30), channel_id=1, source_target_pairs={{0,64},{64,0},{128,192},{192,128},{256,320},{320,256},{384,448},{4... | collective-permute-start | bytes 147464 | tf_op jit(solution)/shard_map/ppermute | solution.py:430
  33.3 0.0 collective-permute-done.2.first_ref
  33.3 2.9 %collective-permute-done.3.second_ref = f32[6,8,256]{2,1,0:T(8,128)S(1)} collective-permute-done((f32[6,8,256]{2,1,0:T(8,128)S(1)}, f32[6,8,256]{2,1,0:T(8,128)S(1)}, u32[]{:S(2)}, u32[]{:S(2)}) %collective-permute-start.3) | collective-permute-done | bytes 49184 | tf_op jit(solution)/shard_map/ppermute | solution.py:430
  36.2 0.4 shard_map.30
  36.5 10.5 %all_to_all.10.got_ref = f32[16,1,128]{2,1,0:T(1,128)S(1)} all-to-all(f32[16,1,128]{2,1,0:T(1,128)S(1)} %get-tuple-element.31), channel_id=1, replica_groups={{256,257,320,321,384,385,448,449,0,1,64,65,128,129,192,193},{258,259,32..., dimensions={0} | all-to-all | bytes 16384 | tf_op jit(solution)/shard_map/all_to_all | solution.py:417
  47.0 0.8 %shard_map.31 = (f32[64,1,128]{2,1,0:T(1,128)}, f32[14,8,256]{2,1,0:T(8,128)S(1)}, f32[14,8,256]{2,1,0:T(8,128)S(1)}) custom-call(s32[1]{0:T(128)} %bitcast.place_ref, f32[16,1,128]{2,1,0:T(1,128)S(1)} %all_to_all.10.got_ref, f32[3,4,8,256]{3,2,1,0:T(8,128)S(1)} %get-tuple-element.23.cot_ref, f32[3,4,8,256]{3,2,1,0:T(8,128)S(1)} %get-tuple-element.24.vel_ref, ...), custom_call_target="tpu_custom_call" | custom-call | tf_op jit(solution)/shard_map/pallas_call | solution.py:396
  47.8 12.5 %all-to-all-start.1 = ((f32[64,1,128]{2,1,0:T(1,128)}), f32[64,1,128]{2,1,0:T(1,128)S(1)}, u32[]{:S(2)}, u32[]{:S(2)}) async-start(f32[64,1,128]{2,1,0:T(1,128)} %get-tuple-element.36.lines_ref), calls=%async_computation.1 | async-start | bytes 65536 | tf_op jit(solution)/shard_map/all_to_all | solution.py:417
  60.3 4.4 %collective-permute-start.4 = (f32[14,8,256]{2,1,0:T(8,128)S(1)}, f32[14,8,256]{2,1,0:T(8,128)S(1)}, u32[]{:S(2)}, u32[]{:S(2)}) collective-permute-start(f32[14,8,256]{2,1,0:T(8,128)S(1)} %get-tuple-element.33), channel_id=1, source_target_pairs={{0,960},{64,128},{128,64},{192,256},{256,192},{320,384},{384,320},... | collective-permute-start | bytes 344072 | tf_op jit(solution)/shard_map/ppermute | solution.py:426
  64.7 1.9 %collective-permute-start.5 = (f32[14,8,256]{2,1,0:T(8,128)S(1)}, f32[14,8,256]{2,1,0:T(8,128)S(1)}, u32[]{:S(2)}, u32[]{:S(2)}) collective-permute-start(f32[14,8,256]{2,1,0:T(8,128)S(1)} %get-tuple-element.34), channel_id=1, source_target_pairs={{0,64},{64,0},{128,192},{192,128},{256,320},{320,256},{384,448},{4... | collective-permute-start | bytes 344072 | tf_op jit(solution)/shard_map/ppermute | solution.py:430
  66.6 0.9 %shard_map.32 = (f32[2,9,16,256]{3,2,1,0:T(8,128)S(1)}, f32[2,16,256]{2,1,0:T(8,128)S(1)}) custom-call(f32[3,4,8,256]{3,2,1,0:T(8,128)S(1)} %get-tuple-element.23.cot_ref, f32[3,4,8,256]{3,2,1,0:T(8,128)S(1)} %get-tuple-element.24.vel_ref, f32[3,4,8,256]{3,2,1,0:T(8,128)S(1)} %get-tuple-element.27.zn_ref, f32[3,4,8,256]{3,2,1,0:T(8,128)S(1)} %get-tuple-element.28.zp_ref, ...), custom_call_target="tpu_custom_call" | custom-call | flops 4000000000 | bytes 2000000 | tf_op jit(solution)/shard_map/pallas_call | solution.py:396
  67.5 0.5 collective-permute-done.4.late1_ref
  68.0 2.3 %collective-permute-done.5.late2_ref = f32[14,8,256]{2,1,0:T(8,128)S(1)} collective-permute-done((f32[14,8,256]{2,1,0:T(8,128)S(1)}, f32[14,8,256]{2,1,0:T(8,128)S(1)}, u32[]{:S(2)}, u32[]{:S(2)}) %collective-permute-start.5) | collective-permute-done | bytes 114720 | tf_op jit(solution)/shard_map/ppermute | solution.py:430
  70.2 0.2 shard_map.33
  70.4 0.0 all-to-all-done.1.sums_ref
  70.4 1.3 %shard_map.34 = f32[3,4,8,256]{3,2,1,0:T(8,128)} custom-call(s32[1]{0:T(128)} %bitcast.place_ref, f32[3,4,8,256]{3,2,1,0:T(8,128)S(1)} %get-tuple-element.23.cot_ref, f32[3,4,8,256]{3,2,1,0:T(8,128)S(1)} %get-tuple-element.24.vel_ref, f32[3,4,8,256]{3,2,1,0:T(8,128)S(1)} %get-tuple-element.27.zn_ref, f32[3,4,8,256]{3,2,1,0:T(8,128)S(1)} %get-tuple-element.28.zp_ref, ...), custom_call_target="tpu_custom_call" | custom-call | tf_op jit(solution)/shard_map/pallas_call | solution.py:396
  (1 shorter events, 0.0 us)
Async XLA Ops:
  1.0 18.0 %collective-permute-start = (f32[3,4,8,256]{3,2,1,0:T(8,128)S(1)}, f32[3,4,8,256]{3,2,1,0:T(8,128)S(1)}, u32[]{:S(2)}, u32[]{:S(2)}) collective-permute-start(f32[3,4,8,256]{3,2,1,0:T(8,128)S(1)} %get-tuple-element.25), channel_id=1, source_target_pairs={{0,63},{1,2},{2,1},{3,4},{4,3},{5,6},{6,5},{7,8},{8,7},{9,10},{10,... | collective-permute-start | bytes 294920 | tf_op jit(solution)/shard_map/ppermute | solution.py:426
  5.5 14.4 %collective-permute-start.1 = (f32[3,4,8,256]{3,2,1,0:T(8,128)S(1)}, f32[3,4,8,256]{3,2,1,0:T(8,128)S(1)}, u32[]{:S(2)}, u32[]{:S(2)}) collective-permute-start(f32[3,4,8,256]{3,2,1,0:T(8,128)S(1)} %get-tuple-element.26), channel_id=1, source_target_pairs={{0,1},{1,0},{2,3},{3,2},{4,5},{5,4},{6,7},{7,6},{8,9},{9,8},{10,11... | collective-permute-start | bytes 294920 | tf_op jit(solution)/shard_map/ppermute | solution.py:430
  20.0 13.2 %collective-permute-start.2 = (f32[6,8,256]{2,1,0:T(8,128)S(1)}, f32[6,8,256]{2,1,0:T(8,128)S(1)}, u32[]{:S(2)}, u32[]{:S(2)}) collective-permute-start(f32[6,8,256]{2,1,0:T(8,128)S(1)} %get-tuple-element.29), channel_id=1, source_target_pairs={{0,960},{64,128},{128,64},{192,256},{256,192},{320,384},{384,320},... | collective-permute-start | bytes 147464 | tf_op jit(solution)/shard_map/ppermute | solution.py:426
  31.3 4.8 %collective-permute-start.3 = (f32[6,8,256]{2,1,0:T(8,128)S(1)}, f32[6,8,256]{2,1,0:T(8,128)S(1)}, u32[]{:S(2)}, u32[]{:S(2)}) collective-permute-start(f32[6,8,256]{2,1,0:T(8,128)S(1)} %get-tuple-element.30), channel_id=1, source_target_pairs={{0,64},{64,0},{128,192},{192,128},{256,320},{320,256},{384,448},{4... | collective-permute-start | bytes 147464 | tf_op jit(solution)/shard_map/ppermute | solution.py:430
  47.8 22.6 %all-to-all-start.1 = ((f32[64,1,128]{2,1,0:T(1,128)}), f32[64,1,128]{2,1,0:T(1,128)S(1)}, u32[]{:S(2)}, u32[]{:S(2)}) async-start(f32[64,1,128]{2,1,0:T(1,128)} %get-tuple-element.36.lines_ref), calls=%async_computation.1 | async-start | bytes 65536 | tf_op jit(solution)/shard_map/all_to_all | solution.py:417
  60.3 7.6 %collective-permute-start.4 = (f32[14,8,256]{2,1,0:T(8,128)S(1)}, f32[14,8,256]{2,1,0:T(8,128)S(1)}, u32[]{:S(2)}, u32[]{:S(2)}) collective-permute-start(f32[14,8,256]{2,1,0:T(8,128)S(1)} %get-tuple-element.33), channel_id=1, source_target_pairs={{0,960},{64,128},{128,64},{192,256},{256,192},{320,384},{384,320},... | collective-permute-start | bytes 344072 | tf_op jit(solution)/shard_map/ppermute | solution.py:426
  64.7 5.5 %collective-permute-start.5 = (f32[14,8,256]{2,1,0:T(8,128)S(1)}, f32[14,8,256]{2,1,0:T(8,128)S(1)}, u32[]{:S(2)}, u32[]{:S(2)}) collective-permute-start(f32[14,8,256]{2,1,0:T(8,128)S(1)} %get-tuple-element.34), channel_id=1, source_target_pairs={{0,64},{64,0},{128,192},{192,128},{256,320},{320,256},{384,448},{4... | collective-permute-start | bytes 344072 | tf_op jit(solution)/shard_map/ppermute | solution.py:430

commit v9 on v7

--- a/solution.py
+++ b/solution.py
@@ -406,7 +406,16 @@
 
 PY = ("y_low", "z")
 PZ = ("y_high", "x", "core")
-STEPS = (("y_high", "y_low", "x"), ("z", "core"))
+STEPS = (("z", "core"), ("y_high", "y_low", "x"))
+
+
+def to_all(rows, axes):
+    sizes = [lax.axis_size(axis) for axis in axes]
+    order = [0]
+    for n in sizes:
+        middle = n // 2 if n > 2 else 0
+        order = [i * n + (k + middle) % n for i in order for k in range(n)]
+    return lax.all_to_all(rows, axes, 0, 0, axis_index_groups=[order])
 
 
 def size(axes):
@@ -442,12 +451,12 @@
         [place],
         held,
     )
-    got = lax.all_to_all(lines, STEPS[0], 0, 0)
+    got = to_all(lines, STEPS[0])
     late = [swap_across(late1, PY), swap_within(late2, PY)]
     inner = call(inner_slopes, [(2, 9, WIDE, 256), (2, WIDE, 256)], [], held[:4] + [lines], 4_000_000_000)
     outer = call(outer_slopes, [(4, 9, WIDE, 256), (4, WIDE, 256)], [place], held[:4] + late, 4_000_000)
     (lines,) = call(merge, [(size(STEPS[1]), 1, 128)], [], [got])
-    sums = lax.all_to_all(lines, STEPS[1], 0, 0)
+    sums = to_all(lines, STEPS[1])
     (out,) = call(finish, [block], [place], held + late + [b, w, *inner, *outer, sums])
     return out
 

time: 72.5 us -> 67.5 us (0.931); the launches traced: 72 us -> 66.2 us
  waiting for transfers between devices: 16 us -> 4.21 us
  starting transfers between devices: 50.7 us -> 56.7 us
    all_to_all x2, waiting for transfers between devices: 12.2 us -> 0.4 us  [to_all(): return lax.all_to_all(rows, axes, 0, 0, axis_index_groups=[order])]
    all_to_all x2, starting transfers between devices: 15 us -> 20.8 us  [to_all(): return lax.all_to_all(rows, axes, 0, 0, axis_index_groups=[order])]
  transfers between devices with their start and end apart: 8 -> 8, of which waited for: 4 -> 3; matrix products, arithmetic and copies ran while one was open for 0% -> 0% of each run, Pallas kernels for 3% -> 3%
where the time goes in v9:
time: 67.5 us; the launch traced here: 66.2 us
  starting transfers between devices  56.7 us (84%)
  waiting for transfers between devices  4.21 us (6%)
  Pallas kernels  4.2 us (6%)
  other arithmetic  0.95 us (1%)
    all_to_all x2, starting transfers between devices, to_all(): return lax.all_to_all(rows, axes, 0, 0, axis_index_groups=[order])  20.8 us
    ppermute x3, starting transfers between devices, swap_across(): lax.ppermute(x, axes, [(i, (i + 1 if i % 2 else i - 1) % n) for i in rang...  18.6 us
    ppermute x3, starting transfers between devices, swap_within(): return lax.ppermute(x, axes, [(i, i ^ 1) for i in range(size(axes))])  17.3 us
    pallas_call x7, Pallas kernels, call(): pl.pallas_call(kernel, out_shape=[jax.ShapeDtypeStruct(s, jnp.float32) fo...  4.2 us
    ppermute x3, waiting for transfers between devices, swap_within(): return lax.ppermute(x, axes, [(i, i ^ 1) for i in range(size(axes))])  3.8 us
  transfers between devices with their start and end apart: 8, of which 3 were waited for; matrix products, arithmetic and copies ran while one was open for 0% of the time, Pallas kernels for 3%

profile of v9, /device:TPU:1, one launch (start us, length us, event | category | flops | bytes accessed | tf_op | source)
XLA Modules:
  0.0 66.2 jit_solution(12565605677425566413)
XLA Ops:
  0.0 1.0 %pad_maximum_fusion.both_ref = f32[6,4,8,256]{3,2,1,0:T(8,128)S(1)} fusion(f32[3,4,8,256]{3,2,1,0:T(8,128)} %param.2, f32[3,4,8,256]{3,2,1,0:T(8,128)} %param.3), kind=kLoop, calls=%fused_computation | loop fusion | flops 49152 | bytes 393216 | tf_op jit(solution)/shard_map/concatenate | solution.py:439
  1.0 4.5 %collective-permute-start = (f32[3,4,8,256]{3,2,1,0:T(8,128)S(1)}, f32[3,4,8,256]{3,2,1,0:T(8,128)S(1)}, u32[]{:S(2)}, u32[]{:S(2)}) collective-permute-start(f32[3,4,8,256]{3,2,1,0:T(8,128)S(1)} %get-tuple-element.24), channel_id=1, source_target_pairs={{0,63},{1,2},{2,1},{3,4},{4,3},{5,6},{6,5},{7,8},{8,7},{9,10},{10,... | collective-permute-start | bytes 294920 | tf_op jit(solution)/shard_map/ppermute | solution.py:427
  5.5 13.5 %collective-permute-start.1 = (f32[3,4,8,256]{3,2,1,0:T(8,128)S(1)}, f32[3,4,8,256]{3,2,1,0:T(8,128)S(1)}, u32[]{:S(2)}, u32[]{:S(2)}) collective-permute-start(f32[3,4,8,256]{3,2,1,0:T(8,128)S(1)} %get-tuple-element.25), channel_id=1, source_target_pairs={{0,1},{1,0},{2,3},{3,2},{4,5},{5,4},{6,7},{7,6},{8,9},{9,8},{10,11... | collective-permute-start | bytes 294920 | tf_op jit(solution)/shard_map/ppermute | solution.py:431
  19.0 0.0 collective-permute-done.cross_ref
  19.0 0.9 %collective-permute-done.1.core_ref = f32[3,4,8,256]{3,2,1,0:T(8,128)S(1)} collective-permute-done((f32[3,4,8,256]{3,2,1,0:T(8,128)S(1)}, f32[3,4,8,256]{3,2,1,0:T(8,128)S(1)}, u32[]{:S(2)}, u32[]{:S(2)}) %collective-permute-start.1) | collective-permute-done | bytes 98336 | tf_op jit(solution)/shard_map/ppermute | solution.py:431
  19.9 0.1 shard_map.29
  20.0 11.3 %collective-permute-start.2 = (f32[6,8,256]{2,1,0:T(8,128)S(1)}, f32[6,8,256]{2,1,0:T(8,128)S(1)}, u32[]{:S(2)}, u32[]{:S(2)}) collective-permute-start(f32[6,8,256]{2,1,0:T(8,128)S(1)} %get-tuple-element.28), channel_id=1, source_target_pairs={{0,960},{64,128},{128,64},{192,256},{256,192},{320,384},{384,320},... | collective-permute-start | bytes 147464 | tf_op jit(solution)/shard_map/ppermute | solution.py:427
  31.3 1.9 %collective-permute-start.3 = (f32[6,8,256]{2,1,0:T(8,128)S(1)}, f32[6,8,256]{2,1,0:T(8,128)S(1)}, u32[]{:S(2)}, u32[]{:S(2)}) collective-permute-start(f32[6,8,256]{2,1,0:T(8,128)S(1)} %get-tuple-element.29), channel_id=1, source_target_pairs={{0,64},{64,0},{128,192},{192,128},{256,320},{320,256},{384,448},{4... | collective-permute-start | bytes 147464 | tf_op jit(solution)/shard_map/ppermute | solution.py:431
  33.3 0.0 collective-permute-done.2.first_ref
  33.3 2.9 %collective-permute-done.3.second_ref = f32[6,8,256]{2,1,0:T(8,128)S(1)} collective-permute-done((f32[6,8,256]{2,1,0:T(8,128)S(1)}, f32[6,8,256]{2,1,0:T(8,128)S(1)}, u32[]{:S(2)}, u32[]{:S(2)}) %collective-permute-start.3) | collective-permute-done | bytes 49184 | tf_op jit(solution)/shard_map/ppermute | solution.py:431
  36.2 1.0 %shard_map.30 = (f32[16,1,128]{2,1,0:T(1,128)}, f32[8,16,256]{2,1,0:T(8,128)S(1)}, f32[6,16,256]{2,1,0:T(8,128)S(1)}, f32[14,8,256]{2,1,0:T(8,128)S(1)}, f32[14,8,256]{2,1,0:T(8,128)S(1)}) custom-call(s32[1]{0:T(128)} %bitcast.place_ref, f32[3,4,8,256]{3,2,1,0:T(8,128)S(1)} %get-tuple-element.22.cot_ref, f32[3,4,8,256]{3,2,1,0:T(8,128)S(1)} %get-tuple-element.23.vel_ref, ...), custom_call_target="tpu_custom_call" | custom-call | tf_op jit(solution)/shard_map/pallas_call | solution.py:397
  37.1 8.7 %all-to-all-start = ((f32[16,1,128]{2,1,0:T(1,128)}), f32[16,1,128]{2,1,0:T(1,128)S(1)}, u32[]{:S(2)}, u32[]{:S(2)}) async-start(f32[16,1,128]{2,1,0:T(1,128)} %get-tuple-element.34.lines_ref), calls=%async_computation | async-start | bytes 16384 | tf_op jit(solution)/shard_map/all_to_all | solution.py:418
  45.8 2.9 %collective-permute-start.4 = (f32[14,8,256]{2,1,0:T(8,128)S(1)}, f32[14,8,256]{2,1,0:T(8,128)S(1)}, u32[]{:S(2)}, u32[]{:S(2)}) collective-permute-start(f32[14,8,256]{2,1,0:T(8,128)S(1)} %get-tuple-element.30), channel_id=1, source_target_pairs={{0,960},{64,128},{128,64},{192,256},{256,192},{320,384},{384,320},... | collective-permute-start | bytes 344072 | tf_op jit(solution)/shard_map/ppermute | solution.py:427
  48.6 1.9 %collective-permute-start.5 = (f32[14,8,256]{2,1,0:T(8,128)S(1)}, f32[14,8,256]{2,1,0:T(8,128)S(1)}, u32[]{:S(2)}, u32[]{:S(2)}) collective-permute-start(f32[14,8,256]{2,1,0:T(8,128)S(1)} %get-tuple-element.31), channel_id=1, source_target_pairs={{0,64},{64,0},{128,192},{192,128},{256,320},{320,256},{384,448},{4... | collective-permute-start | bytes 344072 | tf_op jit(solution)/shard_map/ppermute | solution.py:431
  50.6 0.0 all-to-all-done.got_ref
  50.6 0.8 %shard_map.33 = f32[64,1,128]{2,1,0:T(1,128)} custom-call(f32[16,1,128]{2,1,0:T(1,128)S(1)} %all-to-all-done.got_ref), custom_call_target="tpu_custom_call" | custom-call | tf_op jit(solution)/shard_map/pallas_call | solution.py:397
  51.4 12.1 %all-to-all-start.1 = ((f32[64,1,128]{2,1,0:T(1,128)}), f32[64,1,128]{2,1,0:T(1,128)S(1)}, u32[]{:S(2)}, u32[]{:S(2)}) async-start(f32[64,1,128]{2,1,0:T(1,128)} %shard_map.33), calls=%async_computation.1 | async-start | bytes 65536 | tf_op jit(solution)/shard_map/all_to_all | solution.py:418
  63.5 0.8 %shard_map.31 = (f32[2,9,16,256]{3,2,1,0:T(8,128)S(1)}, f32[2,16,256]{2,1,0:T(8,128)S(1)}) custom-call(f32[3,4,8,256]{3,2,1,0:T(8,128)S(1)} %get-tuple-element.22.cot_ref, f32[3,4,8,256]{3,2,1,0:T(8,128)S(1)} %get-tuple-element.23.vel_ref, f32[3,4,8,256]{3,2,1,0:T(8,128)S(1)} %get-tuple-element.26.zn_ref, f32[3,4,8,256]{3,2,1,0:T(8,128)S(1)} %get-tuple-element.27.zp_ref, ...), custom_call_target="tpu_custom_call" | custom-call | flops 4000000000 | bytes 2000000 | tf_op jit(solution)/shard_map/pallas_call | solution.py:397
  64.3 0.0 collective-permute-done.4.late1_ref
  64.4 0.0 collective-permute-done.5.late2_ref
  64.4 0.2 shard_map.32
  64.6 0.4 all-to-all-done.1.sums_ref
  65.0 1.3 %shard_map.34 = f32[3,4,8,256]{3,2,1,0:T(8,128)} custom-call(s32[1]{0:T(128)} %bitcast.place_ref, f32[3,4,8,256]{3,2,1,0:T(8,128)S(1)} %get-tuple-element.22.cot_ref, f32[3,4,8,256]{3,2,1,0:T(8,128)S(1)} %get-tuple-element.23.vel_ref, f32[3,4,8,256]{3,2,1,0:T(8,128)S(1)} %get-tuple-element.26.zn_ref, f32[3,4,8,256]{3,2,1,0:T(8,128)S(1)} %get-tuple-element.27.zp_ref, ...), custom_call_target="tpu_custom_call" | custom-call | tf_op jit(solution)/shard_map/pallas_call | solution.py:397
  (1 shorter events, 0.0 us)
Async XLA Ops:
  1.0 18.0 %collective-permute-start = (f32[3,4,8,256]{3,2,1,0:T(8,128)S(1)}, f32[3,4,8,256]{3,2,1,0:T(8,128)S(1)}, u32[]{:S(2)}, u32[]{:S(2)}) collective-permute-start(f32[3,4,8,256]{3,2,1,0:T(8,128)S(1)} %get-tuple-element.24), channel_id=1, source_target_pairs={{0,63},{1,2},{2,1},{3,4},{4,3},{5,6},{6,5},{7,8},{8,7},{9,10},{10,... | collective-permute-start | bytes 294920 | tf_op jit(solution)/shard_map/ppermute | solution.py:427
  5.5 14.4 %collective-permute-start.1 = (f32[3,4,8,256]{3,2,1,0:T(8,128)S(1)}, f32[3,4,8,256]{3,2,1,0:T(8,128)S(1)}, u32[]{:S(2)}, u32[]{:S(2)}) collective-permute-start(f32[3,4,8,256]{3,2,1,0:T(8,128)S(1)} %get-tuple-element.25), channel_id=1, source_target_pairs={{0,1},{1,0},{2,3},{3,2},{4,5},{5,4},{6,7},{7,6},{8,9},{9,8},{10,11... | collective-permute-start | bytes 294920 | tf_op jit(solution)/shard_map/ppermute | solution.py:431
  20.0 13.2 %collective-permute-start.2 = (f32[6,8,256]{2,1,0:T(8,128)S(1)}, f32[6,8,256]{2,1,0:T(8,128)S(1)}, u32[]{:S(2)}, u32[]{:S(2)}) collective-permute-start(f32[6,8,256]{2,1,0:T(8,128)S(1)} %get-tuple-element.28), channel_id=1, source_target_pairs={{0,960},{64,128},{128,64},{192,256},{256,192},{320,384},{384,320},... | collective-permute-start | bytes 147464 | tf_op jit(solution)/shard_map/ppermute | solution.py:427
  31.3 4.8 %collective-permute-start.3 = (f32[6,8,256]{2,1,0:T(8,128)S(1)}, f32[6,8,256]{2,1,0:T(8,128)S(1)}, u32[]{:S(2)}, u32[]{:S(2)}) collective-permute-start(f32[6,8,256]{2,1,0:T(8,128)S(1)} %get-tuple-element.29), channel_id=1, source_target_pairs={{0,64},{64,0},{128,192},{192,128},{256,320},{320,256},{384,448},{4... | collective-permute-start | bytes 147464 | tf_op jit(solution)/shard_map/ppermute | solution.py:431
  37.1 13.4 %all-to-all-start = ((f32[16,1,128]{2,1,0:T(1,128)}), f32[16,1,128]{2,1,0:T(1,128)S(1)}, u32[]{:S(2)}, u32[]{:S(2)}) async-start(f32[16,1,128]{2,1,0:T(1,128)} %get-tuple-element.34.lines_ref), calls=%async_computation | async-start | bytes 16384 | tf_op jit(solution)/shard_map/all_to_all | solution.py:418
  45.8 18.6 %collective-permute-start.4 = (f32[14,8,256]{2,1,0:T(8,128)S(1)}, f32[14,8,256]{2,1,0:T(8,128)S(1)}, u32[]{:S(2)}, u32[]{:S(2)}) collective-permute-start(f32[14,8,256]{2,1,0:T(8,128)S(1)} %get-tuple-element.30), channel_id=1, source_target_pairs={{0,960},{64,128},{128,64},{192,256},{256,192},{320,384},{384,320},... | collective-permute-start | bytes 344072 | tf_op jit(solution)/shard_map/ppermute | solution.py:427
  48.6 15.7 %collective-permute-start.5 = (f32[14,8,256]{2,1,0:T(8,128)S(1)}, f32[14,8,256]{2,1,0:T(8,128)S(1)}, u32[]{:S(2)}, u32[]{:S(2)}) collective-permute-start(f32[14,8,256]{2,1,0:T(8,128)S(1)} %get-tuple-element.31), channel_id=1, source_target_pairs={{0,64},{64,0},{128,192},{192,128},{256,320},{320,256},{384,448},{4... | collective-permute-start | bytes 344072 | tf_op jit(solution)/shard_map/ppermute | solution.py:431
  51.4 13.6 %all-to-all-start.1 = ((f32[64,1,128]{2,1,0:T(1,128)}), f32[64,1,128]{2,1,0:T(1,128)S(1)}, u32[]{:S(2)}, u32[]{:S(2)}) async-start(f32[64,1,128]{2,1,0:T(1,128)} %shard_map.33), calls=%async_computation.1 | async-start | bytes 65536 | tf_op jit(solution)/shard_map/all_to_all | solution.py:418

commit v10 on v9

--- a/solution.py
+++ b/solution.py
@@ -451,7 +451,7 @@
         [place],
         held,
     )
-    got = to_all(lines, STEPS[0])
+    got = lax.all_to_all(lines, STEPS[0], 0, 0)
     late = [swap_across(late1, PY), swap_within(late2, PY)]
     inner = call(inner_slopes, [(2, 9, WIDE, 256), (2, WIDE, 256)], [], held[:4] + [lines], 4_000_000_000)
     outer = call(outer_slopes, [(4, 9, WIDE, 256), (4, WIDE, 256)], [place], held[:4] + late, 4_000_000)

time: 67.5 us -> 66.3 us (0.982)
  starting transfers between devices: 56.7 us -> 55.8 us
    all_to_all x2 -> x1, starting transfers between devices: 20.8 us -> 12.4 us  [to_all(): return lax.all_to_all(rows, axes, 0, 0, axis_index_groups=[order])]
    all_to_all x0 -> x1, starting transfers between devices: none -> 5.03 us  [body(): got = lax.all_to_all(lines, STEPS[0], 0, 0)]
    ppermute x3, starting transfers between devices: 18.6 us -> 21 us  [swap_across(): lax.ppermute(x, axes, [(i, (i + 1 if i % 2 else i - 1) % n) for i in rang...]
where the time goes in v10:
time: 66.3 us; the launch traced here: 65.3 us
  starting transfers between devices  55.8 us (84%)
  waiting for transfers between devices  4.21 us (6%)
  Pallas kernels  4.2 us (6%)
  other arithmetic  0.95 us (1%)
    ppermute x3, starting transfers between devices, swap_across(): lax.ppermute(x, axes, [(i, (i + 1 if i % 2 else i - 1) % n) for i in rang...  21 us
    ppermute x3, starting transfers between devices, swap_within(): return lax.ppermute(x, axes, [(i, i ^ 1) for i in range(size(axes))])  17.3 us
    all_to_all x1, starting transfers between devices, to_all(): return lax.all_to_all(rows, axes, 0, 0, axis_index_groups=[order])  12.4 us
    all_to_all x1, starting transfers between devices, body(): got = lax.all_to_all(lines, STEPS[0], 0, 0)  5.03 us
    pallas_call x7, Pallas kernels, call(): pl.pallas_call(kernel, out_shape=[jax.ShapeDtypeStruct(s, jnp.float32) fo...  4.2 us
    ppermute x3, waiting for transfers between devices, swap_within(): return lax.ppermute(x, axes, [(i, i ^ 1) for i in range(size(axes))])  3.8 us
  transfers between devices with their start and end apart: 8, of which 3 were waited for; matrix products, arithmetic and copies ran while one was open for 0% of the time, Pallas kernels for 3%

profile of v10, /device:TPU:1, one launch (start us, length us, event | category | flops | bytes accessed | tf_op | source)
XLA Modules:
  0.0 65.3 jit_solution(8440248025218517512)
XLA Ops:
  0.0 1.0 %pad_maximum_fusion.both_ref = f32[6,4,8,256]{3,2,1,0:T(8,128)S(1)} fusion(f32[3,4,8,256]{3,2,1,0:T(8,128)} %param.2, f32[3,4,8,256]{3,2,1,0:T(8,128)} %param.3), kind=kLoop, calls=%fused_computation | loop fusion | flops 49152 | bytes 393216 | tf_op jit(solution)/shard_map/concatenate | solution.py:439
  1.0 4.5 %collective-permute-start = (f32[3,4,8,256]{3,2,1,0:T(8,128)S(1)}, f32[3,4,8,256]{3,2,1,0:T(8,128)S(1)}, u32[]{:S(2)}, u32[]{:S(2)}) collective-permute-start(f32[3,4,8,256]{3,2,1,0:T(8,128)S(1)} %get-tuple-element.24), channel_id=1, source_target_pairs={{0,63},{1,2},{2,1},{3,4},{4,3},{5,6},{6,5},{7,8},{8,7},{9,10},{10,... | collective-permute-start | bytes 294920 | tf_op jit(solution)/shard_map/ppermute | solution.py:427
  5.5 13.5 %collective-permute-start.1 = (f32[3,4,8,256]{3,2,1,0:T(8,128)S(1)}, f32[3,4,8,256]{3,2,1,0:T(8,128)S(1)}, u32[]{:S(2)}, u32[]{:S(2)}) collective-permute-start(f32[3,4,8,256]{3,2,1,0:T(8,128)S(1)} %get-tuple-element.25), channel_id=1, source_target_pairs={{0,1},{1,0},{2,3},{3,2},{4,5},{5,4},{6,7},{7,6},{8,9},{9,8},{10,11... | collective-permute-start | bytes 294920 | tf_op jit(solution)/shard_map/ppermute | solution.py:431
  19.0 0.0 collective-permute-done.cross_ref
  19.0 0.9 %collective-permute-done.1.core_ref = f32[3,4,8,256]{3,2,1,0:T(8,128)S(1)} collective-permute-done((f32[3,4,8,256]{3,2,1,0:T(8,128)S(1)}, f32[3,4,8,256]{3,2,1,0:T(8,128)S(1)}, u32[]{:S(2)}, u32[]{:S(2)}) %collective-permute-start.1) | collective-permute-done | bytes 98336 | tf_op jit(solution)/shard_map/ppermute | solution.py:431
  19.9 0.1 shard_map.29
  20.0 11.3 %collective-permute-start.2 = (f32[6,8,256]{2,1,0:T(8,128)S(1)}, f32[6,8,256]{2,1,0:T(8,128)S(1)}, u32[]{:S(2)}, u32[]{:S(2)}) collective-permute-start(f32[6,8,256]{2,1,0:T(8,128)S(1)} %get-tuple-element.28), channel_id=1, source_target_pairs={{0,960},{64,128},{128,64},{192,256},{256,192},{320,384},{384,320},... | collective-permute-start | bytes 147464 | tf_op jit(solution)/shard_map/ppermute | solution.py:427
  31.3 1.9 %collective-permute-start.3 = (f32[6,8,256]{2,1,0:T(8,128)S(1)}, f32[6,8,256]{2,1,0:T(8,128)S(1)}, u32[]{:S(2)}, u32[]{:S(2)}) collective-permute-start(f32[6,8,256]{2,1,0:T(8,128)S(1)} %get-tuple-element.29), channel_id=1, source_target_pairs={{0,64},{64,0},{128,192},{192,128},{256,320},{320,256},{384,448},{4... | collective-permute-start | bytes 147464 | tf_op jit(solution)/shard_map/ppermute | solution.py:431
  33.3 0.0 collective-permute-done.2.first_ref
  33.3 2.9 %collective-permute-done.3.second_ref = f32[6,8,256]{2,1,0:T(8,128)S(1)} collective-permute-done((f32[6,8,256]{2,1,0:T(8,128)S(1)}, f32[6,8,256]{2,1,0:T(8,128)S(1)}, u32[]{:S(2)}, u32[]{:S(2)}) %collective-permute-start.3) | collective-permute-done | bytes 49184 | tf_op jit(solution)/shard_map/ppermute | solution.py:431
  36.2 1.0 %shard_map.30 = (f32[16,1,128]{2,1,0:T(1,128)}, f32[8,16,256]{2,1,0:T(8,128)S(1)}, f32[6,16,256]{2,1,0:T(8,128)S(1)}, f32[14,8,256]{2,1,0:T(8,128)S(1)}, f32[14,8,256]{2,1,0:T(8,128)S(1)}) custom-call(s32[1]{0:T(128)} %bitcast.place_ref, f32[3,4,8,256]{3,2,1,0:T(8,128)S(1)} %get-tuple-element.22.cot_ref, f32[3,4,8,256]{3,2,1,0:T(8,128)S(1)} %get-tuple-element.23.vel_ref, ...), custom_call_target="tpu_custom_call" | custom-call | tf_op jit(solution)/shard_map/pallas_call | solution.py:397
  37.1 5.0 %all-to-all-start = ((f32[16,1,128]{2,1,0:T(1,128)}), f32[16,1,128]{2,1,0:T(1,128)S(1)}, u32[]{:S(2)}, u32[]{:S(2)}) async-start(f32[16,1,128]{2,1,0:T(1,128)} %get-tuple-element.34.lines_ref), calls=%async_computation | async-start | bytes 16384 | tf_op jit(solution)/shard_map/all_to_all | solution.py:454
  42.1 5.3 %collective-permute-start.4 = (f32[14,8,256]{2,1,0:T(8,128)S(1)}, f32[14,8,256]{2,1,0:T(8,128)S(1)}, u32[]{:S(2)}, u32[]{:S(2)}) collective-permute-start(f32[14,8,256]{2,1,0:T(8,128)S(1)} %get-tuple-element.30), channel_id=1, source_target_pairs={{0,960},{64,128},{128,64},{192,256},{256,192},{320,384},{384,320},... | collective-permute-start | bytes 344072 | tf_op jit(solution)/shard_map/ppermute | solution.py:427
  47.4 1.9 %collective-permute-start.5 = (f32[14,8,256]{2,1,0:T(8,128)S(1)}, f32[14,8,256]{2,1,0:T(8,128)S(1)}, u32[]{:S(2)}, u32[]{:S(2)}) collective-permute-start(f32[14,8,256]{2,1,0:T(8,128)S(1)} %get-tuple-element.31), channel_id=1, source_target_pairs={{0,64},{64,0},{128,192},{192,128},{256,320},{320,256},{384,448},{4... | collective-permute-start | bytes 344072 | tf_op jit(solution)/shard_map/ppermute | solution.py:431
  49.3 0.0 all-to-all-done.got_ref
  49.3 0.8 %shard_map.33 = f32[64,1,128]{2,1,0:T(1,128)} custom-call(f32[16,1,128]{2,1,0:T(1,128)S(1)} %all-to-all-done.got_ref), custom_call_target="tpu_custom_call" | custom-call | tf_op jit(solution)/shard_map/pallas_call | solution.py:397
  50.1 12.4 %all-to-all-start.1 = ((f32[64,1,128]{2,1,0:T(1,128)}), f32[64,1,128]{2,1,0:T(1,128)S(1)}, u32[]{:S(2)}, u32[]{:S(2)}) async-start(f32[64,1,128]{2,1,0:T(1,128)} %shard_map.33), calls=%async_computation.1 | async-start | bytes 65536 | tf_op jit(solution)/shard_map/all_to_all | solution.py:418
  62.5 0.8 %shard_map.31 = (f32[2,9,16,256]{3,2,1,0:T(8,128)S(1)}, f32[2,16,256]{2,1,0:T(8,128)S(1)}) custom-call(f32[3,4,8,256]{3,2,1,0:T(8,128)S(1)} %get-tuple-element.22.cot_ref, f32[3,4,8,256]{3,2,1,0:T(8,128)S(1)} %get-tuple-element.23.vel_ref, f32[3,4,8,256]{3,2,1,0:T(8,128)S(1)} %get-tuple-element.26.zn_ref, f32[3,4,8,256]{3,2,1,0:T(8,128)S(1)} %get-tuple-element.27.zp_ref, ...), custom_call_target="tpu_custom_call" | custom-call | flops 4000000000 | bytes 2000000 | tf_op jit(solution)/shard_map/pallas_call | solution.py:397
  63.4 0.0 collective-permute-done.4.late1_ref
  63.4 0.0 collective-permute-done.5.late2_ref
  63.4 0.2 shard_map.32
  63.6 0.4 all-to-all-done.1.sums_ref
  64.0 1.3 %shard_map.34 = f32[3,4,8,256]{3,2,1,0:T(8,128)} custom-call(s32[1]{0:T(128)} %bitcast.place_ref, f32[3,4,8,256]{3,2,1,0:T(8,128)S(1)} %get-tuple-element.22.cot_ref, f32[3,4,8,256]{3,2,1,0:T(8,128)S(1)} %get-tuple-element.23.vel_ref, f32[3,4,8,256]{3,2,1,0:T(8,128)S(1)} %get-tuple-element.26.zn_ref, f32[3,4,8,256]{3,2,1,0:T(8,128)S(1)} %get-tuple-element.27.zp_ref, ...), custom_call_target="tpu_custom_call" | custom-call | tf_op jit(solution)/shard_map/pallas_call | solution.py:397
  (1 shorter events, 0.0 us)
Async XLA Ops:
  1.0 18.0 %collective-permute-start = (f32[3,4,8,256]{3,2,1,0:T(8,128)S(1)}, f32[3,4,8,256]{3,2,1,0:T(8,128)S(1)}, u32[]{:S(2)}, u32[]{:S(2)}) collective-permute-start(f32[3,4,8,256]{3,2,1,0:T(8,128)S(1)} %get-tuple-element.24), channel_id=1, source_target_pairs={{0,63},{1,2},{2,1},{3,4},{4,3},{5,6},{6,5},{7,8},{8,7},{9,10},{10,... | collective-permute-start | bytes 294920 | tf_op jit(solution)/shard_map/ppermute | solution.py:427
  5.5 14.4 %collective-permute-start.1 = (f32[3,4,8,256]{3,2,1,0:T(8,128)S(1)}, f32[3,4,8,256]{3,2,1,0:T(8,128)S(1)}, u32[]{:S(2)}, u32[]{:S(2)}) collective-permute-start(f32[3,4,8,256]{3,2,1,0:T(8,128)S(1)} %get-tuple-element.25), channel_id=1, source_target_pairs={{0,1},{1,0},{2,3},{3,2},{4,5},{5,4},{6,7},{7,6},{8,9},{9,8},{10,11... | collective-permute-start | bytes 294920 | tf_op jit(solution)/shard_map/ppermute | solution.py:431
  20.0 13.2 %collective-permute-start.2 = (f32[6,8,256]{2,1,0:T(8,128)S(1)}, f32[6,8,256]{2,1,0:T(8,128)S(1)}, u32[]{:S(2)}, u32[]{:S(2)}) collective-permute-start(f32[6,8,256]{2,1,0:T(8,128)S(1)} %get-tuple-element.28), channel_id=1, source_target_pairs={{0,960},{64,128},{128,64},{192,256},{256,192},{320,384},{384,320},... | collective-permute-start | bytes 147464 | tf_op jit(solution)/shard_map/ppermute | solution.py:427
  31.3 4.8 %collective-permute-start.3 = (f32[6,8,256]{2,1,0:T(8,128)S(1)}, f32[6,8,256]{2,1,0:T(8,128)S(1)}, u32[]{:S(2)}, u32[]{:S(2)}) collective-permute-start(f32[6,8,256]{2,1,0:T(8,128)S(1)} %get-tuple-element.29), channel_id=1, source_target_pairs={{0,64},{64,0},{128,192},{192,128},{256,320},{320,256},{384,448},{4... | collective-permute-start | bytes 147464 | tf_op jit(solution)/shard_map/ppermute | solution.py:431
  37.1 12.2 %all-to-all-start = ((f32[16,1,128]{2,1,0:T(1,128)}), f32[16,1,128]{2,1,0:T(1,128)S(1)}, u32[]{:S(2)}, u32[]{:S(2)}) async-start(f32[16,1,128]{2,1,0:T(1,128)} %get-tuple-element.34.lines_ref), calls=%async_computation | async-start | bytes 16384 | tf_op jit(solution)/shard_map/all_to_all | solution.py:454
  42.1 21.2 %collective-permute-start.4 = (f32[14,8,256]{2,1,0:T(8,128)S(1)}, f32[14,8,256]{2,1,0:T(8,128)S(1)}, u32[]{:S(2)}, u32[]{:S(2)}) collective-permute-start(f32[14,8,256]{2,1,0:T(8,128)S(1)} %get-tuple-element.30), channel_id=1, source_target_pairs={{0,960},{64,128},{128,64},{192,256},{256,192},{320,384},{384,320},... | collective-permute-start | bytes 344072 | tf_op jit(solution)/shard_map/ppermute | solution.py:427
  47.4 16.0 %collective-permute-start.5 = (f32[14,8,256]{2,1,0:T(8,128)S(1)}, f32[14,8,256]{2,1,0:T(8,128)S(1)}, u32[]{:S(2)}, u32[]{:S(2)}) collective-permute-start(f32[14,8,256]{2,1,0:T(8,128)S(1)} %get-tuple-element.31), channel_id=1, source_target_pairs={{0,64},{64,0},{128,192},{192,128},{256,320},{320,256},{384,448},{4... | collective-permute-start | bytes 344072 | tf_op jit(solution)/shard_map/ppermute | solution.py:431
  50.1 13.8 %all-to-all-start.1 = ((f32[64,1,128]{2,1,0:T(1,128)}), f32[64,1,128]{2,1,0:T(1,128)S(1)}, u32[]{:S(2)}, u32[]{:S(2)}) async-start(f32[64,1,128]{2,1,0:T(1,128)} %shard_map.33), calls=%async_computation.1 | async-start | bytes 65536 | tf_op jit(solution)/shard_map/all_to_all | solution.py:418

commit v11 on v10

--- a/solution.py
+++ b/solution.py
@@ -412,8 +412,8 @@
 def to_all(rows, axes):
     sizes = [lax.axis_size(axis) for axis in axes]
     order = [0]
-    for n in sizes:
-        middle = n // 2 if n > 2 else 0
+    for at, n in enumerate(sizes):
+        middle = 0 if at else n // 2
         order = [i * n + (k + middle) % n for i in order for k in range(n)]
     return lax.all_to_all(rows, axes, 0, 0, axis_index_groups=[order])
 

time: 66.3 us -> 67.8 us (1.023)
  waiting for transfers between devices: 4.21 us -> 9.02 us
  starting transfers between devices: 55.8 us -> 52.9 us
    all_to_all x1, waiting for transfers between devices: 0.39 us -> 5.21 us  [to_all(): return lax.all_to_all(rows, axes, 0, 0, axis_index_groups=[order])]
    all_to_all x1, starting transfers between devices: 12.4 us -> 9.48 us  [to_all(): return lax.all_to_all(rows, axes, 0, 0, axis_index_groups=[order])]
where the time goes in v11:
time: 67.8 us; the launch traced here: 67.2 us
  starting transfers between devices  52.9 us (78%)
  waiting for transfers between devices  9.02 us (13%)
  Pallas kernels  4.2 us (6%)
  other arithmetic  0.95 us (1%)
    ppermute x3, starting transfers between devices, swap_across(): lax.ppermute(x, axes, [(i, (i + 1 if i % 2 else i - 1) % n) for i in rang...  21 us
    ppermute x3, starting transfers between devices, swap_within(): return lax.ppermute(x, axes, [(i, i ^ 1) for i in range(size(axes))])  17.3 us
    all_to_all x1, starting transfers between devices, to_all(): return lax.all_to_all(rows, axes, 0, 0, axis_index_groups=[order])  9.48 us
    all_to_all x1, waiting for transfers between devices, to_all(): return lax.all_to_all(rows, axes, 0, 0, axis_index_groups=[order])  5.21 us
    all_to_all x1, starting transfers between devices, body(): got = lax.all_to_all(lines, STEPS[0], 0, 0)  5.03 us
    pallas_call x7, Pallas kernels, call(): pl.pallas_call(kernel, out_shape=[jax.ShapeDtypeStruct(s, jnp.float32) fo...  4.2 us
    ppermute x3, waiting for transfers between devices, swap_within(): return lax.ppermute(x, axes, [(i, i ^ 1) for i in range(size(axes))])  3.8 us
  transfers between devices with their start and end apart: 8, of which 3 were waited for; matrix products, arithmetic and copies ran while one was open for 0% of the time, Pallas kernels for 3%

profile of v11, /device:TPU:1, one launch (start us, length us, event | category | flops | bytes accessed | tf_op | source)
XLA Modules:
  0.0 67.2 jit_solution(1551928538078072877)
XLA Ops:
  0.0 1.0 %pad_maximum_fusion.both_ref = f32[6,4,8,256]{3,2,1,0:T(8,128)S(1)} fusion(f32[3,4,8,256]{3,2,1,0:T(8,128)} %param.2, f32[3,4,8,256]{3,2,1,0:T(8,128)} %param.3), kind=kLoop, calls=%fused_computation | loop fusion | flops 49152 | bytes 393216 | tf_op jit(solution)/shard_map/concatenate | solution.py:439
  1.0 4.5 %collective-permute-start = (f32[3,4,8,256]{3,2,1,0:T(8,128)S(1)}, f32[3,4,8,256]{3,2,1,0:T(8,128)S(1)}, u32[]{:S(2)}, u32[]{:S(2)}) collective-permute-start(f32[3,4,8,256]{3,2,1,0:T(8,128)S(1)} %get-tuple-element.24), channel_id=1, source_target_pairs={{0,63},{1,2},{2,1},{3,4},{4,3},{5,6},{6,5},{7,8},{8,7},{9,10},{10,... | collective-permute-start | bytes 294920 | tf_op jit(solution)/shard_map/ppermute | solution.py:427
  5.5 13.5 %collective-permute-start.1 = (f32[3,4,8,256]{3,2,1,0:T(8,128)S(1)}, f32[3,4,8,256]{3,2,1,0:T(8,128)S(1)}, u32[]{:S(2)}, u32[]{:S(2)}) collective-permute-start(f32[3,4,8,256]{3,2,1,0:T(8,128)S(1)} %get-tuple-element.25), channel_id=1, source_target_pairs={{0,1},{1,0},{2,3},{3,2},{4,5},{5,4},{6,7},{7,6},{8,9},{9,8},{10,11... | collective-permute-start | bytes 294920 | tf_op jit(solution)/shard_map/ppermute | solution.py:431
  19.0 0.0 collective-permute-done.cross_ref
  19.0 0.9 %collective-permute-done.1.core_ref = f32[3,4,8,256]{3,2,1,0:T(8,128)S(1)} collective-permute-done((f32[3,4,8,256]{3,2,1,0:T(8,128)S(1)}, f32[3,4,8,256]{3,2,1,0:T(8,128)S(1)}, u32[]{:S(2)}, u32[]{:S(2)}) %collective-permute-start.1) | collective-permute-done | bytes 98336 | tf_op jit(solution)/shard_map/ppermute | solution.py:431
  19.9 0.1 shard_map.29
  20.0 11.3 %collective-permute-start.2 = (f32[6,8,256]{2,1,0:T(8,128)S(1)}, f32[6,8,256]{2,1,0:T(8,128)S(1)}, u32[]{:S(2)}, u32[]{:S(2)}) collective-permute-start(f32[6,8,256]{2,1,0:T(8,128)S(1)} %get-tuple-element.28), channel_id=1, source_target_pairs={{0,960},{64,128},{128,64},{192,256},{256,192},{320,384},{384,320},... | collective-permute-start | bytes 147464 | tf_op jit(solution)/shard_map/ppermute | solution.py:427
  31.3 1.9 %collective-permute-start.3 = (f32[6,8,256]{2,1,0:T(8,128)S(1)}, f32[6,8,256]{2,1,0:T(8,128)S(1)}, u32[]{:S(2)}, u32[]{:S(2)}) collective-permute-start(f32[6,8,256]{2,1,0:T(8,128)S(1)} %get-tuple-element.29), channel_id=1, source_target_pairs={{0,64},{64,0},{128,192},{192,128},{256,320},{320,256},{384,448},{4... | collective-permute-start | bytes 147464 | tf_op jit(solution)/shard_map/ppermute | solution.py:431
  33.3 0.0 collective-permute-done.2.first_ref
  33.3 2.9 %collective-permute-done.3.second_ref = f32[6,8,256]{2,1,0:T(8,128)S(1)} collective-permute-done((f32[6,8,256]{2,1,0:T(8,128)S(1)}, f32[6,8,256]{2,1,0:T(8,128)S(1)}, u32[]{:S(2)}, u32[]{:S(2)}) %collective-permute-start.3) | collective-permute-done | bytes 49184 | tf_op jit(solution)/shard_map/ppermute | solution.py:431
  36.2 1.0 %shard_map.30 = (f32[16,1,128]{2,1,0:T(1,128)}, f32[8,16,256]{2,1,0:T(8,128)S(1)}, f32[6,16,256]{2,1,0:T(8,128)S(1)}, f32[14,8,256]{2,1,0:T(8,128)S(1)}, f32[14,8,256]{2,1,0:T(8,128)S(1)}) custom-call(s32[1]{0:T(128)} %bitcast.place_ref, f32[3,4,8,256]{3,2,1,0:T(8,128)S(1)} %get-tuple-element.22.cot_ref, f32[3,4,8,256]{3,2,1,0:T(8,128)S(1)} %get-tuple-element.23.vel_ref, ...), custom_call_target="tpu_custom_call" | custom-call | tf_op jit(solution)/shard_map/pallas_call | solution.py:397
  37.1 5.0 %all-to-all-start = ((f32[16,1,128]{2,1,0:T(1,128)}), f32[16,1,128]{2,1,0:T(1,128)S(1)}, u32[]{:S(2)}, u32[]{:S(2)}) async-start(f32[16,1,128]{2,1,0:T(1,128)} %get-tuple-element.34.lines_ref), calls=%async_computation | async-start | bytes 16384 | tf_op jit(solution)/shard_map/all_to_all | solution.py:454
  42.1 5.3 %collective-permute-start.4 = (f32[14,8,256]{2,1,0:T(8,128)S(1)}, f32[14,8,256]{2,1,0:T(8,128)S(1)}, u32[]{:S(2)}, u32[]{:S(2)}) collective-permute-start(f32[14,8,256]{2,1,0:T(8,128)S(1)} %get-tuple-element.30), channel_id=1, source_target_pairs={{0,960},{64,128},{128,64},{192,256},{256,192},{320,384},{384,320},... | collective-permute-start | bytes 344072 | tf_op jit(solution)/shard_map/ppermute | solution.py:427
  47.4 1.9 %collective-permute-start.5 = (f32[14,8,256]{2,1,0:T(8,128)S(1)}, f32[14,8,256]{2,1,0:T(8,128)S(1)}, u32[]{:S(2)}, u32[]{:S(2)}) collective-permute-start(f32[14,8,256]{2,1,0:T(8,128)S(1)} %get-tuple-element.31), channel_id=1, source_target_pairs={{0,64},{64,0},{128,192},{192,128},{256,320},{320,256},{384,448},{4... | collective-permute-start | bytes 344072 | tf_op jit(solution)/shard_map/ppermute | solution.py:431
  49.3 0.0 all-to-all-done.got_ref
  49.3 0.8 %shard_map.33 = f32[64,1,128]{2,1,0:T(1,128)} custom-call(f32[16,1,128]{2,1,0:T(1,128)S(1)} %all-to-all-done.got_ref), custom_call_target="tpu_custom_call" | custom-call | tf_op jit(solution)/shard_map/pallas_call | solution.py:397
  50.1 9.5 %all-to-all-start.1 = ((f32[64,1,128]{2,1,0:T(1,128)}), f32[64,1,128]{2,1,0:T(1,128)S(1)}, u32[]{:S(2)}, u32[]{:S(2)}) async-start(f32[64,1,128]{2,1,0:T(1,128)} %shard_map.33), calls=%async_computation.1 | async-start | bytes 65536 | tf_op jit(solution)/shard_map/all_to_all | solution.py:418
  59.6 0.8 %shard_map.31 = (f32[2,9,16,256]{3,2,1,0:T(8,128)S(1)}, f32[2,16,256]{2,1,0:T(8,128)S(1)}) custom-call(f32[3,4,8,256]{3,2,1,0:T(8,128)S(1)} %get-tuple-element.22.cot_ref, f32[3,4,8,256]{3,2,1,0:T(8,128)S(1)} %get-tuple-element.23.vel_ref, f32[3,4,8,256]{3,2,1,0:T(8,128)S(1)} %get-tuple-element.26.zn_ref, f32[3,4,8,256]{3,2,1,0:T(8,128)S(1)} %get-tuple-element.27.zp_ref, ...), custom_call_target="tpu_custom_call" | custom-call | flops 4000000000 | bytes 2000000 | tf_op jit(solution)/shard_map/pallas_call | solution.py:397
  60.5 0.0 collective-permute-done.4.late1_ref
  60.5 0.0 collective-permute-done.5.late2_ref
  60.5 0.2 shard_map.32
  60.7 5.2 %all-to-all-done.1.sums_ref = f32[64,1,128]{2,1,0:T(1,128)S(1)} async-done(((f32[64,1,128]{2,1,0:T(1,128)}), f32[64,1,128]{2,1,0:T(1,128)S(1)}, u32[]{:S(2)}, u32[]{:S(2)}) %all-to-all-start.1) | async-done | bytes 32800 | tf_op jit(solution)/shard_map/all_to_all | solution.py:418
  65.9 1.3 %shard_map.34 = f32[3,4,8,256]{3,2,1,0:T(8,128)} custom-call(s32[1]{0:T(128)} %bitcast.place_ref, f32[3,4,8,256]{3,2,1,0:T(8,128)S(1)} %get-tuple-element.22.cot_ref, f32[3,4,8,256]{3,2,1,0:T(8,128)S(1)} %get-tuple-element.23.vel_ref, f32[3,4,8,256]{3,2,1,0:T(8,128)S(1)} %get-tuple-element.26.zn_ref, f32[3,4,8,256]{3,2,1,0:T(8,128)S(1)} %get-tuple-element.27.zp_ref, ...), custom_call_target="tpu_custom_call" | custom-call | tf_op jit(solution)/shard_map/pallas_call | solution.py:397
  (1 shorter events, 0.0 us)
Async XLA Ops:
  1.0 18.0 %collective-permute-start = (f32[3,4,8,256]{3,2,1,0:T(8,128)S(1)}, f32[3,4,8,256]{3,2,1,0:T(8,128)S(1)}, u32[]{:S(2)}, u32[]{:S(2)}) collective-permute-start(f32[3,4,8,256]{3,2,1,0:T(8,128)S(1)} %get-tuple-element.24), channel_id=1, source_target_pairs={{0,63},{1,2},{2,1},{3,4},{4,3},{5,6},{6,5},{7,8},{8,7},{9,10},{10,... | collective-permute-start | bytes 294920 | tf_op jit(solution)/shard_map/ppermute | solution.py:427
  5.5 14.4 %collective-permute-start.1 = (f32[3,4,8,256]{3,2,1,0:T(8,128)S(1)}, f32[3,4,8,256]{3,2,1,0:T(8,128)S(1)}, u32[]{:S(2)}, u32[]{:S(2)}) collective-permute-start(f32[3,4,8,256]{3,2,1,0:T(8,128)S(1)} %get-tuple-element.25), channel_id=1, source_target_pairs={{0,1},{1,0},{2,3},{3,2},{4,5},{5,4},{6,7},{7,6},{8,9},{9,8},{10,11... | collective-permute-start | bytes 294920 | tf_op jit(solution)/shard_map/ppermute | solution.py:431
  20.0 13.2 %collective-permute-start.2 = (f32[6,8,256]{2,1,0:T(8,128)S(1)}, f32[6,8,256]{2,1,0:T(8,128)S(1)}, u32[]{:S(2)}, u32[]{:S(2)}) collective-permute-start(f32[6,8,256]{2,1,0:T(8,128)S(1)} %get-tuple-element.28), channel_id=1, source_target_pairs={{0,960},{64,128},{128,64},{192,256},{256,192},{320,384},{384,320},... | collective-permute-start | bytes 147464 | tf_op jit(solution)/shard_map/ppermute | solution.py:427
  31.3 4.8 %collective-permute-start.3 = (f32[6,8,256]{2,1,0:T(8,128)S(1)}, f32[6,8,256]{2,1,0:T(8,128)S(1)}, u32[]{:S(2)}, u32[]{:S(2)}) collective-permute-start(f32[6,8,256]{2,1,0:T(8,128)S(1)} %get-tuple-element.29), channel_id=1, source_target_pairs={{0,64},{64,0},{128,192},{192,128},{256,320},{320,256},{384,448},{4... | collective-permute-start | bytes 147464 | tf_op jit(solution)/shard_map/ppermute | solution.py:431
  37.1 12.2 %all-to-all-start = ((f32[16,1,128]{2,1,0:T(1,128)}), f32[16,1,128]{2,1,0:T(1,128)S(1)}, u32[]{:S(2)}, u32[]{:S(2)}) async-start(f32[16,1,128]{2,1,0:T(1,128)} %get-tuple-element.34.lines_ref), calls=%async_computation | async-start | bytes 16384 | tf_op jit(solution)/shard_map/all_to_all | solution.py:454
  42.1 18.3 %collective-permute-start.4 = (f32[14,8,256]{2,1,0:T(8,128)S(1)}, f32[14,8,256]{2,1,0:T(8,128)S(1)}, u32[]{:S(2)}, u32[]{:S(2)}) collective-permute-start(f32[14,8,256]{2,1,0:T(8,128)S(1)} %get-tuple-element.30), channel_id=1, source_target_pairs={{0,960},{64,128},{128,64},{192,256},{256,192},{320,384},{384,320},... | collective-permute-start | bytes 344072 | tf_op jit(solution)/shard_map/ppermute | solution.py:427
  47.4 13.1 %collective-permute-start.5 = (f32[14,8,256]{2,1,0:T(8,128)S(1)}, f32[14,8,256]{2,1,0:T(8,128)S(1)}, u32[]{:S(2)}, u32[]{:S(2)}) collective-permute-start(f32[14,8,256]{2,1,0:T(8,128)S(1)} %get-tuple-element.31), channel_id=1, source_target_pairs={{0,64},{64,0},{128,192},{192,128},{256,320},{320,256},{384,448},{4... | collective-permute-start | bytes 344072 | tf_op jit(solution)/shard_map/ppermute | solution.py:431
  50.1 15.8 %all-to-all-start.1 = ((f32[64,1,128]{2,1,0:T(1,128)}), f32[64,1,128]{2,1,0:T(1,128)S(1)}, u32[]{:S(2)}, u32[]{:S(2)}) async-start(f32[64,1,128]{2,1,0:T(1,128)} %shard_map.33), calls=%async_computation.1 | async-start | bytes 65536 | tf_op jit(solution)/shard_map/all_to_all | solution.py:418

commit v12 on v11

--- a/solution.py
+++ b/solution.py
@@ -413,7 +413,7 @@
     sizes = [lax.axis_size(axis) for axis in axes]
     order = [0]
     for at, n in enumerate(sizes):
-        middle = 0 if at else n // 2
+        middle = n // 2 if at == len(sizes) - 1 else 0
         order = [i * n + (k + middle) % n for i in order for k in range(n)]
     return lax.all_to_all(rows, axes, 0, 0, axis_index_groups=[order])
 

time: 67.8 us -> 70.2 us (1.035)
  starting transfers between devices: 52.9 us -> 55.1 us
    all_to_all x1, starting transfers between devices: 9.48 us -> 11.7 us  [to_all(): return lax.all_to_all(rows, axes, 0, 0, axis_index_groups=[order])]
where the time goes in v12:
time: 70.2 us; the launch traced here: 69.4 us
  starting transfers between devices  55.1 us (78%)
  waiting for transfers between devices  9.02 us (13%)
  Pallas kernels  4.2 us (6%)
  other arithmetic  0.95 us (1%)
    ppermute x3, starting transfers between devices, swap_across(): lax.ppermute(x, axes, [(i, (i + 1 if i % 2 else i - 1) % n) for i in rang...  21 us
    ppermute x3, starting transfers between devices, swap_within(): return lax.ppermute(x, axes, [(i, i ^ 1) for i in range(size(axes))])  17.3 us
    all_to_all x1, starting transfers between devices, to_all(): return lax.all_to_all(rows, axes, 0, 0, axis_index_groups=[order])  11.7 us
    all_to_all x1, waiting for transfers between devices, to_all(): return lax.all_to_all(rows, axes, 0, 0, axis_index_groups=[order])  5.21 us
    all_to_all x1, starting transfers between devices, body(): got = lax.all_to_all(lines, STEPS[0], 0, 0)  5.03 us
    pallas_call x7, Pallas kernels, call(): pl.pallas_call(kernel, out_shape=[jax.ShapeDtypeStruct(s, jnp.float32) fo...  4.2 us
    ppermute x3, waiting for transfers between devices, swap_within(): return lax.ppermute(x, axes, [(i, i ^ 1) for i in range(size(axes))])  3.8 us
  transfers between devices with their start and end apart: 8, of which 3 were waited for; matrix products, arithmetic and copies ran while one was open for 0% of the time, Pallas kernels for 3%

profile of v12, /device:TPU:1, one launch (start us, length us, event | category | flops | bytes accessed | tf_op | source)
XLA Modules:
  0.0 69.4 jit_solution(1118198282930568530)
XLA Ops:
  0.0 1.0 %pad_maximum_fusion.both_ref = f32[6,4,8,256]{3,2,1,0:T(8,128)S(1)} fusion(f32[3,4,8,256]{3,2,1,0:T(8,128)} %param.2, f32[3,4,8,256]{3,2,1,0:T(8,128)} %param.3), kind=kLoop, calls=%fused_computation | loop fusion | flops 49152 | bytes 393216 | tf_op jit(solution)/shard_map/concatenate | solution.py:439
  1.0 4.5 %collective-permute-start = (f32[3,4,8,256]{3,2,1,0:T(8,128)S(1)}, f32[3,4,8,256]{3,2,1,0:T(8,128)S(1)}, u32[]{:S(2)}, u32[]{:S(2)}) collective-permute-start(f32[3,4,8,256]{3,2,1,0:T(8,128)S(1)} %get-tuple-element.24), channel_id=1, source_target_pairs={{0,63},{1,2},{2,1},{3,4},{4,3},{5,6},{6,5},{7,8},{8,7},{9,10},{10,... | collective-permute-start | bytes 294920 | tf_op jit(solution)/shard_map/ppermute | solution.py:427
  5.5 13.5 %collective-permute-start.1 = (f32[3,4,8,256]{3,2,1,0:T(8,128)S(1)}, f32[3,4,8,256]{3,2,1,0:T(8,128)S(1)}, u32[]{:S(2)}, u32[]{:S(2)}) collective-permute-start(f32[3,4,8,256]{3,2,1,0:T(8,128)S(1)} %get-tuple-element.25), channel_id=1, source_target_pairs={{0,1},{1,0},{2,3},{3,2},{4,5},{5,4},{6,7},{7,6},{8,9},{9,8},{10,11... | collective-permute-start | bytes 294920 | tf_op jit(solution)/shard_map/ppermute | solution.py:431
  19.0 0.0 collective-permute-done.cross_ref
  19.0 0.9 %collective-permute-done.1.core_ref = f32[3,4,8,256]{3,2,1,0:T(8,128)S(1)} collective-permute-done((f32[3,4,8,256]{3,2,1,0:T(8,128)S(1)}, f32[3,4,8,256]{3,2,1,0:T(8,128)S(1)}, u32[]{:S(2)}, u32[]{:S(2)}) %collective-permute-start.1) | collective-permute-done | bytes 98336 | tf_op jit(solution)/shard_map/ppermute | solution.py:431
  19.9 0.1 shard_map.29
  20.0 11.3 %collective-permute-start.2 = (f32[6,8,256]{2,1,0:T(8,128)S(1)}, f32[6,8,256]{2,1,0:T(8,128)S(1)}, u32[]{:S(2)}, u32[]{:S(2)}) collective-permute-start(f32[6,8,256]{2,1,0:T(8,128)S(1)} %get-tuple-element.28), channel_id=1, source_target_pairs={{0,960},{64,128},{128,64},{192,256},{256,192},{320,384},{384,320},... | collective-permute-start | bytes 147464 | tf_op jit(solution)/shard_map/ppermute | solution.py:427
  31.3 1.9 %collective-permute-start.3 = (f32[6,8,256]{2,1,0:T(8,128)S(1)}, f32[6,8,256]{2,1,0:T(8,128)S(1)}, u32[]{:S(2)}, u32[]{:S(2)}) collective-permute-start(f32[6,8,256]{2,1,0:T(8,128)S(1)} %get-tuple-element.29), channel_id=1, source_target_pairs={{0,64},{64,0},{128,192},{192,128},{256,320},{320,256},{384,448},{4... | collective-permute-start | bytes 147464 | tf_op jit(solution)/shard_map/ppermute | solution.py:431
  33.3 0.0 collective-permute-done.2.first_ref
  33.3 2.9 %collective-permute-done.3.second_ref = f32[6,8,256]{2,1,0:T(8,128)S(1)} collective-permute-done((f32[6,8,256]{2,1,0:T(8,128)S(1)}, f32[6,8,256]{2,1,0:T(8,128)S(1)}, u32[]{:S(2)}, u32[]{:S(2)}) %collective-permute-start.3) | collective-permute-done | bytes 49184 | tf_op jit(solution)/shard_map/ppermute | solution.py:431
  36.2 1.0 %shard_map.30 = (f32[16,1,128]{2,1,0:T(1,128)}, f32[8,16,256]{2,1,0:T(8,128)S(1)}, f32[6,16,256]{2,1,0:T(8,128)S(1)}, f32[14,8,256]{2,1,0:T(8,128)S(1)}, f32[14,8,256]{2,1,0:T(8,128)S(1)}) custom-call(s32[1]{0:T(128)} %bitcast.place_ref, f32[3,4,8,256]{3,2,1,0:T(8,128)S(1)} %get-tuple-element.22.cot_ref, f32[3,4,8,256]{3,2,1,0:T(8,128)S(1)} %get-tuple-element.23.vel_ref, ...), custom_call_target="tpu_custom_call" | custom-call | tf_op jit(solution)/shard_map/pallas_call | solution.py:397
  37.1 5.0 %all-to-all-start = ((f32[16,1,128]{2,1,0:T(1,128)}), f32[16,1,128]{2,1,0:T(1,128)S(1)}, u32[]{:S(2)}, u32[]{:S(2)}) async-start(f32[16,1,128]{2,1,0:T(1,128)} %get-tuple-element.34.lines_ref), calls=%async_computation | async-start | bytes 16384 | tf_op jit(solution)/shard_map/all_to_all | solution.py:454
  42.1 5.3 %collective-permute-start.4 = (f32[14,8,256]{2,1,0:T(8,128)S(1)}, f32[14,8,256]{2,1,0:T(8,128)S(1)}, u32[]{:S(2)}, u32[]{:S(2)}) collective-permute-start(f32[14,8,256]{2,1,0:T(8,128)S(1)} %get-tuple-element.30), channel_id=1, source_target_pairs={{0,960},{64,128},{128,64},{192,256},{256,192},{320,384},{384,320},... | collective-permute-start | bytes 344072 | tf_op jit(solution)/shard_map/ppermute | solution.py:427
  47.4 1.9 %collective-permute-start.5 = (f32[14,8,256]{2,1,0:T(8,128)S(1)}, f32[14,8,256]{2,1,0:T(8,128)S(1)}, u32[]{:S(2)}, u32[]{:S(2)}) collective-permute-start(f32[14,8,256]{2,1,0:T(8,128)S(1)} %get-tuple-element.31), channel_id=1, source_target_pairs={{0,64},{64,0},{128,192},{192,128},{256,320},{320,256},{384,448},{4... | collective-permute-start | bytes 344072 | tf_op jit(solution)/shard_map/ppermute | solution.py:431
  49.3 0.0 all-to-all-done.got_ref
  49.3 0.8 %shard_map.33 = f32[64,1,128]{2,1,0:T(1,128)} custom-call(f32[16,1,128]{2,1,0:T(1,128)S(1)} %all-to-all-done.got_ref), custom_call_target="tpu_custom_call" | custom-call | tf_op jit(solution)/shard_map/pallas_call | solution.py:397
  50.1 11.7 %all-to-all-start.1 = ((f32[64,1,128]{2,1,0:T(1,128)}), f32[64,1,128]{2,1,0:T(1,128)S(1)}, u32[]{:S(2)}, u32[]{:S(2)}) async-start(f32[64,1,128]{2,1,0:T(1,128)} %shard_map.33), calls=%async_computation.1 | async-start | bytes 65536 | tf_op jit(solution)/shard_map/all_to_all | solution.py:418
  61.9 0.8 %shard_map.31 = (f32[2,9,16,256]{3,2,1,0:T(8,128)S(1)}, f32[2,16,256]{2,1,0:T(8,128)S(1)}) custom-call(f32[3,4,8,256]{3,2,1,0:T(8,128)S(1)} %get-tuple-element.22.cot_ref, f32[3,4,8,256]{3,2,1,0:T(8,128)S(1)} %get-tuple-element.23.vel_ref, f32[3,4,8,256]{3,2,1,0:T(8,128)S(1)} %get-tuple-element.26.zn_ref, f32[3,4,8,256]{3,2,1,0:T(8,128)S(1)} %get-tuple-element.27.zp_ref, ...), custom_call_target="tpu_custom_call" | custom-call | flops 4000000000 | bytes 2000000 | tf_op jit(solution)/shard_map/pallas_call | solution.py:397
  62.7 0.0 collective-permute-done.4.late1_ref
  62.7 0.0 collective-permute-done.5.late2_ref
  62.7 0.2 shard_map.32
  62.9 5.2 %all-to-all-done.1.sums_ref = f32[64,1,128]{2,1,0:T(1,128)S(1)} async-done(((f32[64,1,128]{2,1,0:T(1,128)}), f32[64,1,128]{2,1,0:T(1,128)S(1)}, u32[]{:S(2)}, u32[]{:S(2)}) %all-to-all-start.1) | async-done | bytes 32800 | tf_op jit(solution)/shard_map/all_to_all | solution.py:418
  68.1 1.3 %shard_map.34 = f32[3,4,8,256]{3,2,1,0:T(8,128)} custom-call(s32[1]{0:T(128)} %bitcast.place_ref, f32[3,4,8,256]{3,2,1,0:T(8,128)S(1)} %get-tuple-element.22.cot_ref, f32[3,4,8,256]{3,2,1,0:T(8,128)S(1)} %get-tuple-element.23.vel_ref, f32[3,4,8,256]{3,2,1,0:T(8,128)S(1)} %get-tuple-element.26.zn_ref, f32[3,4,8,256]{3,2,1,0:T(8,128)S(1)} %get-tuple-element.27.zp_ref, ...), custom_call_target="tpu_custom_call" | custom-call | tf_op jit(solution)/shard_map/pallas_call | solution.py:397
  (1 shorter events, 0.0 us)
Async XLA Ops:
  1.0 18.0 %collective-permute-start = (f32[3,4,8,256]{3,2,1,0:T(8,128)S(1)}, f32[3,4,8,256]{3,2,1,0:T(8,128)S(1)}, u32[]{:S(2)}, u32[]{:S(2)}) collective-permute-start(f32[3,4,8,256]{3,2,1,0:T(8,128)S(1)} %get-tuple-element.24), channel_id=1, source_target_pairs={{0,63},{1,2},{2,1},{3,4},{4,3},{5,6},{6,5},{7,8},{8,7},{9,10},{10,... | collective-permute-start | bytes 294920 | tf_op jit(solution)/shard_map/ppermute | solution.py:427
  5.5 14.4 %collective-permute-start.1 = (f32[3,4,8,256]{3,2,1,0:T(8,128)S(1)}, f32[3,4,8,256]{3,2,1,0:T(8,128)S(1)}, u32[]{:S(2)}, u32[]{:S(2)}) collective-permute-start(f32[3,4,8,256]{3,2,1,0:T(8,128)S(1)} %get-tuple-element.25), channel_id=1, source_target_pairs={{0,1},{1,0},{2,3},{3,2},{4,5},{5,4},{6,7},{7,6},{8,9},{9,8},{10,11... | collective-permute-start | bytes 294920 | tf_op jit(solution)/shard_map/ppermute | solution.py:431
  20.0 13.2 %collective-permute-start.2 = (f32[6,8,256]{2,1,0:T(8,128)S(1)}, f32[6,8,256]{2,1,0:T(8,128)S(1)}, u32[]{:S(2)}, u32[]{:S(2)}) collective-permute-start(f32[6,8,256]{2,1,0:T(8,128)S(1)} %get-tuple-element.28), channel_id=1, source_target_pairs={{0,960},{64,128},{128,64},{192,256},{256,192},{320,384},{384,320},... | collective-permute-start | bytes 147464 | tf_op jit(solution)/shard_map/ppermute | solution.py:427
  31.3 4.8 %collective-permute-start.3 = (f32[6,8,256]{2,1,0:T(8,128)S(1)}, f32[6,8,256]{2,1,0:T(8,128)S(1)}, u32[]{:S(2)}, u32[]{:S(2)}) collective-permute-start(f32[6,8,256]{2,1,0:T(8,128)S(1)} %get-tuple-element.29), channel_id=1, source_target_pairs={{0,64},{64,0},{128,192},{192,128},{256,320},{320,256},{384,448},{4... | collective-permute-start | bytes 147464 | tf_op jit(solution)/shard_map/ppermute | solution.py:431
  37.1 12.2 %all-to-all-start = ((f32[16,1,128]{2,1,0:T(1,128)}), f32[16,1,128]{2,1,0:T(1,128)S(1)}, u32[]{:S(2)}, u32[]{:S(2)}) async-start(f32[16,1,128]{2,1,0:T(1,128)} %get-tuple-element.34.lines_ref), calls=%async_computation | async-start | bytes 16384 | tf_op jit(solution)/shard_map/all_to_all | solution.py:454
  42.1 20.6 %collective-permute-start.4 = (f32[14,8,256]{2,1,0:T(8,128)S(1)}, f32[14,8,256]{2,1,0:T(8,128)S(1)}, u32[]{:S(2)}, u32[]{:S(2)}) collective-permute-start(f32[14,8,256]{2,1,0:T(8,128)S(1)} %get-tuple-element.30), channel_id=1, source_target_pairs={{0,960},{64,128},{128,64},{192,256},{256,192},{320,384},{384,320},... | collective-permute-start | bytes 344072 | tf_op jit(solution)/shard_map/ppermute | solution.py:427
  47.4 15.3 %collective-permute-start.5 = (f32[14,8,256]{2,1,0:T(8,128)S(1)}, f32[14,8,256]{2,1,0:T(8,128)S(1)}, u32[]{:S(2)}, u32[]{:S(2)}) collective-permute-start(f32[14,8,256]{2,1,0:T(8,128)S(1)} %get-tuple-element.31), channel_id=1, source_target_pairs={{0,64},{64,0},{128,192},{192,128},{256,320},{320,256},{384,448},{4... | collective-permute-start | bytes 344072 | tf_op jit(solution)/shard_map/ppermute | solution.py:431
  50.1 18.0 %all-to-all-start.1 = ((f32[64,1,128]{2,1,0:T(1,128)}), f32[64,1,128]{2,1,0:T(1,128)S(1)}, u32[]{:S(2)}, u32[]{:S(2)}) async-start(f32[64,1,128]{2,1,0:T(1,128)} %shard_map.33), calls=%async_computation.1 | async-start | bytes 65536 | tf_op jit(solution)/shard_map/all_to_all | solution.py:418
